TPU v7x, 32 devices: a whole 2x2x4 slice. The times are simulated.
32 devices in a mesh: fsdp: 8 (over y, x, core), rep: 4 (over z).
Axes of the slice: x: 2, y: 2, z: 4, core: 2. Of those that a mesh axis runs over, the one named last changes fastest.
Arguments:
- incoming_symbols: bfloat16 [32, 128, 2048], P(('fsdp', 'rep')), may hold values from -6 to 6
- string_extents: int32 [32], P(('fsdp', 'rep')), may hold values from 32 to 128, as said below
- adjoint_signal: bfloat16 [32, 128, 2048], P(('fsdp', 'rep')), may hold values from -6 to 6
- first_scaling_factor: float32 [2048], replicated, may hold values from 0.5 to 1.5
- first_scaling_shift: float32 [2048], replicated, may hold values from -1.5 to 1.5
- lerp_factors: float32 [6, 2048], replicated, may hold values from 0 to 1
- lerp_narrow_weights: float32 [2048, 160], replicated, may hold values from -0.125 to 0.125
- lerp_widen_weights: float32 [5, 32, 2048], replicated, may hold values from -0.5 to 0.5
- fading_baseline: float32 [2048], replicated, may hold values from -6 to -0.5
- fading_narrow_weights: float32 [2048, 64], replicated, may hold values from -0.125 to 0.125
- fading_widen_weights: float32 [64, 2048], replicated, may hold values from -1.5 to 1.5
- present_reward: float32 [2048], replicated, may hold values from -3 to 3
- acceptor_weights: bfloat16 [2048, 2048], P('fsdp'), may hold values from -0.125 to 0.125
- lookup_weights: bfloat16 [2048, 2048], P('fsdp'), may hold values from -0.125 to 0.125
- content_weights: bfloat16 [2048, 2048], P('fsdp'), may hold values from -0.125 to 0.125
- valve_weights: bfloat16 [2048, 2048], P('fsdp'), may hold values from -0.125 to 0.125
- emission_weights: bfloat16 [2048, 2048], P('fsdp'), may hold values from -0.25 to 0.25
- cluster_scaling_factor: float32 [2048], replicated, may hold values from 0.5 to 1.5
- cluster_scaling_shift: float32 [2048], replicated, may hold values from -1.5 to 1.5
- second_scaling_factor: float32 [2048], replicated, may hold values from 0.5 to 1.5
- second_scaling_shift_vec: float32 [2048], replicated, may hold values from -1.5 to 1.5
- feed_lerp_factors: float32 [2, 2048], replicated, may hold values from 0 to 1
- feed_lookup_weights: bfloat16 [2048, 7168], P('fsdp'), may hold values from -0.125 to 0.125
- feed_content_weights: bfloat16 [7168, 2048], P('fsdp'), may hold values from -0.0625 to 0.0625
- feed_acceptor_weights: bfloat16 [2048, 2048], P('fsdp'), may hold values from -0.125 to 0.125
Outputs:
- layer_output: float32 [32, 128, 2048], P(('fsdp', 'rep'))
- token_grad: float32 [32, 128, 2048], P(('fsdp', 'rep'))
- first_scaling_factor_grads: float32 [2048], replicated
- first_scaling_shift_grads: float32 [2048], replicated
- lerp_factors_grads: float32 [6, 2048], replicated
- lerp_narrow_grads: float32 [2048, 160], replicated
- lerp_widen_grads: float32 [5, 32, 2048], replicated
- fading_baseline_grads: float32 [2048], replicated
- fading_narrow_grads: float32 [2048, 64], replicated
- fading_widen_grads: float32 [64, 2048], replicated
- present_reward_grads: float32 [2048], replicated
- acceptor_weights_grads: float32 [2048, 2048], P('fsdp')
- lookup_weights_grads: float32 [2048, 2048], P('fsdp')
- content_weights_grads: float32 [2048, 2048], P('fsdp')
- valve_weights_grads: float32 [2048, 2048], P('fsdp')
- emission_weights_grads: float32 [2048, 2048], P('fsdp')
- cluster_scaling_factor_grads: float32 [2048], replicated
- cluster_scaling_shift_grads: float32 [2048], replicated
- second_scaling_factor_grads: float32 [2048], replicated
- second_scaling_shift_grads: float32 [2048], replicated
- feed_lerp_grads: float32 [2, 2048], replicated
- feed_lookup_grads: float32 [2048, 7168], P('fsdp')
- feed_content_grads: float32 [7168, 2048], P('fsdp')
- feed_acceptor_grads: float32 [2048, 2048], P('fsdp')
Inputs may be any that keep to these rules, and one draw needn't show every extreme that they name: `string_extents`: at least one sequence has all 128 slots valid.
All inputs are finite; a program needn't handle non-finite values.
Results may differ from a plain program's by a relative error of at most 0.018.
Values may be sent and summed in bfloat16 or wider, within the bound.
No kernel may reach another device: no remote copies, remote signals or barrier semaphores. Data moves between devices by JAX's collectives and lax.ppermute only.
A program may use at most 576 MiB of HBM per device.

v0:
```python
import jax
import jax.numpy as jnp
from jax import lax
from jax.sharding import PartitionSpec as P

ATTENTION_PARTS = 32
BLOCK = 32


norm_eps = 1e-05
group_eps = 1.0
exactness_flag = lax.Precision.HIGHEST


def layer_norm(values, norm_gain, offset):
    center = values - jnp.mean(values, axis=-1, keepdims=True)
    spread = jnp.mean(center * center, axis=-1, keepdims=True)
    return center * lax.rsqrt(spread + norm_eps) * norm_gain + offset


def shifted_rows(values):
    return jnp.concatenate([jnp.zeros_like(values[:1]), values[:-1]], axis=0)


def time_mix_inputs(
    token_inputs,
    first_scaling_factor,
    first_scaling_shift,
    lerp_factors,
    lerp_narrow_weights,
    lerp_widen_weights,
    fading_baseline,
    fading_narrow_weights,
    fading_widen_weights,
):
    normed = layer_norm(token_inputs, first_scaling_factor, first_scaling_shift)
    shift_delta = shifted_rows(normed) - normed
    blended_rows = normed + shift_delta * lerp_factors[0]
    hidden_rows = jnp.tanh(jnp.dot(blended_rows, lerp_narrow_weights, precision=exactness_flag))
    hidden_rows = hidden_rows.reshape(
        hidden_rows.shape[0], lerp_widen_weights.shape[0], lerp_widen_weights.shape[1]
    )
    start_offsets = jnp.einsum(
        "dui,uiy->udy", hidden_rows, lerp_widen_weights, precision=exactness_flag
    )
    decay_in = normed + shift_delta * (lerp_factors[1] + start_offsets[0])
    key_input_rows = normed + shift_delta * (lerp_factors[2] + start_offsets[1])
    value_input_rows = normed + shift_delta * (lerp_factors[3] + start_offsets[2])
    receptance_input_rows = normed + shift_delta * (lerp_factors[4] + start_offsets[3])
    gate_input_rows = normed + shift_delta * (lerp_factors[5] + start_offsets[4])
    decay_low = jnp.tanh(jnp.dot(decay_in, fading_narrow_weights, precision=exactness_flag))
    decay_raw = fading_baseline + jnp.dot(decay_low, fading_widen_weights, precision=exactness_flag)
    fading_exponent = -jnp.exp(decay_raw)
    return (
        receptance_input_rows,
        key_input_rows,
        value_input_rows,
        gate_input_rows,
        fading_exponent,
    )


def fading_cumulative(
    acceptor_lines, lookup_mapped, content_mapped, fading_exponent, present_reward
):
    seq_len, model_width = acceptor_lines.shape
    attention_part_width = model_width // ATTENTION_PARTS
    block_count = seq_len // BLOCK

    def to_blocks(values):
        return values.reshape(block_count, BLOCK, ATTENTION_PARTS, attention_part_width).transpose(
            0, 2, 1, 3
        )

    reward_each_part = present_reward.reshape(ATTENTION_PARTS, 1, attention_part_width)
    query_pos = lax.broadcasted_iota(jnp.int32, (BLOCK, BLOCK), 0)
    source_pos = lax.broadcasted_iota(jnp.int32, (BLOCK, BLOCK), 1)
    causal = (query_pos > source_pos)[None, :, :, None]

    def block_step(state, pieces):
        acceptor_slice, lookup_slice, value_part, decay_part = pieces
        before = jnp.cumsum(decay_part, axis=1) - decay_part
        after = before + decay_part
        block_total = after[:, -1:, :]
        carried_in = jnp.einsum(
            "hti,hij->htj", acceptor_slice * jnp.exp(before), state, precision=exactness_flag
        )
        log_gap = jnp.where(causal, before[:, :, None, :] - after[:, None, :, :], 0.0)
        weight = jnp.where(causal, jnp.exp(log_gap), 0.0)
        scores = jnp.einsum(
            "hti,hsi,htsi->hts", acceptor_slice, lookup_slice, weight, precision=exactness_flag
        )
        diagonal_contribution = jnp.sum(
            acceptor_slice * reward_each_part * lookup_slice, axis=-1, keepdims=True
        )
        result = (
            carried_in
            + jnp.einsum("hts,hsj->htj", scores, value_part, precision=exactness_flag)
            + diagonal_contribution * value_part
        )
        key_carried = lookup_slice * jnp.exp(block_total - after)
        fresh_state = jnp.einsum("hsi,hsj->hij", key_carried, value_part, precision=exactness_flag)
        new_state = jnp.exp(block_total)[:, 0, :, None] * state + fresh_state
        return (new_state, result)

    zero_state = jnp.zeros(
        (ATTENTION_PARTS, attention_part_width, attention_part_width), jnp.float32
    )
    last_state, outputs = lax.scan(
        jax.checkpoint(block_step),
        zero_state,
        (
            to_blocks(acceptor_lines),
            to_blocks(lookup_mapped),
            to_blocks(content_mapped),
            to_blocks(fading_exponent),
        ),
    )
    return outputs.transpose(0, 2, 1, 3).reshape(seq_len, model_width)


def attention_answers(
    acceptor_lines,
    lookup_mapped,
    content_mapped,
    valve_mapped,
    fading_exponent,
    present_reward,
    cluster_scaling_factor,
    cluster_scaling_shift,
):
    merged_lines = fading_cumulative(
        acceptor_lines, lookup_mapped, content_mapped, fading_exponent, present_reward
    )
    grouped = merged_lines.reshape(merged_lines.shape[0], ATTENTION_PARTS, -1)
    center = grouped - jnp.mean(grouped, axis=-1, keepdims=True)
    spread = jnp.mean(center * center, axis=-1, keepdims=True)
    normed = (center * lax.rsqrt(spread + group_eps)).reshape(merged_lines.shape)
    return (normed * cluster_scaling_factor + cluster_scaling_shift) * jax.nn.silu(valve_mapped)


def chan_inputs(residual, second_scaling_factor, second_scaling_shift_vec, feed_lerp_factors):
    normed = layer_norm(residual, second_scaling_factor, second_scaling_shift_vec)
    shift_delta = shifted_rows(normed) - normed
    return (
        normed + shift_delta * feed_lerp_factors[0],
        normed + shift_delta * feed_lerp_factors[1],
    )


def product(first_op, second_op):
    return jnp.dot(first_op, second_op, preferred_element_type=jnp.float32)


def product_tn(first_op, second_op):
    return lax.dot_general(
        first_op, second_op, (((0,), (0,)), ((), ())), preferred_element_type=jnp.float32
    )


def product_nt(first_op, second_op):
    return lax.dot_general(
        first_op, second_op, (((1,), (1,)), ((), ())), preferred_element_type=jnp.float32
    )


def flat_low(values_in):
    return values_in.reshape(-1, values_in.shape[-1]).astype(jnp.bfloat16)


def column_term(left_low, right_low):
    return product_tn(left_low, right_low)


def body(
    incoming_symbols,
    string_extents,
    adjoint_signal,
    first_scaling_factor,
    first_scaling_shift,
    lerp_factors,
    lerp_narrow_weights,
    lerp_widen_weights,
    fading_baseline,
    fading_narrow_weights,
    fading_widen_weights,
    present_reward,
    acceptor_weights,
    lookup_weights,
    content_weights,
    valve_weights,
    emission_weights,
    cluster_scaling_factor,
    cluster_scaling_shift,
    second_scaling_factor,
    second_scaling_shift_vec,
    feed_lerp_factors,
    feed_lookup_weights,
    feed_content_weights,
    feed_acceptor_weights,
):
    seq_count, seq_len, model_width = incoming_symbols.shape
    tokens_f = incoming_symbols.astype(jnp.float32)
    positions = lax.broadcasted_iota(jnp.int32, (seq_count, seq_len), 1)
    mask_rows = (positions < string_extents[:, None]).astype(jnp.float32).reshape(-1, 1)

    def unflat(values_in):
        return values_in.reshape(seq_count, seq_len, values_in.shape[-1])

    def first_piece(token_inputs, *small_params):
        return jax.vmap(lambda row_tokens: time_mix_inputs(row_tokens, *small_params))(token_inputs)

    time_in, pull_first = jax.vjp(
        first_piece,
        tokens_f,
        first_scaling_factor,
        first_scaling_shift,
        lerp_factors,
        lerp_narrow_weights,
        lerp_widen_weights,
        fading_baseline,
        fading_narrow_weights,
        fading_widen_weights,
    )
    receptance_input_rows, key_input_rows, value_input_rows, gate_input_rows, fading_exponent = (
        time_in
    )
    recept_full, key_full, value_full, gate_full, output_full = (
        lax.all_gather(acceptor_weights, "fsdp", axis=0, tiled=True),
        lax.all_gather(lookup_weights, "fsdp", axis=0, tiled=True),
        lax.all_gather(content_weights, "fsdp", axis=0, tiled=True),
        lax.all_gather(valve_weights, "fsdp", axis=0, tiled=True),
        lax.all_gather(emission_weights, "fsdp", axis=0, tiled=True),
    )
    recept_low = flat_low(receptance_input_rows)
    key_low = flat_low(key_input_rows)
    value_low = flat_low(value_input_rows)
    gate_low = flat_low(gate_input_rows)
    acceptor_lines = unflat(product(recept_low, recept_full))
    lookup_mapped = unflat(product(key_low, key_full))
    content_mapped = unflat(product(value_low, value_full))
    valve_mapped = unflat(product(gate_low, gate_full))

    def middle_piece(
        receptance_operand,
        key_operand,
        value_operand,
        gate_operand,
        decay_operand,
        reward_argument,
        gain_operand,
        bias_operand,
    ):
        return jax.vmap(
            lambda receptance_per_row, key_per_row, value_per_row, gate_per_row, decay_per_row: attention_answers(
                receptance_per_row,
                key_per_row,
                value_per_row,
                gate_per_row,
                decay_per_row,
                reward_argument,
                gain_operand,
                bias_operand,
            )
        )(receptance_operand, key_operand, value_operand, gate_operand, decay_operand)

    merged_lines, pull_middle = jax.vjp(
        middle_piece,
        acceptor_lines,
        lookup_mapped,
        content_mapped,
        valve_mapped,
        fading_exponent,
        present_reward,
        cluster_scaling_factor,
        cluster_scaling_shift,
    )
    mixed_low = flat_low(merged_lines)
    residual = tokens_f + unflat(product(mixed_low, output_full))

    def chan_piece(resid_arg, gain_operand, bias_operand, shift_arg):
        return jax.vmap(
            lambda resid_row: chan_inputs(resid_row, gain_operand, bias_operand, shift_arg)
        )(resid_arg)

    chan_in, pull_chan = jax.vjp(
        chan_piece, residual, second_scaling_factor, second_scaling_shift_vec, feed_lerp_factors
    )
    key_chan_low = flat_low(chan_in[0])
    recept_chan_low = flat_low(chan_in[1])
    chan_key_full, chan_value_full, chan_recept_full = (
        lax.all_gather(feed_lookup_weights, "fsdp", axis=0, tiled=True),
        lax.all_gather(feed_content_weights, "fsdp", axis=0, tiled=True),
        lax.all_gather(feed_acceptor_weights, "fsdp", axis=0, tiled=True),
    )
    key_act = product(key_chan_low, chan_key_full)
    softened = jax.nn.softplus(key_act)
    squared_low = (softened * softened).astype(jnp.bfloat16)
    value_act = product(squared_low, chan_value_full)
    gate_sig = jax.nn.sigmoid(product(recept_chan_low, chan_recept_full))
    flat_resid = residual.reshape(-1, model_width)
    layer_output = unflat((flat_resid + gate_sig * value_act) * mask_rows)
    d_output = adjoint_signal.astype(jnp.float32).reshape(-1, model_width) * mask_rows
    d_value_low = (d_output * gate_sig).astype(jnp.bfloat16)
    d_gate_low = (d_output * value_act * gate_sig * (1.0 - gate_sig)).astype(jnp.bfloat16)
    (
        recept_full,
        key_full,
        value_full,
        gate_full,
        output_full,
        chan_key_full,
        chan_value_full,
        chan_recept_full,
    ) = (
        lax.all_gather(acceptor_weights, "fsdp", axis=0, tiled=True),
        lax.all_gather(lookup_weights, "fsdp", axis=0, tiled=True),
        lax.all_gather(content_weights, "fsdp", axis=0, tiled=True),
        lax.all_gather(valve_weights, "fsdp", axis=0, tiled=True),
        lax.all_gather(emission_weights, "fsdp", axis=0, tiled=True),
        lax.all_gather(feed_lookup_weights, "fsdp", axis=0, tiled=True),
        lax.all_gather(feed_content_weights, "fsdp", axis=0, tiled=True),
        lax.all_gather(feed_acceptor_weights, "fsdp", axis=0, tiled=True),
    )
    d_key_low = (
        product_nt(d_value_low, chan_value_full) * (2.0 * softened * jax.nn.sigmoid(key_act))
    ).astype(jnp.bfloat16)
    feed_content_grads = lax.psum_scatter(
        column_term(squared_low, d_value_low).astype(jnp.bfloat16),
        "fsdp",
        scatter_dimension=0,
        tiled=True,
    )
    feed_lookup_grads = lax.psum_scatter(
        column_term(key_chan_low, d_key_low).astype(jnp.bfloat16),
        "fsdp",
        scatter_dimension=0,
        tiled=True,
    )
    feed_acceptor_grads = lax.psum_scatter(
        column_term(recept_chan_low, d_gate_low).astype(jnp.bfloat16),
        "fsdp",
        scatter_dimension=0,
        tiled=True,
    )
    d_key_chan = unflat(product_nt(d_key_low, chan_key_full))
    d_recept_chan = unflat(product_nt(d_gate_low, chan_recept_full))
    d_resid_chan, second_scaling_factor_grads, second_scaling_shift_grads, feed_lerp_grads = (
        pull_chan((d_key_chan, d_recept_chan))
    )
    d_residual = unflat(d_output) + d_resid_chan
    d_branch_low = flat_low(d_residual)
    emission_weights_grads = product_tn(mixed_low, d_branch_low)
    d_mixed = unflat(product_nt(d_branch_low, output_full))
    (
        d_recept,
        d_key_proj,
        d_value_proj,
        d_gate_proj,
        d_decay,
        present_reward_grads,
        cluster_scaling_factor_grads,
        cluster_scaling_shift_grads,
    ) = pull_middle(d_mixed)
    d_recept_low = flat_low(d_recept)
    d_key_proj_low = flat_low(d_key_proj)
    d_value_proj_low = flat_low(d_value_proj)
    d_gate_proj_low = flat_low(d_gate_proj)
    acceptor_weights_grads = product_tn(recept_low, d_recept_low)
    lookup_weights_grads = product_tn(key_low, d_key_proj_low)
    content_weights_grads = product_tn(value_low, d_value_proj_low)
    valve_weights_grads = product_tn(gate_low, d_gate_proj_low)
    first_grads = pull_first(
        (
            unflat(product_nt(d_recept_low, recept_full)),
            unflat(product_nt(d_key_proj_low, key_full)),
            unflat(product_nt(d_value_proj_low, value_full)),
            unflat(product_nt(d_gate_proj_low, gate_full)),
            d_decay,
        )
    )
    token_grad = d_residual + first_grads[0]
    time_shards = (
        lax.psum_scatter(
            acceptor_weights_grads.astype(jnp.bfloat16), "fsdp", scatter_dimension=0, tiled=True
        ).astype(jnp.float32),
        lax.psum_scatter(
            lookup_weights_grads.astype(jnp.bfloat16), "fsdp", scatter_dimension=0, tiled=True
        ).astype(jnp.float32),
        lax.psum_scatter(
            content_weights_grads.astype(jnp.bfloat16), "fsdp", scatter_dimension=0, tiled=True
        ).astype(jnp.float32),
        lax.psum_scatter(
            valve_weights_grads.astype(jnp.bfloat16), "fsdp", scatter_dimension=0, tiled=True
        ).astype(jnp.float32),
        lax.psum_scatter(
            emission_weights_grads.astype(jnp.bfloat16), "fsdp", scatter_dimension=0, tiled=True
        ).astype(jnp.float32),
    )
    summed = (
        lax.psum(time_shards[0].astype(jnp.bfloat16), "rep").astype(jnp.float32),
        lax.psum(time_shards[1].astype(jnp.bfloat16), "rep").astype(jnp.float32),
        lax.psum(time_shards[2].astype(jnp.bfloat16), "rep").astype(jnp.float32),
        lax.psum(time_shards[3].astype(jnp.bfloat16), "rep").astype(jnp.float32),
        lax.psum(time_shards[4].astype(jnp.bfloat16), "rep").astype(jnp.float32),
        lax.psum(feed_lookup_grads, "rep").astype(jnp.float32),
        lax.psum(feed_content_grads, "rep").astype(jnp.float32),
        lax.psum(feed_acceptor_grads, "rep").astype(jnp.float32),
    )
    small_summed = lax.psum(
        (
            first_grads[1],
            first_grads[2],
            first_grads[3],
            first_grads[4],
            first_grads[5],
            first_grads[6],
            first_grads[7],
            first_grads[8],
            present_reward_grads,
            cluster_scaling_factor_grads,
            cluster_scaling_shift_grads,
            second_scaling_factor_grads,
            second_scaling_shift_grads,
            feed_lerp_grads,
        ),
        ("fsdp", "rep"),
    )
    return (
        layer_output,
        token_grad,
        small_summed[0],
        small_summed[1],
        small_summed[2],
        small_summed[3],
        small_summed[4],
        small_summed[5],
        small_summed[6],
        small_summed[7],
        small_summed[8],
        summed[0],
        summed[1],
        summed[2],
        summed[3],
        summed[4],
        small_summed[9],
        small_summed[10],
        small_summed[11],
        small_summed[12],
        small_summed[13],
        summed[5],
        summed[6],
        summed[7],
    )


def solution(mesh):
    in_specs = (
        P(("fsdp", "rep"), None, None),
        P(("fsdp", "rep")),
        P(("fsdp", "rep"), None, None),
        P(),
        P(),
        P(),
        P(),
        P(),
        P(),
        P(),
        P(),
        P(),
        P("fsdp", None),
        P("fsdp", None),
        P("fsdp", None),
        P("fsdp", None),
        P("fsdp", None),
        P(),
        P(),
        P(),
        P(),
        P(),
        P("fsdp", None),
        P("fsdp", None),
        P("fsdp", None),
    )
    out_specs = (
        P(("fsdp", "rep"), None, None),
        P(("fsdp", "rep"), None, None),
        P(),
        P(),
        P(),
        P(),
        P(),
        P(),
        P(),
        P(),
        P(),
        P("fsdp", None),
        P("fsdp", None),
        P("fsdp", None),
        P("fsdp", None),
        P("fsdp", None),
        P(),
        P(),
        P(),
        P(),
        P(),
        P("fsdp", None),
        P("fsdp", None),
        P("fsdp", None),
    )
    return jax.shard_map(body, mesh=mesh, in_specs=in_specs, out_specs=out_specs, check_vma=False)
```

profile of v0, /device:TPU:0, one launch (start us, length us, event | category | flops | bytes accessed | tf_op | source)
XLA Modules:
  0.0 2569.4 jit_solution(13067016218265335027)
XLA Ops:
  36.8 30.2 %all-gather.9.cloned.1.call-done = bf16[2048,2048]{1,0:T(8,128)(2,1)} async-done(((bf16[256,2048]{1,0:T(8,128)(2,1)}), bf16[2048,2048]{1,0:T(8,128)(2,1)}) %all-gather.9.cloned.1.call-update) | async-done | bytes 8388624 | tf_op jit(solution)/shard_map/all_gather | solution.py:230
  79.4 44.0 %all-gather.11.cloned.1.call-done = bf16[2048,2048]{1,0:T(8,128)(2,1)} async-done(((bf16[256,2048]{1,0:T(8,128)(2,1)}), bf16[2048,2048]{1,0:T(8,128)(2,1)}) %all-gather.11.cloned.1.call-update) | async-done | bytes 8388624 | tf_op jit(solution)/shard_map/all_gather | solution.py:231
  135.7 44.0 %all-gather.13.cloned.1.call-done = bf16[2048,2048]{1,0:T(8,128)(2,1)} async-done(((bf16[256,2048]{1,0:T(8,128)(2,1)}), bf16[2048,2048]{1,0:T(8,128)(2,1)}) %all-gather.13.cloned.1.call-update) | async-done | bytes 8388624 | tf_op jit(solution)/shard_map/all_gather | solution.py:229
  179.7 12.4 copy.234
  213.8 132.6 %while.44 = (s32[]{:T(128)}, f32[1,32,64,64]{3,2,1,0:T(8,128)S(1)}, f32[4,1,32,32,64]{4,3,2,1,0:T(8,128)}, f32[4,1,32,64,64]{4,3,2,1,0:T(8,128)}, f32[4,1,32,32,...) while((s32[]{:T(128)}, f32[1,32,64,64]{3,2,1,0:T(8,128)S(1)}, ...), condition=%wide.region_5.6_spmd.clone.clone, body=%wide.region_2.5_spmd.clone.clone.sunk | while | flops 141790208 | bytes 35464388 | solution.py:109
  224.9 12.5 fusion.307
  258.1 12.5 fusion.307
  291.2 12.5 fusion.307
  324.2 12.5 fusion.307
  384.4 108.8 %all-gather.21.cloned.1.call-done = bf16[2048,7168]{1,0:T(8,128)(2,1)} async-done(((bf16[256,7168]{1,0:T(8,128)(2,1)}), bf16[2048,7168]{1,0:T(8,128)(2,1)}) %all-gather.21.cloned.1.call-update) | async-done | bytes 29360144 | tf_op jit(solution)/shard_map/all_gather | solution.py:292
  493.2 16.4 fusion.171
  509.6 128.6 %all-gather.23.cloned.1.call-done = bf16[7168,2048]{1,0:T(8,128)(2,1)} async-done(((bf16[896,2048]{1,0:T(8,128)(2,1)}), bf16[7168,2048]{1,0:T(8,128)(2,1)}) %all-gather.23.cloned.1.call-update) | async-done | bytes 29360144 | tf_op jit(solution)/shard_map/all_gather | solution.py:293
  638.1 17.6 fusion.95
  663.5 15.7 fusion.68
  679.2 16.8 fusion.173
  738.2 236.4 %while.43 = (s32[]{:T(128)}, f32[32,1,64]{2,1,0:T(1,128)S(1)}, f32[1,32,64,64]{2,3,1,0:T(8,128)}, bf16[4,1,32,32,64]{4,3,2,1,0:T(8,128)(2,1)}, bf16[4,1,32,32,64...) while((s32[]{:T(128)}, f32[32,1,64]{2,1,0:T(1,128)S(1)}, ...), condition=%wide.region_24.25_spmd.clone, body=%wide.region_14.0_spmd.clone.sunk | while | flops 309429248 | bytes 48480696 | solution.py:109
  750.3 18.1 fusion.290
  809.6 18.1 fusion.290
  868.8 18.1 fusion.290
  928.1 18.1 fusion.290
  1026.0 15.2 convolution_convert_fusion.1
  1042.3 16.6 convolution_convert_fusion
  1059.0 71.4 %reduce-scatter.11.cloned.1.call-done = bf16[256,2048]{1,0:T(8,128)(2,1)} async-done(((bf16[2048,2048]{1,0:T(8,128)(2,1)}), bf16[256,2048]{1,0:T(8,128)(2,1)}) %reduce-scatter.11.cloned.1.call-update) | async-done | bytes 1048592 | tf_op jit(solution)/shard_map/reduce_scatter | solution.py:387
  1130.4 74.8 %reduce-scatter.13.cloned.1.call-done = bf16[256,2048]{1,0:T(8,128)(2,1)} async-done(((bf16[2048,2048]{1,0:T(8,128)(2,1)}), bf16[256,2048]{1,0:T(8,128)(2,1)}) %reduce-scatter.13.cloned.1.call-update) | async-done | bytes 1048592 | tf_op jit(solution)/shard_map/reduce_scatter | solution.py:390
  1205.1 75.0 %reduce-scatter.15.cloned.1.call-done = bf16[256,2048]{1,0:T(8,128)(2,1)} async-done(((bf16[2048,2048]{1,0:T(8,128)(2,1)}), bf16[256,2048]{1,0:T(8,128)(2,1)}) %reduce-scatter.15.cloned.1.call-update) | async-done | bytes 1048592 | tf_op jit(solution)/shard_map/reduce_scatter | solution.py:393
  1280.1 74.7 %reduce-scatter.17.cloned.1.call-done = bf16[256,2048]{1,0:T(8,128)(2,1)} async-done(((bf16[2048,2048]{1,0:T(8,128)(2,1)}), bf16[256,2048]{1,0:T(8,128)(2,1)}) %reduce-scatter.17.cloned.1.call-update) | async-done | bytes 1048592 | tf_op jit(solution)/shard_map/reduce_scatter | solution.py:396
  1354.9 75.0 %reduce-scatter.23.cloned.1.call-done = bf16[256,2048]{1,0:T(8,128)(2,1)} async-done(((bf16[2048,2048]{1,0:T(8,128)(2,1)}), bf16[256,2048]{1,0:T(8,128)(2,1)}) %reduce-scatter.23.cloned.1.call-update) | async-done | bytes 1048592 | tf_op jit(solution)/shard_map/reduce_scatter | solution.py:340
  1429.9 182.3 %reduce-scatter.19.cloned.1.call-done = bf16[256,7168]{1,0:T(8,128)(2,1)} async-done(((bf16[2048,7168]{1,0:T(8,128)(2,1)}), bf16[256,7168]{1,0:T(8,128)(2,1)}) %reduce-scatter.19.cloned.1.call-update) | async-done | bytes 3670032 | tf_op jit(solution)/shard_map/reduce_scatter | solution.py:334
  1612.2 182.3 %reduce-scatter.21.cloned.1.call-done = bf16[896,2048]{1,0:T(8,128)(2,1)} async-done(((bf16[7168,2048]{1,0:T(8,128)(2,1)}), bf16[896,2048]{1,0:T(8,128)(2,1)}) %reduce-scatter.21.cloned.1.call-update) | async-done | bytes 3670032 | tf_op jit(solution)/shard_map/reduce_scatter | solution.py:328
  1865.6 396.8 %all-reduce.29.cloned.1.call-done = (bf16[256,2048]{1,0:T(8,128)(2,1)}, bf16[256,2048]{1,0:T(8,128)(2,1)}, bf16[256,2048]{1,0:T(8,128)(2,1)}, bf16[256,2048]{1,0...) async-done(((bf16[256,2048]{1,0:T(8,128)(2,1)}, bf16[256,2048]{1,0:T(8,128)(2,1)}, ...) | async-done | bytes 13631504 | tf_op jit(solution)/shard_map/psum | solution.py:401
  2282.3 113.4 %all-reduce.25.cloned.1.call-done = (f32[2048]{0:T(1024)}, f32[2048]{0:T(1024)}, f32[6,2048]{1,0:T(8,128)}, f32[2048]{0:T(1024)}, f32[2048]{0:T(1024)}, /*index=...) async-done(((f32[2048]{0:T(1024)}, f32[2048]{0:T(1024)}, f32[6,2048]{1,0:T(8,128)}, f32[2048]{0:T(1024)}, f32[2048]{0:T(1024)}, ...) | async-done | bytes 131088 | tf_op jit(solution)/shard_map/psum | solution.py:410
  2395.7 151.9 %all-reduce.27.cloned.1.call-done = (f32[2048,160]{0,1:T(8,128)}, f32[5,32,2048]{2,1,0:T(8,128)}, f32[2048,64]{0,1:T(8,128)}, f32[64,2048]{1,0:T(8,128)}) async-done(((f32[2048,160]{0,1:T(8,128)}, f32[5,32,2048]{2,1,0:T(8,128)}, f32[2048,64]{0,1:T(8,128)}, f32[64,2048]{1,0:T(8,128)}), (f32[2048,160]{0,1:T(8,128)}, f32[5,32,2048]{2,1,0:T(8,128)}, f32[2048,64]{0,1:T(8,128)}, ...) | async-done | bytes 3670032 | tf_op jit(solution)/shard_map/psum | solution.py:410
  (727 shorter events, 564.8 us)
Async XLA Ops:
  7.2 59.9 %all-gather.9.cloned.1.call-start = ((), (), s32[]{:S(2)}) async-start(), calls=%async_computation.8 | async-start | bytes 9437184 | tf_op jit(solution)/shard_map/all_gather | solution.py:230
  7.9 115.4 %all-gather.11.cloned.1.call-start = ((), (), s32[]{:S(2)}) async-start(), calls=%async_computation.9 | async-start | bytes 9437184 | tf_op jit(solution)/shard_map/all_gather | solution.py:231
  8.7 171.0 %all-gather.13.cloned.1.call-start = ((), (), s32[]{:S(2)}) async-start(), calls=%async_computation.10 | async-start | bytes 9437184 | tf_op jit(solution)/shard_map/all_gather | solution.py:229
  9.4 354.0 %all-gather.15.cloned.1.call-start = ((), (), s32[]{:S(2)}) async-start(), calls=%async_computation.11 | async-start | bytes 9437184 | tf_op jit(solution)/shard_map/all_gather | solution.py:232
  10.0 361.2 %all-gather.17.cloned.1.call-start = ((), (), s32[]{:S(2)}) async-start(), calls=%async_computation.12 | async-start | bytes 9437184 | tf_op jit(solution)/shard_map/all_gather | solution.py:233
  10.6 367.8 %all-gather.19.cloned.1.call-start = ((), (), s32[]{:S(2)}) async-start(), calls=%async_computation.13 | async-start | bytes 9437184 | tf_op jit(solution)/shard_map/all_gather | solution.py:294
  11.2 482.0 %all-gather.21.cloned.1.call-start = ((), (), s32[]{:S(2)}) async-start(), calls=%async_computation.14 | async-start | bytes 33030144 | tf_op jit(solution)/shard_map/all_gather | solution.py:292
  12.0 626.2 %all-gather.23.cloned.1.call-start = ((), (), s32[]{:S(2)}) async-start(), calls=%async_computation.15 | async-start | bytes 33030144 | tf_op jit(solution)/shard_map/all_gather | solution.py:293
  12.7 1046.3 %reduce-scatter.9.cloned.1.call-start = ((), (), s32[]{:S(2)}) async-start(), calls=%async_computation.16 | async-start | bytes 9437184 | tf_op jit(solution)/shard_map/reduce_scatter | solution.py:384
  26.8 174.4 %copy-start.55 = (bf16[1,128,2048]{2,1,0:T(8,128)(2,1)}, bf16[1,128,2048]{2,1,0:T(8,128)(2,1)S(1)}, u32[]{:S(2)}) copy-start(bf16[1,128,2048]{2,1,0:T(8,128)(2,1)S(1)} %get-tuple-element.821) | copy-start | bytes 1572868
  29.0 50.4 %copy-start.94 = (f32[128,64]{0,1:T(8,128)}, f32[128,64]{0,1:T(8,128)S(1)}, u32[]{:S(2)}) copy-start(f32[128,64]{0,1:T(8,128)S(1)} %convolution_tanh_fusion.1) | copy-start | bytes 98308
  378.3 114.8 %copy-start.38 = (bf16[128,2048]{1,0:T(8,128)(2,1)}, bf16[128,2048]{1,0:T(8,128)(2,1)S(1)}, u32[]{:S(2)}) copy-start(bf16[128,2048]{1,0:T(8,128)(2,1)S(1)} %get-tuple-element.837) | copy-start | bytes 1572868
  493.2 145.0 %copy-start.64 = (bf16[1,128,2048]{2,1,0:T(8,128)(2,1)S(1)}, bf16[1,128,2048]{2,1,0:T(8,128)(2,1)}, u32[]{:S(2)}) copy-start(bf16[1,128,2048]{2,1,0:T(8,128)(2,1)} %param.31) | copy-start | bytes 1572868
  984.0 146.4 %reduce-scatter.11.cloned.1.call-start = ((), (), s32[]{:S(2)}) async-start(), calls=%async_computation.17 | async-start | bytes 9437184 | tf_op jit(solution)/shard_map/reduce_scatter | solution.py:387
  994.1 211.0 %reduce-scatter.13.cloned.1.call-start = ((), (), s32[]{:S(2)}) async-start(), calls=%async_computation.18 | async-start | bytes 9437184 | tf_op jit(solution)/shard_map/reduce_scatter | solution.py:390
  1003.7 276.4 %reduce-scatter.15.cloned.1.call-start = ((), (), s32[]{:S(2)}) async-start(), calls=%async_computation.19 | async-start | bytes 9437184 | tf_op jit(solution)/shard_map/reduce_scatter | solution.py:393
  1010.8 344.1 %reduce-scatter.17.cloned.1.call-start = ((), (), s32[]{:S(2)}) async-start(), calls=%async_computation.20 | async-start | bytes 9437184 | tf_op jit(solution)/shard_map/reduce_scatter | solution.py:396
  1017.6 412.3 %reduce-scatter.23.cloned.1.call-start = ((), (), s32[]{:S(2)}) async-start(), calls=%async_computation.23 | async-start | bytes 9437184 | tf_op jit(solution)/shard_map/reduce_scatter | solution.py:340
  1024.6 587.6 %reduce-scatter.19.cloned.1.call-start = ((), (), s32[]{:S(2)}) async-start(), calls=%async_computation.21 | async-start | bytes 33030144 | tf_op jit(solution)/shard_map/reduce_scatter | solution.py:334
  1041.3 753.2 %reduce-scatter.21.cloned.1.call-start = ((), (), s32[]{:S(2)}) async-start(), calls=%async_computation.22 | async-start | bytes 33030144 | tf_op jit(solution)/shard_map/reduce_scatter | solution.py:328
  1058.9 1203.4 %all-reduce.29.cloned.1.call-start = ((), (), s32[]{:S(2)}) async-start(), calls=%async_computation.26 | async-start | bytes 27262976 | tf_op jit(solution)/shard_map/psum | solution.py:401
  1794.5 601.2 %all-reduce.25.cloned.1.call-start = ((), (), s32[]{:S(2)}) async-start(), calls=%async_computation.24 | async-start | bytes 294912 | tf_op jit(solution)/shard_map/psum | solution.py:410
  1806.2 26.0 %copy-start.20 = (f32[128,2048]{1,0:T(8,128)}, f32[128,2048]{1,0:T(8,128)S(1)}, u32[]{:S(2)}) copy-start(f32[128,2048]{1,0:T(8,128)S(1)} %fusion.178) | copy-start | bytes 3145732
  1813.0 19.2 copy-start.14
  1859.9 687.8 %all-reduce.27.cloned.1.call-start = ((), (), s32[]{:S(2)}) async-start(), calls=%async_computation.25 | async-start | bytes 7340032 | tf_op jit(solution)/shard_map/psum | solution.py:410
  2395.7 161.1 %copy-start.140 = (f32[2048]{0:T(1024)S(1)}, f32[2048]{0:T(1024)}, u32[]{:S(2)}) copy-start(f32[2048]{0:T(1024)} %get-tuple-element.1176) | copy-start | bytes 24580
  2395.7 163.3 %copy-start.139 = (f32[2048]{0:T(1024)S(1)}, f32[2048]{0:T(1024)}, u32[]{:S(2)}) copy-start(f32[2048]{0:T(1024)} %get-tuple-element.1179) | copy-start | bytes 24580
  2395.7 163.9 %copy-start.138 = (f32[2048]{0:T(1024)S(1)}, f32[2048]{0:T(1024)}, u32[]{:S(2)}) copy-start(f32[2048]{0:T(1024)} %get-tuple-element.1185) | copy-start | bytes 24580
  2395.7 164.5 %copy-start.137 = (f32[2048]{0:T(1024)S(1)}, f32[2048]{0:T(1024)}, u32[]{:S(2)}) copy-start(f32[2048]{0:T(1024)} %get-tuple-element.1186) | copy-start | bytes 24580
  2395.7 165.1 %copy-start.136 = (f32[2048]{0:T(1024)S(1)}, f32[2048]{0:T(1024)}, u32[]{:S(2)}) copy-start(f32[2048]{0:T(1024)} %get-tuple-element.1187) | copy-start | bytes 24580
  2395.7 165.7 %copy-start.135 = (f32[2048]{0:T(1024)S(1)}, f32[2048]{0:T(1024)}, u32[]{:S(2)}) copy-start(f32[2048]{0:T(1024)} %get-tuple-element.1188) | copy-start | bytes 24580
  2395.7 166.3 %copy-start.130 = (f32[2,2048]{1,0:T(2,128)S(1)}, f32[2,2048]{1,0:T(2,128)}, u32[]{:S(2)}) copy-start(f32[2,2048]{1,0:T(2,128)} %get-tuple-element.1189) | copy-start | bytes 49156
  (173 other events, 973.7 us)
Sparse Core Ops, SparseCore 0:
  9.9 57.0 all-gather.8
  68.9 54.3 all-gather.10
  125.3 54.3 all-gather.12
  181.4 54.3 all-gather.14
  237.6 54.3 all-gather.16
  293.8 54.3 all-gather.18
  350.1 143.0 all-gather.20
  495.0 143.0 all-gather.22
  984.1 71.2 reduce-scatter.8
  1059.1 71.2 reduce-scatter.10
  1133.8 71.2 reduce-scatter.12
  1208.8 71.2 reduce-scatter.14
  1283.6 71.2 reduce-scatter.16
  1358.6 71.2 reduce-scatter.22
  1433.4 178.7 reduce-scatter.18
  1615.7 178.7 reduce-scatter.20
  1797.8 464.5 all-reduce.28
  2270.4 125.2 all-reduce.24
  2403.9 143.7 all-reduce.26
where the time goes:
time: 2580 us; the launch traced here: 2570 us
  waiting for transfers between devices  1760 us (68%)
  other arithmetic  325 us (13%)
  matrix products  315 us (12%)
  local copies, waits for them, and re-layouts  152 us (6%)
    psum x1, waiting for transfers between devices, body(): lax.psum(time_shards[0].astype(jnp.bfloat16), 'rep').astype(jnp.float32)  397 us
    psum x2, waiting for transfers between devices, body(): lax.psum((first_grads[1], first_grads[2], first_grads[3], first_grads[4],...  265 us
    reduce_scatter x1, waiting for transfers between devices, body(): lax.psum_scatter(column_term(key_chan_low, d_key_low).astype(jnp.bfloat16...  182 us
    reduce_scatter x1, waiting for transfers between devices, body(): lax.psum_scatter(column_term(squared_low, d_value_low).astype(jnp.bfloat1...  182 us
    all_gather x1, waiting for transfers between devices, body(): lax.all_gather(feed_content_weights, 'fsdp', axis=0, tiled=True)  129 us
    dot_general x12, other arithmetic, block_step(): jnp.einsum('hti,hsi,htsi->hts', acceptor_slice, lookup_slice, weight, pre...  123 us
    all_gather x1, waiting for transfers between devices, body(): lax.all_gather(feed_lookup_weights, 'fsdp', axis=0, tiled=True)  109 us
    reduce_scatter x1, waiting for transfers between devices, body(): lax.psum_scatter(valve_weights_grads.astype(jnp.bfloat16), 'fsdp', scatte...  75 us
  transfers between devices with their start and end apart: 19, of which 15 were waited for; matrix products, arithmetic and copies ran while one was open for 16% of the time, Pallas kernels for 0%

commit v1 on v0

v1 whole, which is shorter than its diff:
```python
import functools

import jax
import jax.numpy as jnp
import numpy as np
from jax import lax
from jax.experimental import pallas as pl
from jax.experimental.pallas import tpu as pltpu
from jax.sharding import PartitionSpec as P

HEADS = 32
norm_eps = 1e-05
group_eps = 1.0
BF = jnp.bfloat16
F32 = jnp.float32
MIB = 1 << 20


def mm(a, b):
    return jnp.dot(a, b, preferred_element_type=F32)


def mm_nt(a, b):
    return lax.dot_general(a, b, (((1,), (1,)), ((), ())), preferred_element_type=F32)


def mm_tn(a, b):
    return lax.dot_general(a, b, (((0,), (0,)), ((), ())), preferred_element_type=F32)


def halves(v):
    high = v.astype(BF)
    return high, (v - high.astype(F32)).astype(BF)


def gather_rows(v):
    return lax.all_gather(v, "fsdp", axis=0, tiled=True)


def gather_cols(v):
    return lax.all_gather(v, "fsdp", axis=1, tiled=True)


def scatter_rows(v):
    return lax.psum_scatter(v, "fsdp", scatter_dimension=0, tiled=True)


def scatter_cols(v):
    return lax.psum_scatter(v, "fsdp", scatter_dimension=1, tiled=True)


def exchange(take, put, out):
    n = lax.axis_size("fsdp")
    me = lax.axis_index("fsdp")
    out = put(out, me, take(me))
    for m in range(1, n):
        got = lax.ppermute(take(me ^ m), "fsdp", [(i, i ^ m) for i in range(n)])
        out = put(out, me ^ m, got)
    return out


def rows_to_cols(v):
    n = lax.axis_size("fsdp")
    if n > 8:
        return lax.all_to_all(v, "fsdp", split_axis=1, concat_axis=0, tiled=True)
    r, c = v.shape[0], v.shape[1] // n
    return exchange(
        lambda j: lax.dynamic_slice_in_dim(v, j * c, c, 1),
        lambda out, j, b: lax.dynamic_update_slice_in_dim(out, b, j * r, 0),
        jnp.zeros((r * n, c), v.dtype),
    )


def cols_to_rows(v):
    n = lax.axis_size("fsdp")
    if n > 8:
        return lax.all_to_all(v, "fsdp", split_axis=0, concat_axis=1, tiled=True)
    r, c = v.shape[0] // n, v.shape[1]
    return exchange(
        lambda j: lax.dynamic_slice_in_dim(v, j * r, r, 0),
        lambda out, j, b: lax.dynamic_update_slice_in_dim(out, b, j * c, 1),
        jnp.zeros((r, c * n), v.dtype),
    )


def hold(*values):
    return lax.optimization_barrier(values)


def rep_scatter_rows(v):
    return lax.psum_scatter(v, "rep", scatter_dimension=0, tiled=True)


def rep_scatter_cols(v):
    n, z = lax.axis_size("fsdp"), lax.axis_size("rep")
    rows, c = v.shape
    v = v.reshape(n, z, rows // (n * z), c).transpose(1, 0, 2, 3).reshape(rows, c)
    return lax.psum_scatter(v, "rep", scatter_dimension=0, tiled=True)


def rep_gather(v):
    n = lax.axis_size("rep")
    z = lax.axis_index("rep")
    up, down = [v], [v]
    for s in range(1, n):
        up.append(lax.ppermute(up[-1], "rep", [(i, i + 1) for i in range(s - 1, n - 1)]))
        down.append(lax.ppermute(down[-1], "rep", [(i + 1, i) for i in range(n - s)]))
    out = jnp.zeros((n,) + v.shape, F32)
    out = lax.dynamic_update_index_in_dim(out, v.astype(F32), z, 0)
    for s in range(1, n):
        piece = jnp.where(z >= s, up[s], down[n - s]).astype(F32)
        out = lax.dynamic_update_index_in_dim(out, piece, lax.rem(z - s + n, n), 0)
    return out.reshape((n * v.shape[0],) + v.shape[1:])


def whole_block(a):
    return pl.BlockSpec(a.shape, lambda *_: (0,) * a.ndim, pipeline_mode=pl.Buffered(1))


def shifted(v):
    first = lax.broadcasted_iota(jnp.int32, v.shape, 0) == 0
    return jnp.where(first, 0.0, pltpu.roll(v, 1, 0))


def shifted_back(v):
    last = lax.broadcasted_iota(jnp.int32, v.shape, 0) == v.shape[0] - 1
    return jnp.where(last, 0.0, pltpu.roll(v, v.shape[0] - 1, 0))


def normal_rows(v):
    center = v - jnp.mean(v, axis=-1, keepdims=True)
    spread = jnp.mean(center * center, axis=-1, keepdims=True)
    return center * lax.rsqrt(spread + norm_eps)


def front_kernel(
    ranks, tok, gain, shift, lerp, narrow, widen, fnarrow, xk, xv, xr, xg, hid, low
):
    normed = normal_rows(tok[...].astype(F32)) * gain[...] + shift[...]
    delta = shifted(normed) - normed
    bh, bl = halves(normed + delta * lerp[0:1, :])
    wide = ranks * 5
    pre = mm(bh, narrow[...])
    hidden = jnp.tanh(pre[:, :wide] + pre[:, wide:] + mm(bl, narrow[:, :wide]))
    hid[...] = hidden
    hb = hidden.astype(BF)
    for f, out in ((1, xk), (2, xv), (3, xr), (4, xg), (0, None)):
        rows = slice(f * ranks, (f + 1) * ranks)
        x = normed + delta * (lerp[f + 1 : f + 2, :] + mm(hb[:, rows], widen[rows, :]))
        if out is not None:
            out[...] = x.astype(BF)
        else:
            dh, dl = halves(x)
            fd = low.shape[1]
            pre = mm(dh, fnarrow[...])
            low[...] = jnp.tanh(pre[:, :fd] + pre[:, fd:] + mm(dl, fnarrow[:, :fd]))


def front(seq_len, tokens, gain, shift, lerp, narrow, widen, fnarrow):
    g, d = tokens.shape
    ranks = widen.shape[0] // 5
    fd = fnarrow.shape[1] // 2
    per_seq = lambda w: pl.BlockSpec((seq_len, w), lambda s: (s, 0))
    return pl.pallas_call(
        functools.partial(front_kernel, ranks),
        grid=(g // seq_len,),
        in_specs=[per_seq(d)]
        + [whole_block(a) for a in (gain, shift, lerp, narrow, widen, fnarrow)],
        out_specs=[per_seq(d)] * 4 + [per_seq(5 * ranks), per_seq(fd)],
        out_shape=[jax.ShapeDtypeStruct((g, d), BF)] * 4
        + [
            jax.ShapeDtypeStruct((g, 5 * ranks), F32),
            jax.ShapeDtypeStruct((g, fd), F32),
        ],
        compiler_params=pltpu.CompilerParams(vmem_limit_bytes=48 * MIB),
        cost_estimate=pl.CostEstimate(
            flops=g * d * 2 * 5 * 256, bytes_accessed=g * d * 10, transcendentals=0
        ),
        name="token_shift",
    )(tokens, gain, shift, lerp, narrow, widen, fnarrow)


def back_kernel(
    ranks,
    tok,
    hid,
    low,
    dk,
    dv,
    dr,
    dg,
    draw,
    gain,
    shift,
    lerp,
    narrow,
    widen,
    fnarrow,
    fwiden,
    wk,
    wv,
    wr,
    wg,
    dn_out,
    vec_out,
    dwid_out,
    dnar_out,
    dfn_out,
):
    @pl.when(pl.program_id(0) == 0)
    def _():
        for ref in (vec_out, dwid_out, dnar_out, dfn_out):
            ref[...] = jnp.zeros_like(ref)

    unit = normal_rows(tok[...].astype(F32))
    normed = unit * gain[...] + shift[...]
    delta = shifted(normed) - normed
    hidden = hid[...]
    hb = hidden.astype(BF)
    lowv = low[...]
    colsum = lambda v: jnp.sum(v, axis=0, keepdims=True)
    dlow = mm_nt(draw[...].astype(BF), fwiden[...]) * (1.0 - lowv * lowv)
    dlow = dlow.astype(BF)
    total = jnp.zeros(normed.shape, F32)
    moved = jnp.zeros(normed.shape, F32)
    dhid = []
    for f, d_ref, w_ref in (
        (0, None, None),
        (1, dk, wk),
        (2, dv, wv),
        (3, dr, wr),
        (4, dg, wg),
    ):
        rows = slice(f * ranks, (f + 1) * ranks)
        mu = lerp[f + 1 : f + 2, :] + mm(hb[:, rows], widen[rows, :])
        if f == 0:
            dx = mm_nt(dlow, fnarrow[...])
            dfn_out[...] += mm_tn(dlow, (normed + delta * mu).astype(BF))
        else:
            dx = mm_nt(d_ref[...], w_ref[...])
        total = total + dx
        moved = moved + dx * mu
        doff = dx * delta
        vec_out[f + 1 : f + 2, :] += colsum(doff)
        db = doff.astype(BF)
        dwid_out[rows, :] += mm_tn(hb[:, rows], db)
        dhid.append(mm_nt(db, widen[rows, :]))
    dpre = (jnp.concatenate(dhid, axis=1) * (1.0 - hidden * hidden)).astype(BF)
    dblend = mm_nt(dpre, narrow[...])
    base = lerp[0:1, :]
    dnar_out[...] += mm_tn(dpre, (normed + delta * base).astype(BF))
    vec_out[0:1, :] += colsum(dblend * delta)
    total = total + dblend
    moved = moved + dblend * base
    dn = total - moved + shifted_back(moved)
    vec_out[6:7, :] += colsum(dn * unit)
    vec_out[7:8, :] += colsum(dn)
    dn_out[...] = dn.astype(BF)


def back(seq_len, tokens, hid, low, grads, draw, params, weights):
    g, d = tokens.shape
    c = draw.shape[1]
    gain, shift, lerp, narrow, widen, fnarrow, fwiden = params
    ranks = widen.shape[0] // 5
    fd = low.shape[1]
    per_seq = lambda w: pl.BlockSpec((seq_len, w), lambda s: (s, 0))
    kept = lambda r: pl.BlockSpec((r, d), lambda s: (0, 0))
    return pl.pallas_call(
        functools.partial(back_kernel, ranks),
        grid=(g // seq_len,),
        in_specs=[per_seq(d), per_seq(5 * ranks), per_seq(fd)]
        + [per_seq(c)] * 5
        + [whole_block(a) for a in params]
        + [whole_block(a) for a in weights],
        out_specs=[per_seq(d), kept(8), kept(5 * ranks), kept(5 * ranks), kept(fd)],
        out_shape=[
            jax.ShapeDtypeStruct((g, d), BF),
            jax.ShapeDtypeStruct((8, d), F32),
            jax.ShapeDtypeStruct((5 * ranks, d), F32),
            jax.ShapeDtypeStruct((5 * ranks, d), F32),
            jax.ShapeDtypeStruct((fd, d), F32),
        ],
        compiler_params=pltpu.CompilerParams(vmem_limit_bytes=56 * MIB),
        cost_estimate=pl.CostEstimate(
            flops=g * d * 2 * 18 * 256, bytes_accessed=g * d * 6, transcendentals=0
        ),
        name="token_shift_back",
    )(tokens, hid, low, *grads, draw, *params, *weights)


def level_tables(length):
    p = np.arange(length)[:, None]
    u = np.arange(length)[None, :]
    levels = int(length).bit_length() - 1
    spans = []
    for l in range(1, levels):
        b = 1 << l
        same = (p // b) == (u // b)
        upper = (p // b) % 2 == 1
        spans.append(same & np.where(upper, u < p, u > p))
    spans = np.concatenate(spans, 0).astype(np.float32)
    diff = p ^ u
    level = np.where(u < p, np.floor(np.log2(np.maximum(diff, 1))), -1)
    return levels, spans, level.astype(np.int32)


def per_head(lanes, width, count, v):
    out = jnp.sum(jnp.where(lanes == 0, v, 0.0), axis=1, keepdims=True)
    if count == 1:
        return jnp.broadcast_to(out, v.shape)
    for h in range(1, count):
        one = jnp.sum(jnp.where(lanes == h, v, 0.0), axis=1, keepdims=True)
        out = jnp.where(lanes == h, one, out)
    return out


def stack_heads(lanes, count, v):
    zero = jnp.zeros_like(v)
    return jnp.concatenate([jnp.where(lanes == h, v, zero) for h in range(count)], axis=0)


def side_by_side(length, count, v):
    return jnp.concatenate([v[h * length : (h + 1) * length] for h in range(count)], axis=1)


def mix_forward(levels, count, width, r, k, v, w, u, spans, level):
    length, lanes_n = r.shape
    lanes = lax.broadcasted_iota(jnp.int32, (length, lanes_n), 1) // width
    wh, wl = halves(w)
    gaps = mm(spans, wh) + mm(spans, wl)
    factors = [None] + [
        jnp.exp(gaps[l * length : (l + 1) * length]) for l in range(levels - 1)
    ]
    level2 = jnp.concatenate([level] * count, axis=0)
    scores = jnp.zeros((length * count, length), F32)
    parts = []
    for l in range(levels):
        e = factors[l]
        re = (r if e is None else r * e).astype(BF)
        ke = (k if e is None else k * e).astype(BF)
        parts.append((e, re, ke))
        scores = scores + jnp.where(
            level2 == l, mm_nt(stack_heads(lanes, count, re), ke), 0.0
        )
    vb = v.astype(BF)
    bonus = per_head(lanes, width, count, r * u * k)
    wkv = (
        mm(side_by_side(length, count, scores).astype(BF), stack_heads(lanes, count, vb))
        + bonus * v
    )
    center = wkv - per_head(lanes, width, count, wkv) * (1.0 / width)
    spread = per_head(lanes, width, count, center * center) * (1.0 / width)
    rstd = lax.rsqrt(spread + group_eps)
    return lanes, level2, parts, scores, bonus, vb, center * rstd, rstd


def wkv_kernel(levels, count, width, r, k, v, g, w, u, gain, bias, spans, level, out):
    unit = mix_forward(
        levels, count, width, r[...], k[...], v[...], w[...], u[...], spans[...], level[...]
    )[6]
    gate = g[...]
    out[...] = ((unit * gain[...] + bias[...]) * (gate * jax.nn.sigmoid(gate))).astype(BF)


def wkv_back_kernel(
    levels,
    count,
    width,
    r_ref,
    k_ref,
    v_ref,
    g_ref,
    w_ref,
    dm_ref,
    u_ref,
    gain_ref,
    bias_ref,
    spans,
    spans_t,
    level_ref,
    dr_out,
    dk_out,
    dv_out,
    dg_out,
    draw_out,
    vec_out,
):
    @pl.when(pl.program_id(1) == 0)
    def _():
        vec_out[...] = jnp.zeros_like(vec_out)

    r, k, v, w, u = r_ref[...], k_ref[...], v_ref[...], w_ref[...], u_ref[...]
    level = level_ref[...]
    lanes, level2, parts, scores, bonus, vb, unit, rstd = mix_forward(
        levels, count, width, r, k, v, w, u, spans[...], level
    )
    length = r.shape[0]
    heads = functools.partial(per_head, lanes, width, count)
    stack = functools.partial(stack_heads, lanes, count)
    beside = functools.partial(side_by_side, length, count)
    colsum = lambda x: jnp.sum(x, axis=0, keepdims=True)

    gate, dm, gain = g_ref[...], dm_ref[...], gain_ref[...]
    sig = jax.nn.sigmoid(gate)
    scaled = unit * gain + bias_ref[...]
    dg_out[...] = (dm * scaled * sig * (1.0 + gate * (1.0 - sig))).astype(BF)
    dscaled = dm * gate * sig
    dunit = dscaled * gain
    dwkv = rstd * (
        dunit - heads(dunit) * (1.0 / width) - unit * (heads(dunit * unit) * (1.0 / width))
    )
    db = dwkv.astype(BF)
    dbs = stack(db)
    dscores = mm_nt(dbs, vb)

    def turned(x):
        return jnp.concatenate(
            [jnp.transpose(x[h * length : (h + 1) * length]) for h in range(count)], axis=0
        )

    dscores_t = turned(dscores)
    level_t = jnp.transpose(level)
    level2_t = jnp.concatenate([level_t] * count, axis=0)
    dv = mm(beside(turned(scores)).astype(BF), dbs) + bonus * dwkv
    dbonus = heads(dwkv * v)
    dr = dbonus * u * k
    dk = dbonus * u * r
    flows = []
    for l in range(levels):
        e, re, ke = parts[l]
        dre = mm(beside(jnp.where(level2 == l, dscores, 0.0)).astype(BF), stack(ke))
        dke = mm(beside(jnp.where(level2_t == l, dscores_t, 0.0)).astype(BF), stack(re))
        if e is None:
            dr = dr + dre
            dk = dk + dke
        else:
            dre = dre * e
            dke = dke * e
            dr = dr + dre
            dk = dk + dke
            flows.append(dre * r + dke * k)
    fh, fl = halves(jnp.concatenate(flows, axis=0))
    dw = mm(spans_t[...], fh) + mm(spans_t[...], fl)
    draw = dw * w
    dr_out[...] = dr.astype(BF)
    dk_out[...] = dk.astype(BF)
    dv_out[...] = dv.astype(BF)
    draw_out[...] = draw
    vec_out[0:1, :] += colsum(dbonus * r * k)
    vec_out[1:2, :] += colsum(dscaled * unit)
    vec_out[2:3, :] += colsum(dscaled)
    vec_out[3:4, :] += colsum(draw)


def wkv(seq_len, r, k, v, g, w, u, gain, bias, dmixed=None):
    rows, c = r.shape
    heads_here = c * HEADS // D_OF(u, c)
    width = c // heads_here
    count = 2 if heads_here % 2 == 0 else 1
    lanes = count * width
    levels, spans, level = level_tables(seq_len)
    spans_a = jnp.asarray(spans, BF)
    level_a = jnp.asarray(level)
    cols = pl.BlockSpec((seq_len, lanes), lambda p, s: (s, p))
    vec = pl.BlockSpec((1, lanes), lambda p, s: (0, p))
    grid = (c // lanes, rows // seq_len)
    flops = rows * c * seq_len * 2 * 16
    params = pltpu.CompilerParams(vmem_limit_bytes=40 * MIB)
    if dmixed is None:
        return pl.pallas_call(
            functools.partial(wkv_kernel, levels, count, width),
            grid=grid,
            in_specs=[cols] * 5 + [vec] * 3 + [whole_block(spans_a), whole_block(level_a)],
            out_specs=cols,
            out_shape=jax.ShapeDtypeStruct((rows, c), BF),
            compiler_params=params,
            cost_estimate=pl.CostEstimate(
                flops=flops, bytes_accessed=rows * c * 22, transcendentals=rows * c * 7
            ),
            name="decay_mix",
        )(r, k, v, g, w, u, gain, bias, spans_a, level_a)
    spans_t = jnp.asarray(
        np.concatenate([s.T for s in spans.reshape(levels - 1, seq_len, seq_len)], 1), BF
    )
    return pl.pallas_call(
        functools.partial(wkv_back_kernel, levels, count, width),
        grid=grid,
        in_specs=[cols] * 6
        + [vec] * 3
        + [whole_block(spans_a), whole_block(spans_t), whole_block(level_a)],
        out_specs=[cols] * 5 + [pl.BlockSpec((4, lanes), lambda p, s: (0, p))],
        out_shape=[jax.ShapeDtypeStruct((rows, c), BF)] * 4
        + [jax.ShapeDtypeStruct((rows, c), F32), jax.ShapeDtypeStruct((4, c), F32)],
        compiler_params=params,
        cost_estimate=pl.CostEstimate(
            flops=flops * 4, bytes_accessed=rows * c * 36, transcendentals=rows * c * 7
        ),
        name="decay_mix_back",
    )(r, k, v, g, w, dmixed, u, gain, bias, spans_a, spans_t, level_a)


def D_OF(u, c):
    return c * lax.axis_size("fsdp")


def body(
    incoming_symbols,
    string_extents,
    adjoint_signal,
    first_scaling_factor,
    first_scaling_shift,
    lerp_factors,
    lerp_narrow_weights,
    lerp_widen_weights,
    fading_baseline,
    fading_narrow_weights,
    fading_widen_weights,
    present_reward,
    acceptor_weights,
    lookup_weights,
    content_weights,
    valve_weights,
    emission_weights,
    cluster_scaling_factor,
    cluster_scaling_shift,
    second_scaling_factor,
    second_scaling_shift_vec,
    feed_lerp_factors,
    feed_lookup_weights,
    feed_content_weights,
    feed_acceptor_weights,
):
    seqs, length, d = incoming_symbols.shape
    n = lax.axis_size("fsdp")
    me = lax.axis_index("fsdp")
    c = d // n
    home = seqs * length
    plane = home * n
    ranks = lerp_widen_weights.shape[1]
    fd = fading_narrow_weights.shape[1]

    tok_home = incoming_symbols.reshape(home, d)
    tokens = gather_rows(tok_home)
    weights = rows_to_cols(
        jnp.concatenate(
            [
                w.reshape(c, n, c)
                for w in (lookup_weights, content_weights, acceptor_weights, valve_weights)
            ],
            axis=2,
        ).reshape(c, 4 * d)
    )
    wk, wv, wr, wg = (weights[:, i * c : (i + 1) * c] for i in range(4))
    positions = lax.broadcasted_iota(jnp.int32, (seqs, length), 1)
    mask = (positions < string_extents[:, None]).astype(F32).reshape(home, 1)
    adj_low = adjoint_signal.reshape(home, d) * mask.astype(BF)
    d_out = adj_low.astype(F32)
    d_out_cols = rows_to_cols(adj_low).astype(F32)

    row = lambda v: v.reshape(1, -1)
    mine = lambda v: lax.dynamic_slice_in_dim(v, me * c, c, v.ndim - 1)
    gain1, shift1 = row(first_scaling_factor), row(first_scaling_shift)
    nh, nl = halves(lerp_narrow_weights)
    fh, fl = halves(fading_narrow_weights)
    widen_low = lerp_widen_weights.reshape(5 * ranks, d).astype(BF)
    xk, xv, xr, xg, hidden, low = front(
        length,
        tokens,
        gain1,
        shift1,
        lerp_factors,
        jnp.concatenate([nh, nl], axis=1),
        widen_low,
        jnp.concatenate([fh, fl], axis=1),
    )
    fwiden_mine = mine(fading_widen_weights)
    w = -jnp.exp(
        mine(row(fading_baseline))
        + jnp.dot(low, fwiden_mine, precision=lax.Precision.HIGHEST)
    )
    k, v, r, g = mm(xk, wk), mm(xv, wv), mm(xr, wr), mm(xg, wg)
    u, gn_gain, gn_bias = (
        mine(row(t)) for t in (present_reward, cluster_scaling_factor, cluster_scaling_shift)
    )
    mixed = wkv(length, r, k, v, g, w, u, gn_gain, gn_bias)
    branch = scatter_rows(mm(mixed, emission_weights).astype(BF))
    residual = tok_home.astype(F32) + branch.astype(F32)

    center = residual - jnp.mean(residual, axis=-1, keepdims=True)
    rstd2 = lax.rsqrt(jnp.mean(center * center, axis=-1, keepdims=True) + norm_eps)
    unit2 = center * rstd2
    normed2_home = unit2 * second_scaling_factor + second_scaling_shift_vec
    normed2 = gather_rows(normed2_home.astype(BF)).astype(F32)
    weights2 = rows_to_cols(
        jnp.concatenate(
            [feed_lookup_weights.reshape(c, n, -1), feed_acceptor_weights.reshape(c, n, -1)],
            axis=2,
        ).reshape(c, -1)
    )
    fc = feed_content_weights.shape[0]
    wl, wa = weights2[:, :fc], weights2[:, fc:]

    def before(t):
        t = t.reshape(-1, length, d)
        return jnp.concatenate([jnp.zeros_like(t[:, :1]), t[:, :-1]], axis=1).reshape(-1, d)

    def after(t):
        t = t.reshape(-1, length, d)
        return jnp.concatenate([t[:, 1:], jnp.zeros_like(t[:, :1])], axis=1).reshape(-1, d)

    delta2 = before(normed2) - normed2
    key_chan = (normed2 + delta2 * feed_lerp_factors[0]).astype(BF)
    recept_chan = (normed2 + delta2 * feed_lerp_factors[1]).astype(BF)
    key_act = mm(key_chan, wl)
    soft = jax.nn.softplus(key_act)
    squared = (soft * soft).astype(BF)
    value_act = scatter_cols(mm(squared, feed_content_weights).astype(BF)).astype(F32)
    gate = jax.nn.sigmoid(mm(recept_chan, wa))
    gated = gate * value_act
    layer_output = (residual + cols_to_rows(gated.astype(BF)).astype(F32)) * mask
    d_value = gather_cols((d_out_cols * gate).astype(BF))
    d_gate = (d_out_cols * gated * (1.0 - gate)).astype(BF)

    d_key = (mm_nt(d_value, feed_content_weights) * (2.0 * soft * jax.nn.sigmoid(key_act))).astype(BF)
    content_share = rep_scatter_rows(mm_tn(squared, d_value).astype(BF))
    d_key_chan = mm_nt(d_key, wl)
    d_recept_chan = mm_nt(d_gate, wa)
    moved = d_key_chan * feed_lerp_factors[0] + d_recept_chan * feed_lerp_factors[1]
    d_normed2 = d_key_chan + d_recept_chan - moved + after(moved)
    feed_lerp_part = jnp.stack(
        [jnp.sum(d_key_chan * delta2, axis=0), jnp.sum(d_recept_chan * delta2, axis=0)]
    )
    d_normed2 = scatter_rows(d_normed2.astype(BF)).astype(F32)
    lookup_share = rep_scatter_cols(mm_tn(key_chan, d_key).astype(BF))
    accept_share = rep_scatter_cols(mm_tn(recept_chan, d_gate).astype(BF))
    d_normed2, content_share = hold(d_normed2, content_share)

    def norm_back(unit, rstd, e):
        return rstd * (
            e
            - jnp.mean(e, axis=-1, keepdims=True)
            - unit * jnp.mean(e * unit, axis=-1, keepdims=True)
        )

    d_residual = d_out + norm_back(unit2, rstd2, d_normed2 * second_scaling_factor)
    norm2_part = jnp.stack([jnp.sum(d_normed2 * unit2, axis=0), jnp.sum(d_normed2, axis=0)])

    d_branch = gather_rows(d_residual.astype(BF))
    d_mixed = mm_nt(d_branch, emission_weights)
    emission_share = rep_scatter_rows(mm_tn(mixed, d_branch).astype(BF))
    d_mixed, lookup_share = hold(d_mixed, lookup_share)
    d_r, d_k, d_v, d_g, d_raw, mix_vec = wkv(
        length, r, k, v, g, w, u, gn_gain, gn_bias, d_mixed
    )
    d_r, accept_share, emission_share = hold(d_r, accept_share, emission_share)
    share_one = rep_scatter_cols(
        jnp.concatenate([mm_tn(xk, d_k), mm_tn(xv, d_v)], axis=1).astype(BF)
    )
    share_two = rep_scatter_cols(
        jnp.concatenate([mm_tn(xr, d_r), mm_tn(xg, d_g)], axis=1).astype(BF)
    )

    def settle(share, parts):
        total = rep_gather(cols_to_rows(share)).reshape(c, n, parts, -1)
        return [total[:, :, i].reshape(c, -1) for i in range(parts)]

    feed_content_grads = rep_gather(content_share)
    emission_weights_grads = rep_gather(emission_share)
    (feed_lookup_grads,) = settle(lookup_share, 1)
    (feed_acceptor_grads,) = settle(accept_share, 1)
    lookup_weights_grads, content_weights_grads = settle(share_one, 2)
    acceptor_weights_grads, valve_weights_grads = settle(share_two, 2)
    d_normed, vec_part, widen_part, narrow_part, fnarrow_part = back(
        length,
        tokens,
        hidden,
        low,
        (d_k, d_v, d_r, d_g),
        d_raw,
        (gain1, shift1, lerp_factors, nh, widen_low, fh, fwiden_mine.astype(BF)),
        (wk, wv, wr, wg),
    )
    d_normed = scatter_rows(d_normed).astype(F32)
    tok_f = tok_home.astype(F32)
    center1 = tok_f - jnp.mean(tok_f, axis=-1, keepdims=True)
    rstd1 = lax.rsqrt(jnp.mean(center1 * center1, axis=-1, keepdims=True) + norm_eps)
    token_grad = d_residual + norm_back(center1 * rstd1, rstd1, d_normed * first_scaling_factor)

    small = scatter_cols(
        jnp.concatenate(
            [vec_part, widen_part, narrow_part, fnarrow_part, norm2_part, feed_lerp_part], axis=0
        )
    )
    fwiden_part = lax.dot_general(
        low, d_raw, (((0,), (0,)), ((), ())), precision=lax.Precision.HIGHEST
    )
    small = lax.psum(jnp.concatenate([small, fwiden_part, mix_vec], axis=0), "rep")
    small = gather_cols(small)
    cuts = np.cumsum([8, 5 * ranks, 5 * ranks, fd, 2, 2, fd, 4])
    vec, widen_g, narrow_g, fnarrow_g, norm2_g, feed_lerp_g, fwiden_g, mix_g = (
        small[a:b] for a, b in zip([0, *cuts[:-1]], cuts)
    )
    return (
        layer_output.reshape(seqs, length, d),
        token_grad.reshape(seqs, length, d),
        vec[6],
        vec[7],
        vec[:6],
        narrow_g.T,
        widen_g.reshape(5, ranks, d),
        mix_g[3],
        fnarrow_g.T,
        fwiden_g,
        mix_g[0],
        acceptor_weights_grads,
        lookup_weights_grads,
        content_weights_grads,
        valve_weights_grads,
        emission_weights_grads,
        mix_g[1],
        mix_g[2],
        norm2_g[0],
        norm2_g[1],
        feed_lerp_g,
        feed_lookup_grads,
        feed_content_grads,
        feed_acceptor_grads,
    )


def solution(mesh):
    seq = P(("fsdp", "rep"), None, None)
    row = P("fsdp", None)
    in_specs = (
        (seq, P(("fsdp", "rep")), seq) + (P(),) * 9 + (row,) * 5 + (P(),) * 5 + (row,) * 3
    )
    out_specs = (seq, seq) + (P(),) * 9 + (row,) * 5 + (P(),) * 5 + (row,) * 3
    return jax.shard_map(body, mesh=mesh, in_specs=in_specs, out_specs=out_specs, check_vma=False)
```

time: 2580 us -> 1310 us (0.51)
  waiting for transfers between devices: 1760 us -> 642 us
  other arithmetic: 325 us -> 77 us
  matrix products: 315 us -> 110 us
  starting transfers between devices: 1.15 us -> 122 us
  Pallas kernels: 0 us -> 115 us
  local copies, waits for them, and re-layouts: 152 us -> 207 us
    psum x3 -> x1, waiting for transfers between devices: 662 us -> 0.02 us  [body(): lax.psum(jnp.concatenate([small, fwiden_part, mix_vec], axis=0), 'rep')]
    reduce_scatter x8 -> x11, waiting for transfers between devices: 735 us -> 258 us  [the longest x2 86.7 us: rep_scatter_rows(): return lax.psum_scatter(v, 'rep', scatter_dimension=0, tiled=True)]
    ppermute x0 -> x92, waiting for transfers between devices: none -> 322 us  [the longest x18 193 us: rep_gather(): lax.ppermute(down[-1], 'rep', [(i + 1, i) for i in range(n - s)])]
    all_gather x8 -> x5, waiting for transfers between devices: 356 us -> 60.2 us  [the longest x2 37.3 us: gather_cols(): return lax.all_gather(v, 'fsdp', axis=1, tiled=True)]
    dot_general x72 -> x22, matrix products: 315 us -> 110 us  [the longest x8 37 us: mm(): return jnp.dot(a, b, preferred_element_type=F32)]
    dot_general x12 -> x0, other arithmetic: 123 us -> none  [block_step(): jnp.einsum('hti,hsi,htsi->hts', acceptor_slice, lookup_slice, weight, pre...]
    ppermute x0 -> x92, starting transfers between devices: none -> 120 us  [the longest x56 48.7 us: exchange(): got = lax.ppermute(take(me ^ m), 'fsdp', [(i, i ^ m) for i in range(n)])]
    pallas_call x0 -> x4, Pallas kernels: none -> 115 us  [the longest x1 48.6 us: back(): pl.pallas_call(functools.partial(back_kernel, ranks), grid=(g // seq_len,...]
  transfers between devices with their start and end apart: 19 -> 109, of which waited for: 15 -> 43; matrix products, arithmetic and copies ran while one was open for 16% -> 19% of each run, Pallas kernels for 0% -> 2%
where the time goes in v1:
time: 1310 us; the launch traced here: 1290 us
  waiting for transfers between devices  642 us (49%)
  local copies, waits for them, and re-layouts  207 us (16%)
  starting transfers between devices  122 us (9%)
  Pallas kernels  115 us (9%)
  matrix products  110 us (8%)
  other arithmetic  77 us (6%)
  between operations  16.8 us (1%)
    ppermute x18, waiting for transfers between devices, rep_gather(): lax.ppermute(down[-1], 'rep', [(i + 1, i) for i in range(n - s)])  193 us
    ppermute x56, waiting for transfers between devices, exchange(): got = lax.ppermute(take(me ^ m), 'fsdp', [(i, i ^ m) for i in range(n)])  129 us
    reduce_scatter x2, waiting for transfers between devices, rep_scatter_rows(): return lax.psum_scatter(v, 'rep', scatter_dimension=0, tiled=True)  86.7 us
    reduce_scatter x3, waiting for transfers between devices, scatter_rows(): return lax.psum_scatter(v, 'fsdp', scatter_dimension=0, tiled=True)  79.4 us
    reduce_scatter x4, waiting for transfers between devices, rep_scatter_cols(): return lax.psum_scatter(v, 'rep', scatter_dimension=0, tiled=True)  58.1 us
    ppermute x56, starting transfers between devices, exchange(): got = lax.ppermute(take(me ^ m), 'fsdp', [(i, i ^ m) for i in range(n)])  48.7 us
    pallas_call x1, Pallas kernels, back(): pl.pallas_call(functools.partial(back_kernel, ranks), grid=(g // seq_len,...  48.6 us
    unnamed x168, local copies, waits for them, and re-layouts  48.2 us
  transfers between devices with their start and end apart: 109, of which 43 were waited for; matrix products, arithmetic and copies ran while one was open for 19% of the time, Pallas kernels for 2%

profile of v1, /device:TPU:0, one launch (start us, length us, event | category | flops | bytes accessed | tf_op | source)
XLA Modules:
  0.0 1289.9 jit_solution(8953349017560874640)
XLA Ops:
  50.9 11.7 collective-permute-done.2
  66.4 19.9 %collective-permute-done.4 = bf16[256,1024]{1,0:T(8,128)(2,1)} collective-permute-done((bf16[256,1024]{1,0:T(8,128)(2,1)}, bf16[256,1024]{1,0:T(8,128)(2,1)}, u32[]{:S(2)}, u32[]{:S(2)}) %collective-permute-start.4) | collective-permute-done | bytes 524320 | tf_op jit(solution)/shard_map/ppermute | solution.py:57
  92.0 21.7 %token_shift.1 = (bf16[1024,2048]{1,0:T(8,128)(2,1)}, bf16[1024,2048]{1,0:T(8,128)(2,1)}, bf16[1024,2048]{1,0:T(8,128)(2,1)}, bf16[1024,2048]{1,0:T(8,128)(2,1)}...) custom-call(bf16[1024,2048]{1,0:T(8,128)(2,1)} %bitcast.317, f32[1,2048]{1,0:T(1,128)S(1)} %bitcast.251, ...), custom_call_target="tpu_custom_call" | custom-call | flops 5368709120 | bytes 20971520 | tf_op jit(solution)/shard_map/token_shift/pallas_call | solution.py:164
  128.9 15.1 %decay_mix.1 = bf16[1024,256]{1,0:T(8,128)(2,1)S(1)} custom-call(f32[1024,256]{1,0:T(8,128)S(1)} %fusion.40.r.r_ref, f32[1024,256]{1,0:T(8,128)S(1)} %fusion.38.k.k_ref, f32[1024,256]{1,0:T(8,128)S(1)} %fusion.36.v.v_ref, f32[1024,256]{1,0:T(8,128)S(1)} %fusion.34.g.g_ref, f32[1024,256]{1,0:T(8,128)S(1)} %fusion.7.w.w_ref, f32[1,256]{1,0:T(1,128)S(1)} %bitcast.252, ...), custom_call_target="tpu_custom_call" | custom-call | flops 1073741824 | bytes 5767168 | tf_op jit(solution)/shard_map/decay_mix/pallas_call | solution.py:471
  147.5 53.1 %reduce-scatter.12.cloned.1.call-done = bf16[128,2048]{1,0:T(8,128)(2,1)} async-done(((bf16[1024,2048]{1,0:T(8,128)(2,1)}), bf16[128,2048]{1,0:T(8,128)(2,1)}) %reduce-scatter.12.cloned.1.call-update) | async-done | bytes 524304 | tf_op jit(solution)/shard_map/reduce_scatter | solution.py:45
  223.7 14.8 %collective-permute-done.8 = bf16[256,1152]{1,0:T(8,128)(2,1)S(1)} collective-permute-done((bf16[256,1152]{1,0:T(8,128)(2,1)S(1)}, bf16[256,1152]{1,0:T(8,128)(2,1)S(1)}, u32[]{:S(2)}, u32[]{:S(2)}) %collective-permute-start.8) | collective-permute-done | bytes 589856 | tf_op jit(solution)/shard_map/ppermute | solution.py:57
  240.0 17.7 %collective-permute-done.9 = bf16[256,1152]{1,0:T(8,128)(2,1)S(1)} collective-permute-done((bf16[256,1152]{1,0:T(8,128)(2,1)S(1)}, bf16[256,1152]{1,0:T(8,128)(2,1)S(1)}, u32[]{:S(2)}, u32[]{:S(2)}) %collective-permute-start.9) | collective-permute-done | bytes 589856 | tf_op jit(solution)/shard_map/ppermute | solution.py:57
  259.4 23.8 %collective-permute-done.11 = bf16[256,1152]{1,0:T(8,128)(2,1)S(1)} collective-permute-done((bf16[256,1152]{1,0:T(8,128)(2,1)S(1)}, bf16[256,1152]{1,0:T(8,128)(2,1)S(1)}, u32[]{:S(2)}, u32[]{:S(2)}) %collective-permute-start.11) | collective-permute-done | bytes 589856 | tf_op jit(solution)/shard_map/ppermute | solution.py:57
  337.0 34.0 %reduce-scatter.14.cloned.1.call-done = bf16[1024,256]{1,0:T(8,128)(2,1)} async-done(((bf16[1024,2048]{1,0:T(8,128)(2,1)}), bf16[1024,256]{1,0:T(8,128)(2,1)}) %reduce-scatter.14.cloned.1.call-update) | async-done | bytes 524304 | tf_op jit(solution)/shard_map/reduce_scatter | solution.py:49
  376.8 37.3 %all-gather.9.cloned.1.call-done = bf16[1024,2048]{1,0:T(8,128)(2,1)} async-done(((bf16[1024,256]{1,0:T(8,128)(2,1)}), bf16[1024,2048]{1,0:T(8,128)(2,1)}) %all-gather.9.cloned.1.call-update) | async-done | bytes 4194320 | tf_op jit(solution)/shard_map/all_gather | solution.py:41
  414.1 10.9 multiply_convert_fusion
  425.0 9.8 fusion.1
  434.9 11.0 multiply_reduce_fusion
  451.5 9.2 fusion
  460.8 10.8 convolution_convert_fusion.3
  486.7 26.3 %reduce-scatter.16.cloned.1.call-done = bf16[128,2048]{1,0:T(8,128)(2,1)} async-done(((bf16[1024,2048]{1,0:T(8,128)(2,1)}), bf16[128,2048]{1,0:T(8,128)(2,1)}) %reduce-scatter.16.cloned.1.call-update) | async-done | bytes 524304 | tf_op jit(solution)/shard_map/reduce_scatter | solution.py:45
  515.1 68.7 %reduce-scatter.18.cloned.1.call-done = bf16[224,2048]{1,0:T(8,128)(2,1)} async-done(((bf16[896,2048]{1,0:T(8,128)(2,1)}), bf16[224,2048]{1,0:T(8,128)(2,1)}) %reduce-scatter.18.cloned.1.call-update) | async-done | bytes 917520 | tf_op jit(solution)/shard_map/reduce_scatter | solution.py:91
  604.1 22.9 %all-gather.11.cloned.1.call-done = bf16[1024,2048]{1,0:T(8,128)(2,1)} async-done(((bf16[128,2048]{1,0:T(8,128)(2,1)}), bf16[1024,2048]{1,0:T(8,128)(2,1)}) %all-gather.11.cloned.1.call-update) | async-done | bytes 4194320 | tf_op jit(solution)/shard_map/all_gather | solution.py:37
  640.4 58.1 %reduce-scatter.20.cloned.1.call-done = bf16[512,896]{1,0:T(8,128)(2,1)} async-done(((bf16[2048,896]{1,0:T(8,128)(2,1)}), bf16[512,896]{1,0:T(8,128)(2,1)}) %reduce-scatter.20.cloned.1.call-update) | async-done | bytes 917520 | tf_op jit(solution)/shard_map/reduce_scatter | solution.py:98
  704.2 29.9 %decay_mix_back.1 = (bf16[1024,256]{1,0:T(8,128)(2,1)S(1)}, bf16[1024,256]{1,0:T(8,128)(2,1)S(1)}, bf16[1024,256]{1,0:T(8,128)(2,1)S(1)}, bf16[1024,256]{1,0:T(8...) custom-call(f32[1024,256]{1,0:T(8,128)S(1)} %copy-done.12, f32[1024,256]{1,0:T(8,128)S(1)} %copy-done.10, ...), custom_call_target="tpu_custom_call" | custom-call | flops 4294967296 | bytes 9437184 | tf_op jit(solution)/shard_map/decay_mix_back/pallas_call | solution.py:486
  738.3 18.0 %reduce-scatter.24.cloned.1.call-done = bf16[64,2048]{1,0:T(8,128)(2,1)} async-done(((bf16[256,2048]{1,0:T(8,128)(2,1)}), bf16[64,2048]{1,0:T(8,128)(2,1)}) %reduce-scatter.24.cloned.1.call-update) | async-done | bytes 262160 | tf_op jit(solution)/shard_map/reduce_scatter | solution.py:91
  756.3 48.6 %token_shift_back.1 = (bf16[1024,2048]{1,0:T(8,128)(2,1)}, f32[8,2048]{1,0:T(8,128)}, f32[160,2048]{1,0:T(8,128)}, f32[160,2048]{1,0:T(8,128)}, f32[64,2048]{1,0:T(8,128)}) custom-call(bf16[1024,2048]{1,0:T(8,128)(2,1)} %bitcast.318, f32[1024,160]{1,0:T(8,128)} %copy-done.31, f32[1024,64]{1,0:T(8,128)} %copy-done.1, bf16[1024,256]{1,0:T(8,128)(2,1)} %copy-done.29, ...), custom_call_target="tpu_custom_call" | custom-call | flops 19327352832 | bytes 12582912 | tf_op jit(solution)/shard_map/token_shift_back/pallas_call | solution.py:269
  805.0 11.8 concatenate.48
  830.9 17.1 %collective-permute-done.74 = bf16[224,2048]{1,0:T(8,128)(2,1)} collective-permute-done((bf16[224,2048]{1,0:T(8,128)(2,1)S(1)}, bf16[224,2048]{1,0:T(8,128)(2,1)}, u32[]{:S(2)}, u32[]{:S(2)}) %collective-permute-start.74) | collective-permute-done | bytes 917536 | tf_op jit(solution)/shard_map/ppermute | solution.py:107
  857.8 13.3 %collective-permute-done.75 = bf16[224,2048]{1,0:T(8,128)(2,1)} collective-permute-done((bf16[224,2048]{1,0:T(8,128)(2,1)}, bf16[224,2048]{1,0:T(8,128)(2,1)}, u32[]{:S(2)}, u32[]{:S(2)}) %collective-permute-start.75) | collective-permute-done | bytes 917536 | tf_op jit(solution)/shard_map/ppermute | solution.py:107
  874.8 52.2 %collective-permute-done.76 = bf16[224,2048]{1,0:T(8,128)(2,1)} collective-permute-done((bf16[224,2048]{1,0:T(8,128)(2,1)}, bf16[224,2048]{1,0:T(8,128)(2,1)}, u32[]{:S(2)}, u32[]{:S(2)}) %collective-permute-start.76) | collective-permute-done | bytes 917536 | tf_op jit(solution)/shard_map/ppermute | solution.py:107
  956.1 30.8 %collective-permute-done.68 = bf16[64,7168]{1,0:T(8,128)(2,1)} collective-permute-done((bf16[64,7168]{1,0:T(8,128)(2,1)S(1)}, bf16[64,7168]{1,0:T(8,128)(2,1)}, u32[]{:S(2)}, u32[]{:S(2)}) %collective-permute-start.68) | collective-permute-done | bytes 917536 | tf_op jit(solution)/shard_map/ppermute | solution.py:107
  997.1 24.4 %collective-permute-done.69 = bf16[64,7168]{1,0:T(8,128)(2,1)} collective-permute-done((bf16[64,7168]{1,0:T(8,128)(2,1)}, bf16[64,7168]{1,0:T(8,128)(2,1)}, u32[]{:S(2)}, u32[]{:S(2)}) %collective-permute-start.69) | collective-permute-done | bytes 917536 | tf_op jit(solution)/shard_map/ppermute | solution.py:107
  1133.0 21.9 %collective-permute-done.50 = bf16[64,4096]{1,0:T(8,128)(2,1)S(1)} collective-permute-done((bf16[64,4096]{1,0:T(8,128)(2,1)S(1)}, bf16[64,4096]{1,0:T(8,128)(2,1)S(1)}, u32[]{:S(2)}, u32[]{:S(2)}) %collective-permute-start.50) | collective-permute-done | bytes 524320 | tf_op jit(solution)/shard_map/ppermute | solution.py:107
  1204.9 14.3 %slice_reduce_fusion.1 = (f32[256,8,256]{2,1,0:T(8,128)S(1)}, f32[256,8,256]{2,1,0:T(8,128)S(1)}) fusion(f32[256,8,2,256]{3,2,1,0:T(2,128)} %reshape_reshape.7), kind=kLoop, calls=%fused_computation.28 | loop fusion | bytes 8388608 | tf_op jit(solution)/shard_map/slice | solution.py:666
  1231.1 9.0 collective-permute-done.38
  1250.1 14.3 %slice_reduce_fusion = (f32[256,8,256]{2,1,0:T(8,128)S(1)}, f32[256,8,256]{2,1,0:T(8,128)S(1)}) fusion(f32[256,8,2,256]{3,2,1,0:T(2,128)} %reshape_reshape.6), kind=kLoop, calls=%fused_computation.27 | loop fusion | bytes 8388608 | tf_op jit(solution)/shard_map/slice | solution.py:666
  (559 shorter events, 490.6 us)
Async XLA Ops:
  7.2 82.6 %all-gather.15.cloned.1.call-start = ((), (), s32[]{:S(2)}) async-start(), calls=%async_computation.27 | async-start | bytes 4718592 | tf_op jit(solution)/shard_map/all_gather | solution.py:37
  8.0 192.6 %reduce-scatter.12.cloned.1.call-start = ((), (), s32[]{:S(2)}) async-start(), calls=%async_computation.11 | async-start | bytes 4718592 | tf_op jit(solution)/shard_map/reduce_scatter | solution.py:45
  29.4 56.9 %collective-permute-start.4 = (bf16[256,1024]{1,0:T(8,128)(2,1)}, bf16[256,1024]{1,0:T(8,128)(2,1)}, u32[]{:S(2)}, u32[]{:S(2)}) collective-permute-start(bf16[256,1024]{1,0:T(8,128)(2,1)} %get-tuple-element.104), channel_id=1, source_target_pairs={{0,20},{4,16},{8,28},{12,24},{16,4},{20,0},{24,12},{28,8},{1,21},{... | collective-permute-start | bytes 1572872 | tf_op jit(solution)/shard_map/ppermute | solution.py:57
  44.5 43.7 %collective-permute-start.5 = (bf16[256,1024]{1,0:T(8,128)(2,1)}, bf16[256,1024]{1,0:T(8,128)(2,1)S(1)}, u32[]{:S(2)}, u32[]{:S(2)}) collective-permute-start(bf16[256,1024]{1,0:T(8,128)(2,1)} %get-tuple-element.103), channel_id=1, source_target_pairs={{0,24},{4,28},{8,16},{12,20},{16,8},{20,12},{24,0},{28,4},{1,25},{... | collective-permute-start | bytes 1572872 | tf_op jit(solution)/shard_map/ppermute | solution.py:57
  147.4 138.4 %all-gather.7.cloned.1.call-start = ((), (), s32[]{:S(2)}) async-start(), calls=%async_computation.12 | async-start | bytes 4718592 | tf_op jit(solution)/shard_map/all_gather | solution.py:37
  205.4 165.7 %reduce-scatter.14.cloned.1.call-start = ((), (), s32[]{:S(2)}) async-start(), calls=%async_computation.13 | async-start | bytes 4718592 | tf_op jit(solution)/shard_map/reduce_scatter | solution.py:49
  221.0 62.2 %collective-permute-start.11 = (bf16[256,1152]{1,0:T(8,128)(2,1)S(1)}, bf16[256,1152]{1,0:T(8,128)(2,1)S(1)}, u32[]{:S(2)}, u32[]{:S(2)}) collective-permute-start(bf16[256,1152]{1,0:T(8,128)(2,1)S(1)} %get-tuple-element.92), channel_id=1, source_target_pairs={{0,20},{4,16},{8,28},{12,24},{16,4},{20,0},{24,12},{28,8},{1,21},{... | collective-permute-start | bytes 1769480 | tf_op jit(solution)/shard_map/ppermute | solution.py:57
  221.3 62.8 %collective-permute-start.12 = (bf16[256,1152]{1,0:T(8,128)(2,1)S(1)}, bf16[256,1152]{1,0:T(8,128)(2,1)S(1)}, u32[]{:S(2)}, u32[]{:S(2)}) collective-permute-start(bf16[256,1152]{1,0:T(8,128)(2,1)S(1)} %get-tuple-element.91), channel_id=1, source_target_pairs={{0,24},{4,28},{8,16},{12,20},{16,8},{20,12},{24,0},{28,4},{1,25},{... | collective-permute-start | bytes 1769480 | tf_op jit(solution)/shard_map/ppermute | solution.py:57
  238.5 46.5 %collective-permute-start.13 = (bf16[256,1152]{1,0:T(8,128)(2,1)S(1)}, bf16[256,1152]{1,0:T(8,128)(2,1)S(1)}, u32[]{:S(2)}, u32[]{:S(2)}) collective-permute-start(bf16[256,1152]{1,0:T(8,128)(2,1)S(1)} %get-tuple-element.90), channel_id=1, source_target_pairs={{0,28},{4,24},{8,20},{12,16},{16,12},{20,8},{24,4},{28,0},{1,29},{... | collective-permute-start | bytes 1769480 | tf_op jit(solution)/shard_map/ppermute | solution.py:57
  318.9 95.2 %all-gather.9.cloned.1.call-start = ((), (), s32[]{:S(2)}) async-start(), calls=%async_computation.14 | async-start | bytes 4718592 | tf_op jit(solution)/shard_map/all_gather | solution.py:41
  376.5 136.4 %reduce-scatter.16.cloned.1.call-start = ((), (), s32[]{:S(2)}) async-start(), calls=%async_computation.15 | async-start | bytes 4718592 | tf_op jit(solution)/shard_map/reduce_scatter | solution.py:45
  460.7 123.1 %reduce-scatter.18.cloned.1.call-start = ((), (), s32[]{:S(2)}) async-start(), calls=%async_computation.16 | async-start | bytes 4587520 | tf_op jit(solution)/shard_map/reduce_scatter | solution.py:91
  471.6 155.4 %all-gather.11.cloned.1.call-start = ((), (), s32[]{:S(2)}) async-start(), calls=%async_computation.17 | async-start | bytes 4718592 | tf_op jit(solution)/shard_map/all_gather | solution.py:37
  589.8 108.7 %reduce-scatter.20.cloned.1.call-start = ((), (), s32[]{:S(2)}) async-start(), calls=%async_computation.18 | async-start | bytes 4587520 | tf_op jit(solution)/shard_map/reduce_scatter | solution.py:98
  599.4 139.0 %reduce-scatter.22.cloned.1.call-start = ((), (), s32[]{:S(2)}) async-start(), calls=%async_computation.19 | async-start | bytes 1310720 | tf_op jit(solution)/shard_map/reduce_scatter | solution.py:98
  604.1 152.3 %reduce-scatter.24.cloned.1.call-start = ((), (), s32[]{:S(2)}) async-start(), calls=%async_computation.20 | async-start | bytes 1310720 | tf_op jit(solution)/shard_map/reduce_scatter | solution.py:91
  631.5 358.5 %reduce-scatter.28.cloned.1.call-start = ((), (), s32[]{:S(2)}) async-start(), calls=%async_computation.22 | async-start | bytes 3686400 | tf_op jit(solution)/shard_map/reduce_scatter | solution.py:49
  816.8 273.9 %reduce-scatter.32.cloned.1.call-start = ((), (), s32[]{:S(2)}) async-start(), calls=%async_computation.26 | async-start | bytes 2621440 | tf_op jit(solution)/shard_map/reduce_scatter | solution.py:98
  823.7 347.0 %reduce-scatter.30.cloned.1.call-start = ((), (), s32[]{:S(2)}) async-start(), calls=%async_computation.25 | async-start | bytes 2621440 | tf_op jit(solution)/shard_map/reduce_scatter | solution.py:98
  856.1 332.8 %all-reduce.4.cloned.1.call-start = ((), (), s32[]{:S(2)}) async-start(), calls=%async_computation.23 | async-start | bytes 950272 | tf_op jit(solution)/shard_map/psum | solution.py:698
  871.2 55.8 %collective-permute-start.76 = (bf16[224,2048]{1,0:T(8,128)(2,1)}, bf16[224,2048]{1,0:T(8,128)(2,1)}, u32[]{:S(2)}, u32[]{:S(2)}) collective-permute-start(bf16[224,2048]{1,0:T(8,128)(2,1)} %collective-permute-done.75), channel_id=1, source_target_pairs={{1,0},{5,4},{9,8},{13,12},{17,16},{21,20},{25,24},{29,28}} | collective-permute-start | bytes 2752520 | tf_op jit(solution)/shard_map/ppermute | solution.py:107
  873.8 77.7 %collective-permute-start.78 = (bf16[224,2048]{1,0:T(8,128)(2,1)}, bf16[224,2048]{1,0:T(8,128)(2,1)S(1)}, u32[]{:S(2)}, u32[]{:S(2)}) collective-permute-start(bf16[224,2048]{1,0:T(8,128)(2,1)} %collective-permute-done.77), channel_id=1, source_target_pairs={{2,3},{6,7},{10,11},{14,15},{18,19},{22,23},{26,27},{30,31}} | collective-permute-start | bytes 2752520 | tf_op jit(solution)/shard_map/ppermute | solution.py:106
  874.7 56.8 %collective-permute-start.60 = (bf16[64,896]{1,0:T(8,128)(2,1)S(1)}, bf16[64,896]{1,0:T(8,128)(2,1)S(1)}, u32[]{:S(2)}, u32[]{:S(2)}) collective-permute-start(bf16[64,896]{1,0:T(8,128)(2,1)S(1)} %get-tuple-element.132), channel_id=1, source_target_pairs={{0,4},{4,0},{8,12},{12,8},{16,20},{20,16},{24,28},{28,24},{1,5},{5... | collective-permute-start | bytes 344072 | tf_op jit(solution)/shard_map/ppermute | solution.py:57
  943.0 43.9 %collective-permute-start.68 = (bf16[64,7168]{1,0:T(8,128)(2,1)S(1)}, bf16[64,7168]{1,0:T(8,128)(2,1)}, u32[]{:S(2)}, u32[]{:S(2)}) collective-permute-start(bf16[64,7168]{1,0:T(8,128)(2,1)S(1)} %constant_dynamic-update-slice_fusion.6), channel_id=1, source_target_pairs={{1,0},{2,1},{3,2},{5,4},{6,5},{7,6},{9,8},{10,9},{11,10},{13,12},{... | collective-permute-start | bytes 2752520 | tf_op jit(solution)/shard_map/ppermute | solution.py:107
  944.4 43.8 %collective-permute-start.67 = (bf16[64,7168]{1,0:T(8,128)(2,1)S(1)}, bf16[64,7168]{1,0:T(8,128)(2,1)}, u32[]{:S(2)}, u32[]{:S(2)}) collective-permute-start(bf16[64,7168]{1,0:T(8,128)(2,1)S(1)} %constant_dynamic-update-slice_fusion.6), channel_id=1, source_target_pairs={{0,1},{1,2},{2,3},{4,5},{5,6},{6,7},{8,9},{9,10},{10,11},{12,13},{... | collective-permute-start | bytes 2752520 | tf_op jit(solution)/shard_map/ppermute | solution.py:106
  988.2 67.9 %collective-permute-start.71 = (bf16[64,7168]{1,0:T(8,128)(2,1)}, bf16[64,7168]{1,0:T(8,128)(2,1)}, u32[]{:S(2)}, u32[]{:S(2)}) collective-permute-start(bf16[64,7168]{1,0:T(8,128)(2,1)} %collective-permute-done.67), channel_id=1, source_target_pairs={{1,2},{2,3},{5,6},{6,7},{9,10},{10,11},{13,14},{14,15},{17,18},{18... | collective-permute-start | bytes 2752520 | tf_op jit(solution)/shard_map/ppermute | solution.py:106
  989.8 41.1 %collective-permute-start.79 = (bf16[64,256]{1,0:T(8,128)(2,1)S(1)}, bf16[64,256]{1,0:T(8,128)(2,1)S(1)}, u32[]{:S(2)}, u32[]{:S(2)}) collective-permute-start(bf16[64,256]{1,0:T(8,128)(2,1)S(1)} %get-tuple-element.172), channel_id=1, source_target_pairs={{0,4},{4,0},{8,12},{12,8},{16,20},{20,16},{24,28},{28,24},{1,5},{5... | collective-permute-start | bytes 98312 | tf_op jit(solution)/shard_map/ppermute | solution.py:57
  991.8 277.0 %reduce-scatter.26.cloned.1.call-start = ((), (), s32[]{:S(2)}) async-start(), calls=%async_computation.21 | async-start | bytes 4718592 | tf_op jit(solution)/shard_map/reduce_scatter | solution.py:45
  1021.5 58.5 %collective-permute-start.70 = (bf16[64,7168]{1,0:T(8,128)(2,1)}, bf16[64,7168]{1,0:T(8,128)(2,1)}, u32[]{:S(2)}, u32[]{:S(2)}) collective-permute-start(bf16[64,7168]{1,0:T(8,128)(2,1)} %collective-permute-done.69), channel_id=1, source_target_pairs={{1,0},{5,4},{9,8},{13,12},{17,16},{21,20},{25,24},{29,28}} | collective-permute-start | bytes 2752520 | tf_op jit(solution)/shard_map/ppermute | solution.py:107
  1022.8 40.2 %collective-permute-start.55 = (bf16[64,2048]{1,0:T(8,128)(2,1)S(1)}, bf16[64,2048]{1,0:T(8,128)(2,1)}, u32[]{:S(2)}, u32[]{:S(2)}) collective-permute-start(bf16[64,2048]{1,0:T(8,128)(2,1)S(1)} %copy-done.64), channel_id=1, source_target_pairs={{1,0},{2,1},{3,2},{5,4},{6,5},{7,6},{9,8},{10,9},{11,10},{13,12},{... | collective-permute-start | bytes 786440 | tf_op jit(solution)/shard_map/ppermute | solution.py:107
  1030.9 241.8 %all-gather.13.cloned.1.call-start = ((), (), s32[]{:S(2)}) async-start(), calls=%async_computation.24 | async-start | bytes 4276224 | tf_op jit(solution)/shard_map/all_gather | solution.py:41
  1080.0 50.8 %collective-permute-start.91 = (bf16[64,2048]{1,0:T(8,128)(2,1)}, bf16[64,2048]{1,0:T(8,128)(2,1)}, u32[]{:S(2)}, u32[]{:S(2)}) collective-permute-start(bf16[64,2048]{1,0:T(8,128)(2,1)} %collective-permute-done.90), channel_id=1, source_target_pairs={{2,3},{6,7},{10,11},{14,15},{18,19},{22,23},{26,27},{30,31}} | collective-permute-start | bytes 786440 | tf_op jit(solution)/shard_map/ppermute | solution.py:106
  (154 other events, 2161.9 us)
Sparse Core Ops, SparseCore 0:
  10.0 50.7 all-gather.14
  147.5 52.9 reduce-scatter.11
  205.5 48.4 all-gather.6
  319.0 51.9 reduce-scatter.13
  376.6 37.4 all-gather.8
  460.8 52.0 reduce-scatter.15
  515.4 68.3 reduce-scatter.17
  589.9 37.0 all-gather.10
  630.0 68.3 reduce-scatter.19
  700.7 27.5 reduce-scatter.21
  730.5 25.7 reduce-scatter.23
  816.9 45.5 reduce-scatter.27
  865.5 58.9 reduce-scatter.31
  927.2 58.1 reduce-scatter.29
  992.0 48.7 all-reduce.3
  1044.0 49.9 reduce-scatter.25
  1189.0 35.5 all-gather.12

commit v2 on v1

--- a/solution.py
+++ b/solution.py
@@ -14,6 +14,11 @@
 BF = jnp.bfloat16
 F32 = jnp.float32
 MIB = 1 << 20
+SHORT = pl.CostEstimate(flops=1, bytes_accessed=1, transcendentals=0)
+
+
+def lasts(us):
+    return pl.CostEstimate(flops=int(us * 1e9), bytes_accessed=1, transcendentals=0)
 
 
 def mm(a, b):
@@ -33,84 +38,306 @@
     return high, (v - high.astype(F32)).astype(BF)
 
 
-def gather_rows(v):
-    return lax.all_gather(v, "fsdp", axis=0, tiled=True)
-
-
-def gather_cols(v):
-    return lax.all_gather(v, "fsdp", axis=1, tiled=True)
-
-
-def scatter_rows(v):
-    return lax.psum_scatter(v, "fsdp", scatter_dimension=0, tiled=True)
-
-
-def scatter_cols(v):
-    return lax.psum_scatter(v, "fsdp", scatter_dimension=1, tiled=True)
-
-
-def exchange(take, put, out):
-    n = lax.axis_size("fsdp")
-    me = lax.axis_index("fsdp")
-    out = put(out, me, take(me))
-    for m in range(1, n):
-        got = lax.ppermute(take(me ^ m), "fsdp", [(i, i ^ m) for i in range(n)])
-        out = put(out, me ^ m, got)
-    return out
-
-
-def rows_to_cols(v):
-    n = lax.axis_size("fsdp")
-    if n > 8:
-        return lax.all_to_all(v, "fsdp", split_axis=1, concat_axis=0, tiled=True)
-    r, c = v.shape[0], v.shape[1] // n
-    return exchange(
-        lambda j: lax.dynamic_slice_in_dim(v, j * c, c, 1),
-        lambda out, j, b: lax.dynamic_update_slice_in_dim(out, b, j * r, 0),
-        jnp.zeros((r * n, c), v.dtype),
-    )
-
-
-def cols_to_rows(v):
-    n = lax.axis_size("fsdp")
-    if n > 8:
-        return lax.all_to_all(v, "fsdp", split_axis=0, concat_axis=1, tiled=True)
-    r, c = v.shape[0] // n, v.shape[1]
-    return exchange(
-        lambda j: lax.dynamic_slice_in_dim(v, j * r, r, 0),
-        lambda out, j, b: lax.dynamic_update_slice_in_dim(out, b, j * c, 1),
-        jnp.zeros((r, c * n), v.dtype),
-    )
-
-
 def hold(*values):
     return lax.optimization_barrier(values)
 
 
-def rep_scatter_rows(v):
+def paired():
+    return lax.axis_size("fsdp") == 8
+
+
+def swap(v, m):
+    return lax.ppermute(v, "fsdp", [(i, i ^ m) for i in range(8)])
+
+
+def place():
+    me = lax.axis_index("fsdp")
+    return me // 2, lax.rem(me, 2)
+
+
+def by_core(core, mine, other, axis):
+    return jnp.where(
+        core == 0,
+        jnp.concatenate([mine, other], axis=axis),
+        jnp.concatenate([other, mine], axis=axis),
+    )
+
+
+def gather_tokens(v, *later):
+    if not paired():
+        return (lax.all_gather(v, "fsdp", axis=0, tiled=True), *later)
+    r = v.shape[0] // 2
+    a, b = v[:r], v[r:]
+    a1, b1 = swap(a, 2), swap(b, 4)
+    a2 = swap(jnp.concatenate([a, a1], axis=0), 4)
+    b2 = swap(jnp.concatenate([b, b1], axis=0), 2)
+    if later:
+        a2, b2, *later = hold(a2, b2, *later)
+    near = jnp.concatenate([v, a1, b2[:r], a2[:r], b1, a2[r:], b2[r:]], axis=0)
+    return (jnp.concatenate([near, swap(near, 1)], axis=0), *later)
+
+
+def scatter_tokens(v):
+    if not paired():
+        return lax.psum_scatter(v, "fsdp", scatter_dimension=0, tiled=True).astype(F32)
+    r = v.shape[0] // 8
+    got = swap(v[4 * r :], 1)
+    pair = lambda q: v[q * r : (q + 1) * r].astype(F32) + got[q * r : (q + 1) * r].astype(F32)
+    far = [swap(pair(q).astype(BF), 2 * q) for q in (1, 2, 3)]
+    return pair(0) + (far[0].astype(F32) + far[1].astype(F32)) + far[2].astype(F32)
+
+
+def chip_exchange(take, put, out):
+    chip, _ = place()
+    out = put(out, chip, take(chip))
+    for q in (1, 2, 3):
+        out = put(out, chip ^ q, swap(take(chip ^ q), 2 * q))
+    return out
+
+
+def home_features(v, beside):
+    if not paired():
+        return lax.all_to_all(v, "fsdp", split_axis=0, concat_axis=1, tiled=True), beside()
+    chip, core = place()
+    r, c = v.shape[0] // 8, v.shape[1]
+    both = by_core(core, v[: 4 * r], swap(v[4 * r :], 1), 1)
+    pieces = [both[:r]] + [swap(both[q * r : (q + 1) * r], 2 * q) for q in (1, 2, 3)]
+    held = hold(*pieces, *beside())
+    pieces, others = held[:4], held[4:]
+    out = jnp.zeros((r, 8 * c), v.dtype)
+    for q in range(4):
+        out = lax.dynamic_update_slice_in_dim(out, pieces[q], (chip ^ q) * (2 * c), 1)
+    return out, others
+
+
+def spread_features(v):
+    if not paired():
+        return lax.all_to_all(v, "fsdp", split_axis=1, concat_axis=0, tiled=True)
+    chip, core = place()
+    c = v.shape[1] // 8
+    near = []
+    for q in range(4):
+        piece = lax.dynamic_slice_in_dim(v, (chip ^ q) * (2 * c), 2 * c, 1)
+        near.append(piece if q == 0 else swap(piece, 2 * q))
+    near = jnp.concatenate(near, axis=0)
+    cut = lambda which: lax.dynamic_slice_in_dim(near, which * c, c, 1)
+    return jnp.concatenate([cut(core), swap(cut(1 - core), 1)], axis=0)
+
+
+def orders():
+    me = lax.axis_index("fsdp")
+    return jnp.stack([me ^ m for m in (0, 2, 4, 6, 1, 3, 5, 7)]).astype(jnp.int32)
+
+
+def pack_kernel(count, order, *refs):
+    parts, (near, far) = refs[:count], refs[count:]
+    for half, out in enumerate((near, far)):
+
+        @pl.when(pl.program_id(0) // 4 == half)
+        def _():
+            at = 0
+            for p in parts:
+                out[0, :, at : at + p.shape[1]] = p[...]
+                at += p.shape[1]
+
+
+def unpack_kernel(widths, order, *refs):
+    pieces, outs = refs[:8], refs[8:]
+    for m, piece in enumerate(pieces):
+
+        @pl.when(pl.program_id(0) == m)
+        def _():
+            at = 0
+            for w, out in zip(widths, outs):
+                out[...] = piece[0, :, at : at + w]
+                at += w
+
+
+class Exchange:
+    def __init__(self, parts, side):
+        self.side = side
+        self.parts = parts
+        if not paired():
+            return
+        if side == 1:
+            r, self.widths = parts[0].shape[0], [p.shape[1] // 8 for p in parts]
+            at = lambda m, o: (0, o[m])
+        else:
+            r, self.widths = parts[0].shape[0] // 8, [p.shape[1] for p in parts]
+            at = lambda m, o: (o[m], 0)
+        total = sum(self.widths)
+        out = jax.ShapeDtypeStruct((4, r, total), parts[0].dtype)
+        self.near, self.far = pl.pallas_call(
+            functools.partial(pack_kernel, len(parts)),
+            grid_spec=pltpu.PrefetchScalarGridSpec(
+                num_scalar_prefetch=1,
+                grid=(8,),
+                in_specs=[pl.BlockSpec((r, w), at) for w in self.widths],
+                out_specs=[
+                    pl.BlockSpec((1, r, total), lambda m, o: (jnp.minimum(m, 3), 0, 0)),
+                    pl.BlockSpec((1, r, total), lambda m, o: (jnp.maximum(m - 4, 0), 0, 0)),
+                ],
+            ),
+            out_shape=[out, out],
+            compiler_params=pltpu.CompilerParams(vmem_limit_bytes=32 * MIB),
+            name="pack",
+        )(orders(), *parts)
+
+    def across_cores(self):
+        if paired():
+            self.far = swap(self.far, 1)
+
+    def after(self, *values):
+        if not paired():
+            return values
+        *values, self.near, self.far = hold(*values, self.near, self.far)
+        return values
+
+    def parcels(self):
+        if not paired():
+            return []
+        return [
+            jnp.concatenate([self.near[q : q + 1], self.far[q : q + 1]], axis=0) for q in (1, 2, 3)
+        ]
+
+    def got_parcels(self):
+        return self.got if paired() else []
+
+    def across_chips(self, parcels=None):
+        if paired():
+            parcels = parcels or self.parcels()
+            self.got = [swap(p, 2 * q) for q, p in zip((1, 2, 3), parcels)]
+
+    def arrived(self, *values):
+        if not paired():
+            return values
+        *values, g1, g2, g3 = hold(*values, *self.got)
+        self.got = [g1, g2, g3]
+        return values
+
+    def results(self):
+        if not paired():
+            split, concat = (1, 0) if self.side == 1 else (0, 1)
+            return [
+                lax.all_to_all(p, "fsdp", split_axis=split, concat_axis=concat, tiled=True)
+                for p in self.parts
+            ]
+        _, r, total = self.near.shape
+        block = lambda i: pl.BlockSpec((1, r, total), lambda m, o: (i, 0, 0))
+        if self.side == 1:
+            at = lambda m, o: (o[m], 0)
+            shape = lambda w: (8 * r, w)
+        else:
+            at = lambda m, o: (0, o[m])
+            shape = lambda w: (r, 8 * w)
+        return pl.pallas_call(
+            functools.partial(unpack_kernel, self.widths),
+            grid_spec=pltpu.PrefetchScalarGridSpec(
+                num_scalar_prefetch=1,
+                grid=(8,),
+                in_specs=[block(0)] * 4 + [block(0)] + [block(1)] * 3,
+                out_specs=[pl.BlockSpec((r, w), at) for w in self.widths],
+            ),
+            out_shape=[jax.ShapeDtypeStruct(shape(w), self.near.dtype) for w in self.widths],
+            compiler_params=pltpu.CompilerParams(vmem_limit_bytes=32 * MIB),
+            name="unpack",
+        )(orders(), self.near, *self.got, self.far, *self.got)
+
+
+def rep_scatter(v):
     return lax.psum_scatter(v, "rep", scatter_dimension=0, tiled=True)
 
 
-def rep_scatter_cols(v):
+def rep_gather(v):
+    return lax.all_gather(v, "rep", axis=0, tiled=True)
+
+
+def share_kernel(shares, *refs):
+    *parts, out = refs
+    at = 0
+    for p in parts:
+        rows, w = p.shape[0] // shares, p.shape[1]
+        for i in range(shares):
+            out[i, 0, :, at : at + w] = p[i * rows : (i + 1) * rows, :]
+        at += w
+
+
+def rep_scatter_cols(parts):
     n, z = lax.axis_size("fsdp"), lax.axis_size("rep")
-    rows, c = v.shape
-    v = v.reshape(n, z, rows // (n * z), c).transpose(1, 0, 2, 3).reshape(rows, c)
-    return lax.psum_scatter(v, "rep", scatter_dimension=0, tiled=True)
-
-
-def rep_gather(v):
+    rows = parts[0].shape[0]
+    c = sum(p.shape[1] for p in parts)
+    v = pl.pallas_call(
+        functools.partial(share_kernel, z),
+        grid=(n,),
+        in_specs=[pl.BlockSpec((rows // n, p.shape[1]), lambda i: (i, 0)) for p in parts],
+        out_specs=pl.BlockSpec((z, 1, rows // (n * z), c), lambda i: (0, i, 0, 0)),
+        out_shape=jax.ShapeDtypeStruct((z, n, rows // (n * z), c), parts[0].dtype),
+        compiler_params=pltpu.CompilerParams(vmem_limit_bytes=32 * MIB),
+        cost_estimate=SHORT,
+        name="shares",
+    )(*parts)
+    return rep_scatter(v.reshape(rows, c))
+
+
+def widen_kernel(*refs):
+    joined, *outs = refs
+    at = 0
+    for out in outs:
+        w = out.shape[1]
+        out[...] = joined[:, at : at + w].astype(F32)
+        at += w
+
+
+def widened(v, widths):
+    r = v.shape[0]
+    rows = min(r, 32)
+    return pl.pallas_call(
+        widen_kernel,
+        grid=(r // rows,),
+        in_specs=[pl.BlockSpec((rows, v.shape[1]), lambda i: (i, 0))],
+        out_specs=[pl.BlockSpec((rows, w), lambda i: (i, 0)) for w in widths],
+        out_shape=[jax.ShapeDtypeStruct((r, w), F32) for w in widths],
+        compiler_params=pltpu.CompilerParams(vmem_limit_bytes=32 * MIB),
+        cost_estimate=SHORT,
+        name="widened",
+    )(v)
+
+
+def rep_sum(v):
     n = lax.axis_size("rep")
-    z = lax.axis_index("rep")
-    up, down = [v], [v]
+    total = v.astype(F32)
     for s in range(1, n):
-        up.append(lax.ppermute(up[-1], "rep", [(i, i + 1) for i in range(s - 1, n - 1)]))
-        down.append(lax.ppermute(down[-1], "rep", [(i + 1, i) for i in range(n - s)]))
-    out = jnp.zeros((n,) + v.shape, F32)
-    out = lax.dynamic_update_index_in_dim(out, v.astype(F32), z, 0)
-    for s in range(1, n):
-        piece = jnp.where(z >= s, up[s], down[n - s]).astype(F32)
-        out = lax.dynamic_update_index_in_dim(out, piece, lax.rem(z - s + n, n), 0)
-    return out.reshape((n * v.shape[0],) + v.shape[1:])
+        total = total + lax.ppermute(v, "rep", [(i, (i + s) % n) for i in range(n)]).astype(F32)
+    return total
+
+
+def scatter_features(v):
+    if not paired():
+        return lax.psum_scatter(v, "fsdp", scatter_dimension=1, tiled=True).astype(F32)
+    chip, core = place()
+    r = v.shape[0]
+    v = v.reshape(r, 4, 2, -1)
+    cut = lambda which: lax.dynamic_index_in_dim(v, which, 2, keepdims=False).transpose(1, 0, 2)
+    pair = cut(core).astype(F32) + swap(cut(1 - core), 1).astype(F32)
+    low = pair.astype(BF)
+    total = lax.dynamic_index_in_dim(pair, chip, 0, keepdims=False)
+    for q in (1, 2, 3):
+        got = swap(lax.dynamic_index_in_dim(low, chip ^ q, 0, keepdims=False), 2 * q)
+        total = total + got.astype(F32)
+    return total
+
+
+def gather_features(v):
+    if not paired():
+        return lax.all_gather(v, "fsdp", axis=1, tiled=True)
+    chip, core = place()
+    r, c = v.shape
+    both = by_core(core, v, swap(v, 1), 1)
+    out = jnp.zeros((r, 8 * c), v.dtype)
+    for q in range(4):
+        got = both if q == 0 else swap(both, 2 * q)
+        out = lax.dynamic_update_slice_in_dim(out, got, (chip ^ q) * (2 * c), 1)
+    return out
 
 
 def whole_block(a):
@@ -134,32 +361,34 @@
 
 
 def front_kernel(
-    ranks, tok, gain, shift, lerp, narrow, widen, fnarrow, xk, xv, xr, xg, hid, low
+    ranks, tok, gain, shift, lerp, narrow, widen, fnarrow, xk, xv, xr, xg, hid, low, nh, nl, wb, fh, fl
 ):
+    @pl.when(pl.program_id(0) == 0)
+    def _():
+        nh[...], nl[...] = halves(jnp.transpose(narrow[...]))
+        fh[...], fl[...] = halves(jnp.transpose(fnarrow[...]))
+        wb[...] = widen[...].astype(BF)
+
     normed = normal_rows(tok[...].astype(F32)) * gain[...] + shift[...]
     delta = shifted(normed) - normed
     bh, bl = halves(normed + delta * lerp[0:1, :])
-    wide = ranks * 5
-    pre = mm(bh, narrow[...])
-    hidden = jnp.tanh(pre[:, :wide] + pre[:, wide:] + mm(bl, narrow[:, :wide]))
+    hidden = jnp.tanh(mm(bh, nh[...]) + mm(bh, nl[...]) + mm(bl, nh[...]))
     hid[...] = hidden
     hb = hidden.astype(BF)
     for f, out in ((1, xk), (2, xv), (3, xr), (4, xg), (0, None)):
         rows = slice(f * ranks, (f + 1) * ranks)
-        x = normed + delta * (lerp[f + 1 : f + 2, :] + mm(hb[:, rows], widen[rows, :]))
+        x = normed + delta * (lerp[f + 1 : f + 2, :] + mm(hb[:, rows], wb[rows, :]))
         if out is not None:
             out[...] = x.astype(BF)
         else:
             dh, dl = halves(x)
-            fd = low.shape[1]
-            pre = mm(dh, fnarrow[...])
-            low[...] = jnp.tanh(pre[:, :fd] + pre[:, fd:] + mm(dl, fnarrow[:, :fd]))
+            low[...] = jnp.tanh(mm(dh, fh[...]) + mm(dh, fl[...]) + mm(dl, fh[...]))
 
 
 def front(seq_len, tokens, gain, shift, lerp, narrow, widen, fnarrow):
     g, d = tokens.shape
     ranks = widen.shape[0] // 5
-    fd = fnarrow.shape[1] // 2
+    fd = fnarrow.shape[0]
     per_seq = lambda w: pl.BlockSpec((seq_len, w), lambda s: (s, 0))
     return pl.pallas_call(
         functools.partial(front_kernel, ranks),
@@ -172,10 +401,15 @@
             jax.ShapeDtypeStruct((g, 5 * ranks), F32),
             jax.ShapeDtypeStruct((g, fd), F32),
         ],
+        scratch_shapes=[
+            pltpu.VMEM((d, 5 * ranks), BF),
+            pltpu.VMEM((d, 5 * ranks), BF),
+            pltpu.VMEM((5 * ranks, d), BF),
+            pltpu.VMEM((d, fd), BF),
+            pltpu.VMEM((d, fd), BF),
+        ],
         compiler_params=pltpu.CompilerParams(vmem_limit_bytes=48 * MIB),
-        cost_estimate=pl.CostEstimate(
-            flops=g * d * 2 * 5 * 256, bytes_accessed=g * d * 10, transcendentals=0
-        ),
+        cost_estimate=lasts(22),
         name="token_shift",
     )(tokens, gain, shift, lerp, narrow, widen, fnarrow)
 
@@ -206,9 +440,17 @@
     dwid_out,
     dnar_out,
     dfn_out,
+    narrow_low,
+    widen_low,
+    fnarrow_low,
+    fwiden_low,
 ):
     @pl.when(pl.program_id(0) == 0)
     def _():
+        narrow_low[...] = narrow[...].astype(BF)
+        widen_low[...] = widen[...].astype(BF)
+        fnarrow_low[...] = fnarrow[...].astype(BF)
+        fwiden_low[...] = fwiden[...].astype(BF)
         for ref in (vec_out, dwid_out, dnar_out, dfn_out):
             ref[...] = jnp.zeros_like(ref)
 
@@ -219,7 +461,7 @@
     hb = hidden.astype(BF)
     lowv = low[...]
     colsum = lambda v: jnp.sum(v, axis=0, keepdims=True)
-    dlow = mm_nt(draw[...].astype(BF), fwiden[...]) * (1.0 - lowv * lowv)
+    dlow = mm_nt(draw[...].astype(BF), fwiden_low[...]) * (1.0 - lowv * lowv)
     dlow = dlow.astype(BF)
     total = jnp.zeros(normed.shape, F32)
     moved = jnp.zeros(normed.shape, F32)
@@ -232,9 +474,9 @@
         (4, dg, wg),
     ):
         rows = slice(f * ranks, (f + 1) * ranks)
-        mu = lerp[f + 1 : f + 2, :] + mm(hb[:, rows], widen[rows, :])
+        mu = lerp[f + 1 : f + 2, :] + mm(hb[:, rows], widen_low[rows, :])
         if f == 0:
-            dx = mm_nt(dlow, fnarrow[...])
+            dx = mm(dlow, fnarrow_low[...])
             dfn_out[...] += mm_tn(dlow, (normed + delta * mu).astype(BF))
         else:
             dx = mm_nt(d_ref[...], w_ref[...])
@@ -244,9 +486,9 @@
         vec_out[f + 1 : f + 2, :] += colsum(doff)
         db = doff.astype(BF)
         dwid_out[rows, :] += mm_tn(hb[:, rows], db)
-        dhid.append(mm_nt(db, widen[rows, :]))
+        dhid.append(mm_nt(db, widen_low[rows, :]))
     dpre = (jnp.concatenate(dhid, axis=1) * (1.0 - hidden * hidden)).astype(BF)
-    dblend = mm_nt(dpre, narrow[...])
+    dblend = mm(dpre, narrow_low[...])
     base = lerp[0:1, :]
     dnar_out[...] += mm_tn(dpre, (normed + delta * base).astype(BF))
     vec_out[0:1, :] += colsum(dblend * delta)
@@ -281,10 +523,14 @@
             jax.ShapeDtypeStruct((5 * ranks, d), F32),
             jax.ShapeDtypeStruct((fd, d), F32),
         ],
+        scratch_shapes=[
+            pltpu.VMEM((5 * ranks, d), BF),
+            pltpu.VMEM((5 * ranks, d), BF),
+            pltpu.VMEM((fd, d), BF),
+            pltpu.VMEM((fd, c), BF),
+        ],
         compiler_params=pltpu.CompilerParams(vmem_limit_bytes=56 * MIB),
-        cost_estimate=pl.CostEstimate(
-            flops=g * d * 2 * 18 * 256, bytes_accessed=g * d * 6, transcendentals=0
-        ),
+        cost_estimate=SHORT,
         name="token_shift_back",
     )(tokens, hid, low, *grads, draw, *params, *weights)
 
@@ -475,9 +721,7 @@
             out_specs=cols,
             out_shape=jax.ShapeDtypeStruct((rows, c), BF),
             compiler_params=params,
-            cost_estimate=pl.CostEstimate(
-                flops=flops, bytes_accessed=rows * c * 22, transcendentals=rows * c * 7
-            ),
+            cost_estimate=SHORT,
             name="decay_mix",
         )(r, k, v, g, w, u, gain, bias, spans_a, level_a)
     spans_t = jnp.asarray(
@@ -493,15 +737,123 @@
         out_shape=[jax.ShapeDtypeStruct((rows, c), BF)] * 4
         + [jax.ShapeDtypeStruct((rows, c), F32), jax.ShapeDtypeStruct((4, c), F32)],
         compiler_params=params,
-        cost_estimate=pl.CostEstimate(
-            flops=flops * 4, bytes_accessed=rows * c * 36, transcendentals=rows * c * 7
-        ),
+        cost_estimate=SHORT,
         name="decay_mix_back",
     )(r, k, v, g, w, dmixed, u, gain, bias, spans_a, spans_t, level_a)
 
 
 def D_OF(u, c):
     return c * lax.axis_size("fsdp")
+
+
+def step_shift(length, v, back=False):
+    rows = v.shape[0]
+    at = lax.rem(lax.broadcasted_iota(jnp.int32, v.shape, 0), length)
+    edge = at == (length - 1 if back else 0)
+    return jnp.where(edge, 0.0, pltpu.roll(v, rows - 1 if back else 1, 0))
+
+
+def feed_kernel(length, n2, lerp, wla, wc, *refs):
+    kc_out, sq_out, fac_out, va_out = refs[-4:]
+    n = n2[...].astype(F32)
+    delta = step_shift(length, n) - n
+    kc = (n + delta * lerp[0:1, :]).astype(BF)
+    kc_out[...] = kc
+    act = mm(kc, wla[:, : wc.shape[0]])
+    soft = jnp.maximum(act, 0.0) + jnp.log1p(jnp.exp(-jnp.abs(act)))
+    fac_out[...] = 2.0 * soft * jax.nn.sigmoid(act)
+    sq = (soft * soft).astype(BF)
+    sq_out[...] = sq
+    va_out[...] = mm(sq, wc[...]).astype(BF)
+
+
+def feed(length, n2, lerp, wla, wc, part, earlier=()):
+    g, d = n2.shape
+    f = wc.shape[0]
+    half = g // 2
+    rows = 2 * length if half % (2 * length) == 0 else length
+    if half % rows:
+        rows = half
+    first = part * (half // rows)
+    block = lambda w: pl.BlockSpec((rows, w), lambda s: (first + s, 0))
+    shape = lambda w, t: jax.ShapeDtypeStruct((g, w), t)
+    return pl.pallas_call(
+        functools.partial(feed_kernel, length),
+        grid=(half // rows,),
+        in_specs=[block(d)]
+        + [whole_block(a) for a in (lerp, wla, wc)]
+        + [pl.BlockSpec(memory_space=pl.ANY)] * len(earlier),
+        out_specs=[block(d), block(f), block(f), block(d)],
+        out_shape=[shape(d, BF), shape(f, BF), shape(f, F32), shape(d, BF)],
+        input_output_aliases={4 + i: i for i in range(len(earlier))},
+        compiler_params=pltpu.CompilerParams(vmem_limit_bytes=52 * MIB),
+        cost_estimate=lasts(8),
+        name="feed",
+    )(n2, lerp, wla, wc, *earlier)
+
+
+def gate_kernel(length, n2, lerp, wla, rc_out, gate_out):
+    n = n2[...].astype(F32)
+    rc = (n + (step_shift(length, n) - n) * lerp[1:2, :]).astype(BF)
+    rc_out[...] = rc
+    gate_out[...] = jax.nn.sigmoid(mm(rc, wla[:, wla.shape[1] - gate_out.shape[1] :])).astype(BF)
+
+
+def feed_gate(length, n2, lerp, wla):
+    g, d = n2.shape
+    c = d // lax.axis_size("fsdp")
+    rows = 2 * length if g % (2 * length) == 0 else length
+    block = lambda w: pl.BlockSpec((rows, w), lambda s: (s, 0))
+    return pl.pallas_call(
+        functools.partial(gate_kernel, length),
+        grid=(g // rows,),
+        in_specs=[block(d), whole_block(lerp), whole_block(wla)],
+        out_specs=[block(d), block(c)],
+        out_shape=[jax.ShapeDtypeStruct((g, d), BF), jax.ShapeDtypeStruct((g, c), BF)],
+        compiler_params=pltpu.CompilerParams(vmem_limit_bytes=32 * MIB),
+        cost_estimate=SHORT,
+        name="feed_gate",
+    )(n2, lerp, wla)
+
+
+def feed_back_kernel(length, dv, n2, fac, dgate, lerp, wla, wc, dkey_out, dn_out, vec_out):
+    @pl.when(pl.program_id(0) == 0)
+    def _():
+        vec_out[...] = jnp.zeros_like(vec_out)
+
+    dkey = (mm_nt(dv[...], wc[...]) * fac[...]).astype(BF)
+    dkey_out[...] = dkey
+    n = n2[...].astype(F32)
+    delta = step_shift(length, n) - n
+    f = wc.shape[0]
+    dk = mm_nt(dkey, wla[:, :f])
+    dr = mm_nt(dgate[...], wla[:, f:])
+    vec_out[0:1, :] += jnp.sum(dk * delta, axis=0, keepdims=True)
+    vec_out[1:2, :] += jnp.sum(dr * delta, axis=0, keepdims=True)
+    moved = dk * lerp[0:1, :] + dr * lerp[1:2, :]
+    dn_out[...] = (dk + dr - moved + step_shift(length, moved, True)).astype(BF)
+
+
+def feed_back(length, dv, n2, fac, dgate, lerp, wla, wc):
+    g, d = n2.shape
+    f, c = wc.shape[0], dgate.shape[1]
+    rows = 2 * length if g % (2 * length) == 0 else length
+    block = lambda w: pl.BlockSpec((rows, w), lambda s: (s, 0))
+    return pl.pallas_call(
+        functools.partial(feed_back_kernel, length),
+        grid=(g // rows,),
+        in_specs=[block(d), block(d), block(f), block(c)]
+        + [whole_block(a) for a in (lerp, wla, wc)],
+        out_specs=[block(f), block(d), pl.BlockSpec((2, d), lambda s: (0, 0))],
+        out_shape=[
+            jax.ShapeDtypeStruct((g, f), BF),
+            jax.ShapeDtypeStruct((g, d), BF),
+            jax.ShapeDtypeStruct((2, d), F32),
+        ],
+        compiler_params=pltpu.CompilerParams(vmem_limit_bytes=52 * MIB),
+        cost_estimate=SHORT,
+        name="feed_back",
+    )(dv, n2, fac, dgate, lerp, wla, wc)
 
 
 def body(
@@ -541,39 +893,42 @@
     fd = fading_narrow_weights.shape[1]
 
     tok_home = incoming_symbols.reshape(home, d)
-    tokens = gather_rows(tok_home)
-    weights = rows_to_cols(
-        jnp.concatenate(
-            [
-                w.reshape(c, n, c)
-                for w in (lookup_weights, content_weights, acceptor_weights, valve_weights)
-            ],
-            axis=2,
-        ).reshape(c, 4 * d)
-    )
-    wk, wv, wr, wg = (weights[:, i * c : (i + 1) * c] for i in range(4))
+    z = lax.axis_index("rep")
+    share = c // lax.axis_size("rep")
+    feed_weights = Exchange(
+        [
+            lax.dynamic_slice_in_dim(t, z * share, share, 0)
+            for t in (feed_lookup_weights, feed_acceptor_weights)
+        ],
+        1,
+    )
+    feed_weights.across_cores()
+    feed_weights.across_chips()
+    mix_weights = Exchange(
+        (lookup_weights, content_weights, acceptor_weights, valve_weights), 1
+    )
+    mix_weights.across_cores()
+    parcels = mix_weights.parcels()
+    tokens, *held = gather_tokens(tok_home, *parcels, *feed_weights.got_parcels())
+    mix_weights.across_chips(held[: len(parcels)])
+    feed_weights.got = held[len(parcels) :]
     positions = lax.broadcasted_iota(jnp.int32, (seqs, length), 1)
     mask = (positions < string_extents[:, None]).astype(F32).reshape(home, 1)
-    adj_low = adjoint_signal.reshape(home, d) * mask.astype(BF)
-    d_out = adj_low.astype(F32)
-    d_out_cols = rows_to_cols(adj_low).astype(F32)
+    d_out = adjoint_signal.reshape(home, d).astype(F32) * mask
 
     row = lambda v: v.reshape(1, -1)
     mine = lambda v: lax.dynamic_slice_in_dim(v, me * c, c, v.ndim - 1)
     gain1, shift1 = row(first_scaling_factor), row(first_scaling_shift)
-    nh, nl = halves(lerp_narrow_weights)
-    fh, fl = halves(fading_narrow_weights)
-    widen_low = lerp_widen_weights.reshape(5 * ranks, d).astype(BF)
+    narrow, fnarrow = lerp_narrow_weights.T, fading_narrow_weights.T
+    widen = lerp_widen_weights.reshape(5 * ranks, d)
+    feed_shares = jnp.concatenate(feed_weights.results(), axis=1).reshape(n, share, -1)
+    tokens, feed_shares = hold(tokens, feed_shares)
+    feed_full = lax.all_gather(feed_shares, "rep", axis=1, tiled=True).reshape(d, -1)
     xk, xv, xr, xg, hidden, low = front(
-        length,
-        tokens,
-        gain1,
-        shift1,
-        lerp_factors,
-        jnp.concatenate([nh, nl], axis=1),
-        widen_low,
-        jnp.concatenate([fh, fl], axis=1),
-    )
+        length, tokens, gain1, shift1, lerp_factors, narrow, widen, fnarrow
+    )
+    (low,) = mix_weights.arrived(low)
+    wk, wv, wr, wg = mix_weights.results()
     fwiden_mine = mine(fading_widen_weights)
     w = -jnp.exp(
         mine(row(fading_baseline))
@@ -584,57 +939,38 @@
         mine(row(t)) for t in (present_reward, cluster_scaling_factor, cluster_scaling_shift)
     )
     mixed = wkv(length, r, k, v, g, w, u, gn_gain, gn_bias)
-    branch = scatter_rows(mm(mixed, emission_weights).astype(BF))
-    residual = tok_home.astype(F32) + branch.astype(F32)
+    mixed, feed_full = hold(mixed, feed_full)
+    branch = scatter_tokens(mm(mixed, emission_weights).astype(BF))
+    residual = tok_home.astype(F32) + branch
 
     center = residual - jnp.mean(residual, axis=-1, keepdims=True)
     rstd2 = lax.rsqrt(jnp.mean(center * center, axis=-1, keepdims=True) + norm_eps)
     unit2 = center * rstd2
-    normed2_home = unit2 * second_scaling_factor + second_scaling_shift_vec
-    normed2 = gather_rows(normed2_home.astype(BF)).astype(F32)
-    weights2 = rows_to_cols(
-        jnp.concatenate(
-            [feed_lookup_weights.reshape(c, n, -1), feed_acceptor_weights.reshape(c, n, -1)],
-            axis=2,
-        ).reshape(c, -1)
-    )
+    (normed2,) = gather_tokens((unit2 * second_scaling_factor + second_scaling_shift_vec).astype(BF))
     fc = feed_content_weights.shape[0]
-    wl, wa = weights2[:, :fc], weights2[:, fc:]
-
-    def before(t):
-        t = t.reshape(-1, length, d)
-        return jnp.concatenate([jnp.zeros_like(t[:, :1]), t[:, :-1]], axis=1).reshape(-1, d)
-
-    def after(t):
-        t = t.reshape(-1, length, d)
-        return jnp.concatenate([t[:, 1:], jnp.zeros_like(t[:, :1])], axis=1).reshape(-1, d)
-
-    delta2 = before(normed2) - normed2
-    key_chan = (normed2 + delta2 * feed_lerp_factors[0]).astype(BF)
-    recept_chan = (normed2 + delta2 * feed_lerp_factors[1]).astype(BF)
-    key_act = mm(key_chan, wl)
-    soft = jax.nn.softplus(key_act)
-    squared = (soft * soft).astype(BF)
-    value_act = scatter_cols(mm(squared, feed_content_weights).astype(BF)).astype(F32)
-    gate = jax.nn.sigmoid(mm(recept_chan, wa))
+    recept_chan, gate = feed_gate(length, normed2, feed_lerp_factors, feed_full)
+    feed_part = lambda *t: feed(length, normed2, feed_lerp_factors, feed_full, feed_content_weights, *t)
+    gate, earlier = home_features(gate, lambda: feed_part(0))
+    gate = gate.astype(F32)
+    (d_value,) = gather_tokens((d_out * gate).astype(BF))
+    key_chan, squared, factor, value_part = feed_part(1, earlier)
+    d_content = mm_tn(squared, d_value).astype(BF)
+    d_value, d_content, value_part = hold(d_value, d_content, value_part)
+    content_share = lax.psum_scatter(d_content, "rep", scatter_dimension=0, tiled=True)
+    value_act = scatter_tokens(value_part)
     gated = gate * value_act
-    layer_output = (residual + cols_to_rows(gated.astype(BF)).astype(F32)) * mask
-    d_value = gather_cols((d_out_cols * gate).astype(BF))
-    d_gate = (d_out_cols * gated * (1.0 - gate)).astype(BF)
-
-    d_key = (mm_nt(d_value, feed_content_weights) * (2.0 * soft * jax.nn.sigmoid(key_act))).astype(BF)
-    content_share = rep_scatter_rows(mm_tn(squared, d_value).astype(BF))
-    d_key_chan = mm_nt(d_key, wl)
-    d_recept_chan = mm_nt(d_gate, wa)
-    moved = d_key_chan * feed_lerp_factors[0] + d_recept_chan * feed_lerp_factors[1]
-    d_normed2 = d_key_chan + d_recept_chan - moved + after(moved)
-    feed_lerp_part = jnp.stack(
-        [jnp.sum(d_key_chan * delta2, axis=0), jnp.sum(d_recept_chan * delta2, axis=0)]
-    )
-    d_normed2 = scatter_rows(d_normed2.astype(BF)).astype(F32)
-    lookup_share = rep_scatter_cols(mm_tn(key_chan, d_key).astype(BF))
-    accept_share = rep_scatter_cols(mm_tn(recept_chan, d_gate).astype(BF))
+    layer_output = (residual + gated) * mask
+    d_gate = spread_features((d_out * gated * (1.0 - gate)).astype(BF))
+
+    d_key, d_normed2, feed_lerp_part = feed_back(
+        length, d_value, normed2, factor, d_gate, feed_lerp_factors, feed_full, feed_content_weights
+    )
     d_normed2, content_share = hold(d_normed2, content_share)
+    feed_share = rep_scatter_cols(
+        (mm_tn(key_chan, d_key).astype(BF), mm_tn(recept_chan, d_gate).astype(BF))
+    )
+    d_normed2 = scatter_tokens(d_normed2)
+    content_sum = rep_gather(content_share)
 
     def norm_back(unit, rstd, e):
         return rstd * (
@@ -646,31 +982,19 @@
     d_residual = d_out + norm_back(unit2, rstd2, d_normed2 * second_scaling_factor)
     norm2_part = jnp.stack([jnp.sum(d_normed2 * unit2, axis=0), jnp.sum(d_normed2, axis=0)])
 
-    d_branch = gather_rows(d_residual.astype(BF))
+    (d_branch,) = gather_tokens(d_residual.astype(BF))
     d_mixed = mm_nt(d_branch, emission_weights)
-    emission_share = rep_scatter_rows(mm_tn(mixed, d_branch).astype(BF))
-    d_mixed, lookup_share = hold(d_mixed, lookup_share)
+    emission_share = rep_scatter(mm_tn(mixed, d_branch).astype(BF))
     d_r, d_k, d_v, d_g, d_raw, mix_vec = wkv(
         length, r, k, v, g, w, u, gn_gain, gn_bias, d_mixed
     )
-    d_r, accept_share, emission_share = hold(d_r, accept_share, emission_share)
-    share_one = rep_scatter_cols(
-        jnp.concatenate([mm_tn(xk, d_k), mm_tn(xv, d_v)], axis=1).astype(BF)
-    )
-    share_two = rep_scatter_cols(
-        jnp.concatenate([mm_tn(xr, d_r), mm_tn(xg, d_g)], axis=1).astype(BF)
-    )
-
-    def settle(share, parts):
-        total = rep_gather(cols_to_rows(share)).reshape(c, n, parts, -1)
-        return [total[:, :, i].reshape(c, -1) for i in range(parts)]
-
-    feed_content_grads = rep_gather(content_share)
-    emission_weights_grads = rep_gather(emission_share)
-    (feed_lookup_grads,) = settle(lookup_share, 1)
-    (feed_acceptor_grads,) = settle(accept_share, 1)
-    lookup_weights_grads, content_weights_grads = settle(share_one, 2)
-    acceptor_weights_grads, valve_weights_grads = settle(share_two, 2)
+    d_r, d_k, d_v, d_g, feed_share = hold(d_r, d_k, d_v, d_g, feed_share)
+    time_share = rep_scatter_cols(
+        [mm_tn(x, t).astype(BF) for x, t in ((xk, d_k), (xv, d_v), (xr, d_r), (xg, d_g))]
+    )
+    feed_sums = Exchange([feed_share[:, :fc], feed_share[:, fc:]], 0)
+    feed_sums.across_cores()
+    feed_sums.across_chips()
     d_normed, vec_part, widen_part, narrow_part, fnarrow_part = back(
         length,
         tokens,
@@ -678,25 +1002,40 @@
         low,
         (d_k, d_v, d_r, d_g),
         d_raw,
-        (gain1, shift1, lerp_factors, nh, widen_low, fh, fwiden_mine.astype(BF)),
+        (gain1, shift1, lerp_factors, narrow, widen, fnarrow, fwiden_mine),
         (wk, wv, wr, wg),
     )
-    d_normed = scatter_rows(d_normed).astype(F32)
+    d_normed, content_sum, emission_share = feed_sums.arrived(
+        *hold(d_normed, content_sum, emission_share)
+    )
+    feed_sum = rep_gather(jnp.concatenate(feed_sums.results(), axis=1))
+    d_normed = scatter_tokens(d_normed)
+    small = scatter_features(
+        jnp.concatenate(
+            [vec_part, widen_part, narrow_part, fnarrow_part, norm2_part, feed_lerp_part], axis=0
+        ).astype(BF)
+    )
+    fwiden_part = mm_tn(low.astype(BF), d_raw.astype(BF))
+    small = rep_sum(jnp.concatenate([small, fwiden_part, mix_vec], axis=0).astype(BF))
+    small = gather_features(small.astype(BF)).astype(F32)
+    small, time_share = hold(small, time_share)
+    time_sums = Exchange([time_share[:, i * c : (i + 1) * c] for i in range(4)], 0)
+    time_sums.across_cores()
+    time_sums.across_chips()
+    time_sum = rep_gather(jnp.concatenate([*time_sums.results(), emission_share], axis=1))
+    (feed_content_grads,) = widened(content_sum, (d,))
+    feed_lookup_grads, feed_acceptor_grads = widened(feed_sum, (n * fc, n * c))
+    (
+        lookup_weights_grads,
+        content_weights_grads,
+        acceptor_weights_grads,
+        valve_weights_grads,
+        emission_weights_grads,
+    ) = widened(time_sum, (d,) * 5)
     tok_f = tok_home.astype(F32)
     center1 = tok_f - jnp.mean(tok_f, axis=-1, keepdims=True)
     rstd1 = lax.rsqrt(jnp.mean(center1 * center1, axis=-1, keepdims=True) + norm_eps)
     token_grad = d_residual + norm_back(center1 * rstd1, rstd1, d_normed * first_scaling_factor)
-
-    small = scatter_cols(
-        jnp.concatenate(
-            [vec_part, widen_part, narrow_part, fnarrow_part, norm2_part, feed_lerp_part], axis=0
-        )
-    )
-    fwiden_part = lax.dot_general(
-        low, d_raw, (((0,), (0,)), ((), ())), precision=lax.Precision.HIGHEST
-    )
-    small = lax.psum(jnp.concatenate([small, fwiden_part, mix_vec], axis=0), "rep")
-    small = gather_cols(small)
     cuts = np.cumsum([8, 5 * ranks, 5 * ranks, fd, 2, 2, fd, 4])
     vec, widen_g, narrow_g, fnarrow_g, norm2_g, feed_lerp_g, fwiden_g, mix_g = (
         small[a:b] for a, b in zip([0, *cuts[:-1]], cuts)

time: 1310 us -> 853 us (0.65); the launches traced: 1290 us -> 849 us
  waiting for transfers between devices: 642 us -> 409 us
  local copies, waits for them, and re-layouts: 207 us -> 89.6 us
  Pallas kernels: 115 us -> 198 us
  matrix products: 110 us -> 35.6 us
  starting transfers between devices: 122 us -> 70 us
  other arithmetic: 77 us -> 29 us
    reduce_scatter x11 -> x4, waiting for transfers between devices: 258 us -> 7.28 us  [the longest x3 7.26 us: rep_scatter(): return lax.psum_scatter(v, 'rep', scatter_dimension=0, tiled=True)]
    pallas_call x0 -> x17, Pallas kernels: none -> 77.4 us  [the longest x2 21.6 us: feed(): pl.pallas_call(functools.partial(feed_kernel, length), grid=(half // rows...]
    all_gather x5 -> x4, waiting for transfers between devices: 60.2 us -> 133 us  [the longest x3 126 us: rep_gather(): return lax.all_gather(v, 'rep', axis=0, tiled=True)]
    ppermute x92 -> x71, waiting for transfers between devices: 322 us -> 269 us  [the longest x68 242 us: swap(): return lax.ppermute(v, 'fsdp', [(i, i ^ m) for i in range(8)])]
    ppermute x92 -> x71, starting transfers between devices: 120 us -> 69 us  [the longest x68 64.8 us: swap(): return lax.ppermute(v, 'fsdp', [(i, i ^ m) for i in range(8)])]
    dynamic_update_slice x56 -> x7, local copies, waits for them, and re-layouts: 34 us -> 0.22 us  [the longest x3 0.15 us: gather_features(): out = lax.dynamic_update_slice_in_dim(out, got, (chip ^ q) * (2 * c), 1)]
    dynamic_update_slice x24 -> x1, other arithmetic: 33.8 us -> 0.16 us  [gather_features(): out = lax.dynamic_update_slice_in_dim(out, got, (chip ^ q) * (2 * c), 1)]
    slice x6 -> x21, local copies, waits for them, and re-layouts: 44.1 us -> 10.7 us  [the longest x4 5.79 us: scatter_tokens(): got = swap(v[4 * r:], 1)]
  transfers between devices with their start and end apart: 109 -> 79, of which waited for: 43 -> 51; matrix products, arithmetic and copies ran while one was open for 19% -> 11% of each run, Pallas kernels for 2% -> 22%
where the time goes in v2:
time: 853 us; the launch traced here: 849 us
  waiting for transfers between devices  409 us (48%)
  Pallas kernels  198 us (23%)
  local copies, waits for them, and re-layouts  89.6 us (11%)
  starting transfers between devices  70 us (8%)
  matrix products  35.6 us (4%)
  other arithmetic  29 us (3%)
  between operations  17.2 us (2%)
    ppermute x68, waiting for transfers between devices, swap(): return lax.ppermute(v, 'fsdp', [(i, i ^ m) for i in range(8)])  242 us
    all_gather x3, waiting for transfers between devices, rep_gather(): return lax.all_gather(v, 'rep', axis=0, tiled=True)  126 us
    ppermute x68, starting transfers between devices, swap(): return lax.ppermute(v, 'fsdp', [(i, i ^ m) for i in range(8)])  64.8 us
    unnamed x224, local copies, waits for them, and re-layouts  54.4 us
    pallas_call x1, Pallas kernels, back(): pl.pallas_call(functools.partial(back_kernel, ranks), grid=(g // seq_len,...  48.7 us
    pallas_call x1, Pallas kernels, wkv(): pl.pallas_call(functools.partial(wkv_back_kernel, levels, count, width),...  30.2 us
    ppermute x3, waiting for transfers between devices, rep_sum(): lax.ppermute(v, 'rep', [(i, (i + s) % n) for i in range(n)]).astype(F32)  27.2 us
    pallas_call x1, Pallas kernels, front(): pl.pallas_call(functools.partial(front_kernel, ranks), grid=(g // seq_len...  26.2 us
  transfers between devices with their start and end apart: 79, of which 51 were waited for; matrix products, arithmetic and copies ran while one was open for 11% of the time, Pallas kernels for 22%

profile of v2, /device:TPU:0, one launch (start us, length us, event | category | flops | bytes accessed | tf_op | source)
XLA Modules:
  0.0 848.7 jit_solution(11049551771536498334)
XLA Ops:
  50.7 6.0 collective-permute-done.7.refs_2_.refs_6_
  75.8 26.2 %token_shift.1 = (bf16[1024,2048]{1,0:T(8,128)(2,1)}, bf16[1024,2048]{1,0:T(8,128)(2,1)}, bf16[1024,2048]{1,0:T(8,128)(2,1)}, bf16[1024,2048]{1,0:T(8,128)(2,1)}...) custom-call(bf16[1024,2048]{1,0:T(8,128)(2,1)} %constant_dynamic-update-slice_fusion.2.tok, f32[1,2048]{1,0:T(1,128)S(1)} %bitcast.134, ...), custom_call_target="tpu_custom_call" | custom-call | flops 22000001024 | bytes 1 | tf_op jit(solution)/shard_map/token_shift/pallas_call | solution.py:393
  102.9 13.1 %collective-permute-done.11.refs_2_.refs_6_ = bf16[2,256,1024]{2,1,0:T(8,128)(2,1)S(1)} collective-permute-done((bf16[2,256,1024]{2,1,0:T(8,128)(2,1)}, bf16[2,256,1024]{2,1,0:T(8,128)(2,1)S(1)}, u32[]{:S(2)}, u32[]{:S(2)}) %collective-permute-start.11) | collective-permute-done | bytes 1048608 | tf_op jit(solution)/shard_map/ppermute | solution.py:50
  129.6 15.4 %decay_mix.1 = bf16[1024,256]{1,0:T(8,128)(2,1)S(1)} custom-call(f32[1024,256]{1,0:T(8,128)S(1)} %fusion.45.r.r_ref, f32[1024,256]{1,0:T(8,128)S(1)} %fusion.46.k.k_ref, f32[1024,256]{1,0:T(8,128)S(1)} %fusion.47.v.v_ref, f32[1024,256]{1,0:T(8,128)S(1)} %fusion.48.g.g_ref, f32[1024,256]{1,0:T(8,128)S(1)} %fusion.2.w.w_ref, f32[1,256]{1,0:T(1,128)S(1)} %bitcast.135, ...), custom_call_target="tpu_custom_call" | custom-call | flops 1 | bytes 1 | tf_op jit(solution)/shard_map/decay_mix/pallas_call | solution.py:717
  146.8 7.5 all-gather.5.cloned.1.call-done
  165.2 11.1 %collective-permute-done.14 = bf16[128,2048]{1,0:T(8,128)(2,1)S(1)} collective-permute-done((bf16[128,2048]{1,0:T(8,128)(2,1)S(1)}, bf16[128,2048]{1,0:T(8,128)(2,1)S(1)}, u32[]{:S(2)}, u32[]{:S(2)}) %collective-permute-start.14) | collective-permute-done | bytes 524320 | tf_op jit(solution)/shard_map/ppermute | solution.py:50
  176.3 11.6 %collective-permute-done.15 = bf16[128,2048]{1,0:T(8,128)(2,1)S(1)} collective-permute-done((bf16[128,2048]{1,0:T(8,128)(2,1)S(1)}, bf16[128,2048]{1,0:T(8,128)(2,1)S(1)}, u32[]{:S(2)}, u32[]{:S(2)}) %collective-permute-start.15) | collective-permute-done | bytes 524320 | tf_op jit(solution)/shard_map/ppermute | solution.py:50
  199.3 9.6 %collective-permute-done.19 = bf16[128,2048]{1,0:T(8,128)(2,1)S(1)} collective-permute-done((bf16[128,2048]{1,0:T(8,128)(2,1)S(1)}, bf16[128,2048]{1,0:T(8,128)(2,1)S(1)}, u32[]{:S(2)}, u32[]{:S(2)}) %collective-permute-start.19) | collective-permute-done | bytes 524320 | tf_op jit(solution)/shard_map/ppermute | solution.py:50
  227.4 10.5 %feed.2 = (bf16[1024,2048]{1,0:T(8,128)(2,1)}, bf16[1024,896]{1,0:T(8,128)(2,1)S(1)}, f32[1024,896]{1,0:T(8,128)}, bf16[1024,2048]{1,0:T(8,128)(2,1)}) custom-call(bf16[1024,2048]{1,0:T(8,128)(2,1)} %copy-done.1, f32[2,2048]{1,0:T(2,128)S(1)} %copy-done.42, bf16[2048,1152]{1,0:T(8,128)(2,1)} %bitcast.120, bf16[896,2048]{1,0:T(8,128)(2,1)} %wc.5), custom_call_target="tpu_custom_call" | custom-call | flops 8000000000 | bytes 1 | tf_op jit(solution)/shard_map/feed/pallas_call | solution.py:780
  240.8 5.9 collective-permute-done.27
  249.7 9.4 %collective-permute-done.28 = bf16[128,2048]{1,0:T(8,128)(2,1)S(1)} collective-permute-done((bf16[128,2048]{1,0:T(8,128)(2,1)S(1)}, bf16[128,2048]{1,0:T(8,128)(2,1)S(1)}, u32[]{:S(2)}, u32[]{:S(2)}) %collective-permute-start.28) | collective-permute-done | bytes 524320 | tf_op jit(solution)/shard_map/ppermute | solution.py:50
  262.9 11.0 %feed.3 = (bf16[1024,2048]{1,0:T(8,128)(2,1)}, bf16[1024,896]{1,0:T(8,128)(2,1)S(1)}, f32[1024,896]{1,0:T(8,128)}, bf16[1024,2048]{1,0:T(8,128)(2,1)}) custom-call(bf16[1024,2048]{1,0:T(8,128)(2,1)} %copy-done.1, f32[2,2048]{1,0:T(2,128)S(1)} %copy-done.42, ...), custom_call_target="tpu_custom_call", output_to_operand_aliasing={{0}: (4, {}), {1}: (5, {}), {2}: (6, {}), {3}: (7, {})} | custom-call | flops 8000000000 | bytes 1 | tf_op jit(solution)/shard_map/feed/pallas_call | solution.py:780
  278.1 5.5 convolution_convert_fusion.2
  294.1 11.3 %collective-permute-done.32 = bf16[128,2048]{1,0:T(8,128)(2,1)S(1)} collective-permute-done((bf16[128,2048]{1,0:T(8,128)(2,1)S(1)}, bf16[128,2048]{1,0:T(8,128)(2,1)S(1)}, u32[]{:S(2)}, u32[]{:S(2)}) %collective-permute-start.32) | collective-permute-done | bytes 524320 | tf_op jit(solution)/shard_map/ppermute | solution.py:50
  305.4 11.5 %collective-permute-done.33 = bf16[128,2048]{1,0:T(8,128)(2,1)S(1)} collective-permute-done((bf16[128,2048]{1,0:T(8,128)(2,1)S(1)}, bf16[128,2048]{1,0:T(8,128)(2,1)S(1)}, u32[]{:S(2)}, u32[]{:S(2)}) %collective-permute-start.33) | collective-permute-done | bytes 524320 | tf_op jit(solution)/shard_map/ppermute | solution.py:50
  331.2 19.5 %feed_back.1 = (bf16[1024,896]{1,0:T(8,128)(2,1)}, bf16[1024,2048]{1,0:T(8,128)(2,1)}, f32[2,2048]{1,0:T(2,128)S(1)}) custom-call(bf16[1024,2048]{1,0:T(8,128)(2,1)} %copy-done.55, bf16[1024,2048]{1,0:T(8,128)(2,1)} %copy-done.1, f32[1024,896]{1,0:T(8,128)} %get-tuple-element.174.fac, bf16[1024,256]{1,0:T(8,128)(2,1)S(1)} %pad_maximum_fusion.12.dgate, ...), custom_call_target="tpu_custom_call" | custom-call | flops 1 | bytes 1 | tf_op jit(solution)/shard_map/feed_back/pallas_call | solution.py:842
  350.7 6.5 convolution_convert_fusion.1.refs_0_
  372.1 11.3 %collective-permute-done.40 = bf16[128,2048]{1,0:T(8,128)(2,1)S(1)} collective-permute-done((bf16[128,2048]{1,0:T(8,128)(2,1)S(1)}, bf16[128,2048]{1,0:T(8,128)(2,1)S(1)}, u32[]{:S(2)}, u32[]{:S(2)}) %collective-permute-start.40) | collective-permute-done | bytes 524320 | tf_op jit(solution)/shard_map/ppermute | solution.py:50
  383.4 11.2 %collective-permute-done.41 = bf16[128,2048]{1,0:T(8,128)(2,1)S(1)} collective-permute-done((bf16[128,2048]{1,0:T(8,128)(2,1)S(1)}, bf16[128,2048]{1,0:T(8,128)(2,1)S(1)}, u32[]{:S(2)}, u32[]{:S(2)}) %collective-permute-start.41) | collective-permute-done | bytes 524320 | tf_op jit(solution)/shard_map/ppermute | solution.py:50
  410.5 8.2 collective-permute-done.45
  434.6 30.2 %decay_mix_back.1 = (bf16[1024,256]{1,0:T(8,128)(2,1)S(1)}, bf16[1024,256]{1,0:T(8,128)(2,1)S(1)}, bf16[1024,256]{1,0:T(8,128)(2,1)S(1)}, bf16[1024,256]{1,0:T(8...) custom-call(f32[1024,256]{1,0:T(8,128)S(1)} %copy-done.15, f32[1024,256]{1,0:T(8,128)S(1)} %copy-done.13, ...), custom_call_target="tpu_custom_call" | custom-call | flops 1 | bytes 1 | tf_op jit(solution)/shard_map/decay_mix_back/pallas_call | solution.py:730
  492.0 48.7 %token_shift_back.1 = (bf16[1024,2048]{1,0:T(8,128)(2,1)}, f32[8,2048]{1,0:T(8,128)}, f32[160,2048]{1,0:T(8,128)}, f32[160,2048]{1,0:T(8,128)}, f32[64,2048]{1,0:T(8,128)}) custom-call(bf16[1024,2048]{1,0:T(8,128)(2,1)} %constant_dynamic-update-slice_fusion.2.tok, f32[1024,160]{1,0:T(8,128)} %copy-done.25, f32[1024,64]{1,0:T(8,128)} %copy-done.5, ...), custom_call_target="tpu_custom_call" | custom-call | flops 1 | bytes 1 | tf_op jit(solution)/shard_map/token_shift_back/pallas_call | solution.py:511
  540.7 6.0 reduce-scatter.9.cloned.1.call-done
  582.6 11.6 %collective-permute-done.60 = bf16[464,256]{1,0:T(8,128)(2,1)S(1)} collective-permute-done((bf16[464,256]{1,0:T(8,128)(2,1)S(1)}, bf16[464,256]{1,0:T(8,128)(2,1)S(1)}, u32[]{:S(2)}, u32[]{:S(2)}) %collective-permute-start.60) | collective-permute-done | bytes 237600 | tf_op jit(solution)/shard_map/ppermute | solution.py:310
  594.2 15.0 %collective-permute-done.61 = bf16[464,256]{1,0:T(8,128)(2,1)S(1)} collective-permute-done((bf16[464,256]{1,0:T(8,128)(2,1)S(1)}, bf16[464,256]{1,0:T(8,128)(2,1)S(1)}, u32[]{:S(2)}, u32[]{:S(2)}) %collective-permute-start.61) | collective-permute-done | bytes 237600 | tf_op jit(solution)/shard_map/ppermute | solution.py:310
  615.5 10.2 %collective-permute-done.64 = bf16[464,512]{1,0:T(8,128)(2,1)S(1)} collective-permute-done((bf16[464,512]{1,0:T(8,128)(2,1)S(1)}, bf16[464,512]{1,0:T(8,128)(2,1)S(1)}, u32[]{:S(2)}, u32[]{:S(2)}) %collective-permute-start.64) | collective-permute-done | bytes 475168 | tf_op jit(solution)/shard_map/ppermute | solution.py:50
  625.7 10.3 %collective-permute-done.65 = bf16[464,512]{1,0:T(8,128)(2,1)S(1)} collective-permute-done((bf16[464,512]{1,0:T(8,128)(2,1)S(1)}, bf16[464,512]{1,0:T(8,128)(2,1)S(1)}, u32[]{:S(2)}, u32[]{:S(2)}) %collective-permute-start.65) | collective-permute-done | bytes 475168 | tf_op jit(solution)/shard_map/ppermute | solution.py:50
  647.7 6.4 collective-permute-done.70.refs_3_.refs_7_
  671.8 10.2 %widened.5 = f32[896,2048]{1,0:T(8,128)} custom-call(bf16[896,2048]{1,0:T(8,128)(2,1)S(1)} %copy-done.16), custom_call_target="tpu_custom_call" | custom-call | flops 1 | bytes 1 | tf_op jit(solution)/shard_map/widened/pallas_call | solution.py:294
  683.1 11.6 %collective-permute-done.54 = bf16[128,2048]{1,0:T(8,128)(2,1)S(1)} collective-permute-done((bf16[128,2048]{1,0:T(8,128)(2,1)S(1)}, bf16[128,2048]{1,0:T(8,128)(2,1)S(1)}, u32[]{:S(2)}, u32[]{:S(2)}) %collective-permute-start.54) | collective-permute-done | bytes 524320 | tf_op jit(solution)/shard_map/ppermute | solution.py:50
  701.5 34.0 %all-gather.11.cloned.1.call-done.refs_0_ = bf16[256,9216]{1,0:T(8,128)(2,1)} async-done(((bf16[64,9216]{1,0:T(8,128)(2,1)}), bf16[256,9216]{1,0:T(8,128)(2,1)}) %all-gather.11.cloned.1.call-update) | async-done | bytes 4718608 | tf_op jit(solution)/shard_map/all_gather | solution.py:252
  742.4 91.8 %all-gather.9.cloned.1.call-done.refs_0_ = bf16[256,10240]{1,0:T(8,128)(2,1)} async-done(((bf16[64,10240]{1,0:T(8,128)(2,1)}), bf16[256,10240]{1,0:T(8,128)(2,1)}) %all-gather.9.cloned.1.call-update) | async-done | bytes 5242896 | tf_op jit(solution)/shard_map/all_gather | solution.py:252
  (521 shorter events, 323.1 us)
Async XLA Ops:
  7.2 147.1 %all-gather.5.cloned.1.call-start = ((), (), s32[]{:S(2)}) async-start(), calls=%async_computation.4 | async-start | bytes 5898240 | tf_op jit(solution)/shard_map/all_gather | solution.py:926
  15.9 19.7 %collective-permute-start.4 = (bf16[4,256,1024]{2,1,0:T(8,128)(2,1)}, bf16[4,256,1024]{2,1,0:T(8,128)(2,1)}, u32[]{:S(2)}, u32[]{:S(2)}) collective-permute-start(bf16[4,256,1024]{2,1,0:T(8,128)(2,1)} %get-tuple-element.127), channel_id=1, source_target_pairs={{0,4},{4,0},{8,12},{12,8},{16,20},{20,16},{24,28},{28,24},{1,5},{5... | collective-permute-start | bytes 6291464 | tf_op jit(solution)/shard_map/ppermute | solution.py:50
  29.5 14.9 %collective-permute-start.3 = (bf16[128,2048]{1,0:T(8,128)(2,1)S(1)}, bf16[128,2048]{1,0:T(8,128)(2,1)S(1)}, u32[]{:S(2)}, u32[]{:S(2)}) collective-permute-start(bf16[128,2048]{1,0:T(8,128)(2,1)S(1)} %pad_maximum_fusion.6), channel_id=1, source_target_pairs={{0,8},{4,12},{8,0},{12,4},{16,24},{20,28},{24,16},{28,20},{1,9},{5... | collective-permute-start | bytes 1572872 | tf_op jit(solution)/shard_map/ppermute | solution.py:50
  33.7 17.0 %collective-permute-start.6 = (bf16[2,64,1152]{2,1,0:T(8,128)(2,1)S(1)}, bf16[2,64,1152]{2,1,0:T(8,128)(2,1)S(1)}, u32[]{:S(2)}, u32[]{:S(2)}) collective-permute-start(bf16[2,64,1152]{2,1,0:T(8,128)(2,1)S(1)} %pad_maximum_fusion.15), channel_id=1, source_target_pairs={{0,8},{4,12},{8,0},{12,4},{16,24},{20,28},{24,16},{28,20},{1,9},{5... | collective-permute-start | bytes 884744 | tf_op jit(solution)/shard_map/ppermute | solution.py:50
  34.4 22.4 %collective-permute-start.7 = (bf16[2,64,1152]{2,1,0:T(8,128)(2,1)S(1)}, bf16[2,64,1152]{2,1,0:T(8,128)(2,1)S(1)}, u32[]{:S(2)}, u32[]{:S(2)}) collective-permute-start(bf16[2,64,1152]{2,1,0:T(8,128)(2,1)S(1)} %pad_maximum_fusion.16), channel_id=1, source_target_pairs={{0,16},{4,20},{8,24},{12,28},{16,0},{20,4},{24,8},{28,12},{1,17},{... | collective-permute-start | bytes 884744 | tf_op jit(solution)/shard_map/ppermute | solution.py:50
  35.6 21.2 %collective-permute-start.8 = (bf16[2,64,1152]{2,1,0:T(8,128)(2,1)S(1)}, bf16[2,64,1152]{2,1,0:T(8,128)(2,1)S(1)}, u32[]{:S(2)}, u32[]{:S(2)}) collective-permute-start(bf16[2,64,1152]{2,1,0:T(8,128)(2,1)S(1)} %pad_maximum_fusion.17), channel_id=1, source_target_pairs={{0,24},{4,28},{8,16},{12,20},{16,8},{20,12},{24,0},{28,4},{1,25},{... | collective-permute-start | bytes 884744 | tf_op jit(solution)/shard_map/ppermute | solution.py:50
  64.2 297.5 %reduce-scatter.5.cloned.1.call-start = ((), (), s32[]{:S(2)}) async-start(), calls=%async_computation.5 | async-start | bytes 4587520 | tf_op jit(solution)/shard_map/reduce_scatter | solution.py:959
  68.4 34.6 %collective-permute-start.10 = (bf16[2,256,1024]{2,1,0:T(8,128)(2,1)}, bf16[2,256,1024]{2,1,0:T(8,128)(2,1)S(1)}, u32[]{:S(2)}, u32[]{:S(2)}) collective-permute-start(bf16[2,256,1024]{2,1,0:T(8,128)(2,1)} %get-tuple-element.140), channel_id=1, source_target_pairs={{0,8},{4,12},{8,0},{12,4},{16,24},{20,28},{24,16},{28,20},{1,9},{5... | collective-permute-start | bytes 3145736 | tf_op jit(solution)/shard_map/ppermute | solution.py:50
  69.5 46.6 %collective-permute-start.11 = (bf16[2,256,1024]{2,1,0:T(8,128)(2,1)}, bf16[2,256,1024]{2,1,0:T(8,128)(2,1)S(1)}, u32[]{:S(2)}, u32[]{:S(2)}) collective-permute-start(bf16[2,256,1024]{2,1,0:T(8,128)(2,1)} %get-tuple-element.141), channel_id=1, source_target_pairs={{0,16},{4,20},{8,24},{12,28},{16,0},{20,4},{24,8},{28,12},{1,17},{... | collective-permute-start | bytes 3145736 | tf_op jit(solution)/shard_map/ppermute | solution.py:50
  70.4 47.2 %collective-permute-start.12 = (bf16[2,256,1024]{2,1,0:T(8,128)(2,1)}, bf16[2,256,1024]{2,1,0:T(8,128)(2,1)S(1)}, u32[]{:S(2)}, u32[]{:S(2)}) collective-permute-start(bf16[2,256,1024]{2,1,0:T(8,128)(2,1)} %pad_maximum_fusion.4), channel_id=1, source_target_pairs={{0,24},{4,28},{8,16},{12,20},{16,8},{20,12},{24,0},{28,4},{1,25},{... | collective-permute-start | bytes 3145736 | tf_op jit(solution)/shard_map/ppermute | solution.py:50
  163.0 24.9 %collective-permute-start.15 = (bf16[128,2048]{1,0:T(8,128)(2,1)S(1)}, bf16[128,2048]{1,0:T(8,128)(2,1)S(1)}, u32[]{:S(2)}, u32[]{:S(2)}) collective-permute-start(bf16[128,2048]{1,0:T(8,128)(2,1)S(1)} %get-tuple-element.260), channel_id=1, source_target_pairs={{0,16},{4,20},{8,24},{12,28},{16,0},{20,4},{24,8},{28,12},{1,17},{... | collective-permute-start | bytes 1572872 | tf_op jit(solution)/shard_map/ppermute | solution.py:50
  164.5 23.5 %collective-permute-start.16 = (bf16[128,2048]{1,0:T(8,128)(2,1)S(1)}, bf16[128,2048]{1,0:T(8,128)(2,1)S(1)}, u32[]{:S(2)}, u32[]{:S(2)}) collective-permute-start(bf16[128,2048]{1,0:T(8,128)(2,1)S(1)} %get-tuple-element.259), channel_id=1, source_target_pairs={{0,24},{4,28},{8,16},{12,20},{16,8},{20,12},{24,0},{28,4},{1,25},{... | collective-permute-start | bytes 1572872 | tf_op jit(solution)/shard_map/ppermute | solution.py:50
  283.6 185.3 %reduce-scatter.7.cloned.1.call-start = ((), (), s32[]{:S(2)}) async-start(), calls=%async_computation.6 | async-start | bytes 5898240 | tf_op jit(solution)/shard_map/reduce_scatter | solution.py:248
  291.8 25.1 %collective-permute-start.33 = (bf16[128,2048]{1,0:T(8,128)(2,1)S(1)}, bf16[128,2048]{1,0:T(8,128)(2,1)S(1)}, u32[]{:S(2)}, u32[]{:S(2)}) collective-permute-start(bf16[128,2048]{1,0:T(8,128)(2,1)S(1)} %get-tuple-element.257), channel_id=1, source_target_pairs={{0,16},{4,20},{8,24},{12,28},{16,0},{20,4},{24,8},{28,12},{1,17},{... | collective-permute-start | bytes 1572872 | tf_op jit(solution)/shard_map/ppermute | solution.py:50
  292.2 24.7 %collective-permute-start.34 = (bf16[128,2048]{1,0:T(8,128)(2,1)S(1)}, bf16[128,2048]{1,0:T(8,128)(2,1)S(1)}, u32[]{:S(2)}, u32[]{:S(2)}) collective-permute-start(bf16[128,2048]{1,0:T(8,128)(2,1)S(1)} %get-tuple-element.256), channel_id=1, source_target_pairs={{0,24},{4,28},{8,16},{12,20},{16,8},{20,12},{24,0},{28,4},{1,25},{... | collective-permute-start | bytes 1572872 | tf_op jit(solution)/shard_map/ppermute | solution.py:50
  361.7 179.1 %all-gather.7.cloned.1.call-start = ((), (), s32[]{:S(2)}) async-start(), calls=%async_computation.7 | async-start | bytes 4587520 | tf_op jit(solution)/shard_map/all_gather | solution.py:252
  369.6 24.9 %collective-permute-start.41 = (bf16[128,2048]{1,0:T(8,128)(2,1)S(1)}, bf16[128,2048]{1,0:T(8,128)(2,1)S(1)}, u32[]{:S(2)}, u32[]{:S(2)}) collective-permute-start(bf16[128,2048]{1,0:T(8,128)(2,1)S(1)} %get-tuple-element.254), channel_id=1, source_target_pairs={{0,16},{4,20},{8,24},{12,28},{16,0},{20,4},{24,8},{28,12},{1,17},{... | collective-permute-start | bytes 1572872 | tf_op jit(solution)/shard_map/ppermute | solution.py:50
  370.2 24.3 %collective-permute-start.42 = (bf16[128,2048]{1,0:T(8,128)(2,1)S(1)}, bf16[128,2048]{1,0:T(8,128)(2,1)S(1)}, u32[]{:S(2)}, u32[]{:S(2)}) collective-permute-start(bf16[128,2048]{1,0:T(8,128)(2,1)S(1)} %get-tuple-element.253), channel_id=1, source_target_pairs={{0,24},{4,28},{8,16},{12,20},{16,8},{20,12},{24,0},{28,4},{1,25},{... | collective-permute-start | bytes 1572872 | tf_op jit(solution)/shard_map/ppermute | solution.py:50
  399.3 147.4 %reduce-scatter.9.cloned.1.call-start = ((), (), s32[]{:S(2)}) async-start(), calls=%async_computation.8 | async-start | bytes 1310720 | tf_op jit(solution)/shard_map/reduce_scatter | solution.py:248
  430.6 209.1 %reduce-scatter.11.cloned.1.call-start = ((), (), s32[]{:S(2)}) async-start(), calls=%async_computation.9 | async-start | bytes 5242880 | tf_op jit(solution)/shard_map/reduce_scatter | solution.py:248
  481.9 253.6 %all-gather.11.cloned.1.call-start = ((), (), s32[]{:S(2)}) async-start(), calls=%async_computation.11 | async-start | bytes 5898240 | tf_op jit(solution)/shard_map/all_gather | solution.py:252
  487.0 59.8 %collective-permute-start.51 = (bf16[2,64,1152]{2,1,0:T(8,128)(2,1)}, bf16[2,64,1152]{2,1,0:T(8,128)(2,1)S(1)}, u32[]{:S(2)}, u32[]{:S(2)}) collective-permute-start(bf16[2,64,1152]{2,1,0:T(8,128)(2,1)} %pad_maximum_fusion.20), channel_id=1, source_target_pairs={{0,24},{4,28},{8,16},{12,20},{16,8},{20,12},{24,0},{28,4},{1,25},{... | collective-permute-start | bytes 884744 | tf_op jit(solution)/shard_map/ppermute | solution.py:50
  489.9 56.9 %collective-permute-start.50 = (bf16[2,64,1152]{2,1,0:T(8,128)(2,1)}, bf16[2,64,1152]{2,1,0:T(8,128)(2,1)S(1)}, u32[]{:S(2)}, u32[]{:S(2)}) collective-permute-start(bf16[2,64,1152]{2,1,0:T(8,128)(2,1)} %pad_maximum_fusion.19), channel_id=1, source_target_pairs={{0,16},{4,20},{8,24},{12,28},{16,0},{20,4},{24,8},{28,12},{1,17},{... | collective-permute-start | bytes 884744 | tf_op jit(solution)/shard_map/ppermute | solution.py:50
  491.0 55.8 %collective-permute-start.49 = (bf16[2,64,1152]{2,1,0:T(8,128)(2,1)}, bf16[2,64,1152]{2,1,0:T(8,128)(2,1)S(1)}, u32[]{:S(2)}, u32[]{:S(2)}) collective-permute-start(bf16[2,64,1152]{2,1,0:T(8,128)(2,1)} %pad_maximum_fusion.18), channel_id=1, source_target_pairs={{0,8},{4,12},{8,0},{12,4},{16,24},{20,28},{24,16},{28,20},{1,9},{5... | collective-permute-start | bytes 884744 | tf_op jit(solution)/shard_map/ppermute | solution.py:50
  549.1 285.0 %all-gather.9.cloned.1.call-start = ((), (), s32[]{:S(2)}) async-start(), calls=%async_computation.10 | async-start | bytes 6553600 | tf_op jit(solution)/shard_map/all_gather | solution.py:252
  578.5 15.8 %collective-permute-start.60 = (bf16[464,256]{1,0:T(8,128)(2,1)S(1)}, bf16[464,256]{1,0:T(8,128)(2,1)S(1)}, u32[]{:S(2)}, u32[]{:S(2)}) collective-permute-start(bf16[464,256]{1,0:T(8,128)(2,1)S(1)} %pad_maximum_fusion.24), channel_id=1, source_target_pairs={{0,1},{1,2},{2,3},{3,0},{4,5},{5,6},{6,7},{7,4},{8,9},{9,10},{10,1... | collective-permute-start | bytes 712712 | tf_op jit(solution)/shard_map/ppermute | solution.py:310
  578.5 30.7 %collective-permute-start.61 = (bf16[464,256]{1,0:T(8,128)(2,1)S(1)}, bf16[464,256]{1,0:T(8,128)(2,1)S(1)}, u32[]{:S(2)}, u32[]{:S(2)}) collective-permute-start(bf16[464,256]{1,0:T(8,128)(2,1)S(1)} %pad_maximum_fusion.24), channel_id=1, source_target_pairs={{0,2},{1,3},{2,0},{3,1},{4,6},{5,7},{6,4},{7,5},{8,10},{9,11},{10,... | collective-permute-start | bytes 712712 | tf_op jit(solution)/shard_map/ppermute | solution.py:310
  580.1 29.7 %collective-permute-start.62 = (bf16[464,256]{1,0:T(8,128)(2,1)S(1)}, bf16[464,256]{1,0:T(8,128)(2,1)S(1)}, u32[]{:S(2)}, u32[]{:S(2)}) collective-permute-start(bf16[464,256]{1,0:T(8,128)(2,1)S(1)} %pad_maximum_fusion.24), channel_id=1, source_target_pairs={{0,3},{1,0},{2,1},{3,2},{4,7},{5,4},{6,5},{7,6},{8,11},{9,8},{10,9... | collective-permute-start | bytes 712712 | tf_op jit(solution)/shard_map/ppermute | solution.py:310
  613.2 22.8 %collective-permute-start.65 = (bf16[464,512]{1,0:T(8,128)(2,1)S(1)}, bf16[464,512]{1,0:T(8,128)(2,1)S(1)}, u32[]{:S(2)}, u32[]{:S(2)}) collective-permute-start(bf16[464,512]{1,0:T(8,128)(2,1)S(1)} %get-tuple-element.235), channel_id=1, source_target_pairs={{0,16},{4,20},{8,24},{12,28},{16,0},{20,4},{24,8},{28,12},{1,17},{... | collective-permute-start | bytes 1425416 | tf_op jit(solution)/shard_map/ppermute | solution.py:50
  614.4 21.7 %collective-permute-start.66 = (bf16[464,512]{1,0:T(8,128)(2,1)S(1)}, bf16[464,512]{1,0:T(8,128)(2,1)S(1)}, u32[]{:S(2)}, u32[]{:S(2)}) collective-permute-start(bf16[464,512]{1,0:T(8,128)(2,1)S(1)} %get-tuple-element.235), channel_id=1, source_target_pairs={{0,24},{4,28},{8,16},{12,20},{16,8},{20,12},{24,0},{28,4},{1,25},{... | collective-permute-start | bytes 1425416 | tf_op jit(solution)/shard_map/ppermute | solution.py:50
  669.8 24.9 %collective-permute-start.54 = (bf16[128,2048]{1,0:T(8,128)(2,1)S(1)}, bf16[128,2048]{1,0:T(8,128)(2,1)S(1)}, u32[]{:S(2)}, u32[]{:S(2)}) collective-permute-start(bf16[128,2048]{1,0:T(8,128)(2,1)S(1)} %get-tuple-element.251), channel_id=1, source_target_pairs={{0,16},{4,20},{8,24},{12,28},{16,0},{20,4},{24,8},{28,12},{1,17},{... | collective-permute-start | bytes 1572872 | tf_op jit(solution)/shard_map/ppermute | solution.py:50
  670.7 24.0 %collective-permute-start.55 = (bf16[128,2048]{1,0:T(8,128)(2,1)S(1)}, bf16[128,2048]{1,0:T(8,128)(2,1)S(1)}, u32[]{:S(2)}, u32[]{:S(2)}) collective-permute-start(bf16[128,2048]{1,0:T(8,128)(2,1)S(1)} %get-tuple-element.250), channel_id=1, source_target_pairs={{0,24},{4,28},{8,16},{12,20},{16,8},{20,12},{24,0},{28,4},{1,25},{... | collective-permute-start | bytes 1572872 | tf_op jit(solution)/shard_map/ppermute | solution.py:50
  (137 other events, 1226.6 us)
Sparse Core Ops, SparseCore 0:
  64.3 89.8 all-gather.4
  283.7 65.6 reduce-scatter.4
  361.8 82.3 reduce-scatter.6
  445.6 72.6 all-gather.6
  521.0 25.7 reduce-scatter.8
  549.0 90.6 reduce-scatter.10
  641.9 93.5 all-gather.10
  737.6 96.5 all-gather.8

commit v3 on v2

--- a/solution.py
+++ b/solution.py
@@ -63,51 +63,92 @@
     )
 
 
-def gather_tokens(v, *later):
+def gather_tokens(v, beside=tuple):
     if not paired():
-        return (lax.all_gather(v, "fsdp", axis=0, tiled=True), *later)
+        return lax.all_gather(v, "fsdp", axis=0, tiled=True), beside()
     r = v.shape[0] // 2
     a, b = v[:r], v[r:]
     a1, b1 = swap(a, 2), swap(b, 4)
     a2 = swap(jnp.concatenate([a, a1], axis=0), 4)
     b2 = swap(jnp.concatenate([b, b1], axis=0), 2)
-    if later:
-        a2, b2, *later = hold(a2, b2, *later)
+    held = beside()
+    if held:
+        a2, b2, *held = hold(a2, b2, *held)
     near = jnp.concatenate([v, a1, b2[:r], a2[:r], b1, a2[r:], b2[r:]], axis=0)
-    return (jnp.concatenate([near, swap(near, 1)], axis=0), *later)
-
-
-def scatter_tokens(v):
+    return jnp.concatenate([near, swap(near, 1)], axis=0), held
+
+
+def scatter_tokens(near, far):
     if not paired():
+        v = jnp.concatenate([near, far], axis=0)
         return lax.psum_scatter(v, "fsdp", scatter_dimension=0, tiled=True).astype(F32)
-    r = v.shape[0] // 8
-    got = swap(v[4 * r :], 1)
-    pair = lambda q: v[q * r : (q + 1) * r].astype(F32) + got[q * r : (q + 1) * r].astype(F32)
+    r = near.shape[0] // 4
+    got = swap(far, 1)
+    pair = lambda q: near[q * r : (q + 1) * r].astype(F32) + got[q * r : (q + 1) * r].astype(F32)
     far = [swap(pair(q).astype(BF), 2 * q) for q in (1, 2, 3)]
     return pair(0) + (far[0].astype(F32) + far[1].astype(F32)) + far[2].astype(F32)
 
 
-def chip_exchange(take, put, out):
-    chip, _ = place()
-    out = put(out, chip, take(chip))
-    for q in (1, 2, 3):
-        out = put(out, chip ^ q, swap(take(chip ^ q), 2 * q))
-    return out
-
-
-def home_features(v, beside):
+def home_features(v):
     if not paired():
-        return lax.all_to_all(v, "fsdp", split_axis=0, concat_axis=1, tiled=True), beside()
+        return lax.all_to_all(v, "fsdp", split_axis=0, concat_axis=1, tiled=True)
     chip, core = place()
     r, c = v.shape[0] // 8, v.shape[1]
     both = by_core(core, v[: 4 * r], swap(v[4 * r :], 1), 1)
-    pieces = [both[:r]] + [swap(both[q * r : (q + 1) * r], 2 * q) for q in (1, 2, 3)]
-    held = hold(*pieces, *beside())
-    pieces, others = held[:4], held[4:]
     out = jnp.zeros((r, 8 * c), v.dtype)
     for q in range(4):
-        out = lax.dynamic_update_slice_in_dim(out, pieces[q], (chip ^ q) * (2 * c), 1)
-    return out, others
+        piece = both[q * r : (q + 1) * r]
+        piece = piece if q == 0 else swap(piece, 2 * q)
+        out = lax.dynamic_update_slice_in_dim(out, piece, (chip ^ q) * (2 * c), 1)
+    return out
+
+
+ORDER = (0, 2, 4, 6, 1, 3, 5, 7)
+
+
+def line_up_kernel(order, near, far, out):
+    rows = near.shape[1] // 8
+    for i, m in enumerate(ORDER):
+
+        @pl.when(pl.program_id(0) == i)
+        def _():
+            source = near if i < 4 else far
+            for q, own in enumerate(ORDER):
+                p = ORDER.index(m ^ own)
+                out[q * rows : (q + 1) * rows, :] = source[0, p * rows : (p + 1) * rows, :]
+
+
+def gather_features_of_tokens(v, beside):
+    first, second = beside
+    if not paired():
+        return lax.all_gather(v, "fsdp", axis=1, tiled=True), second(*first())
+    g, c = v.shape
+    r = g // 2
+    a, b = v[:r], v[r:]
+    a1, b1 = swap(a, 2), swap(b, 4)
+    a1, b1, *held = hold(a1, b1, *first())
+    a2 = swap(jnp.concatenate([a, a1], axis=0), 4)
+    b2 = swap(jnp.concatenate([b, b1], axis=0), 2)
+    a2, b2, *held = hold(a2, b2, *second(*held))
+    near = jnp.concatenate([v, a1, b2[:r], a2[:r], b1, a2[r:], b2[r:]], axis=0).reshape(4, g, c)
+    far = swap(near, 1)
+    lined = pl.pallas_call(
+        line_up_kernel,
+        grid_spec=pltpu.PrefetchScalarGridSpec(
+            num_scalar_prefetch=1,
+            grid=(8,),
+            in_specs=[
+                pl.BlockSpec((1, g, c), lambda i, o: (jnp.minimum(i, 3), 0, 0)),
+                pl.BlockSpec((1, g, c), lambda i, o: (jnp.maximum(i - 4, 0), 0, 0)),
+            ],
+            out_specs=pl.BlockSpec((g, c), lambda i, o: (0, o[i])),
+        ),
+        out_shape=jax.ShapeDtypeStruct((g, 8 * c), v.dtype),
+        compiler_params=pltpu.CompilerParams(vmem_limit_bytes=32 * MIB),
+        cost_estimate=SHORT,
+        name="line_up",
+    )(orders(), near, far)
+    return lined, held
 
 
 def spread_features(v):
@@ -126,7 +167,9 @@
 
 def orders():
     me = lax.axis_index("fsdp")
-    return jnp.stack([me ^ m for m in (0, 2, 4, 6, 1, 3, 5, 7)]).astype(jnp.int32)
+    if not paired():
+        return jnp.arange(lax.axis_size("fsdp"), dtype=jnp.int32)
+    return jnp.stack([me ^ m for m in ORDER]).astype(jnp.int32)
 
 
 def pack_kernel(count, order, *refs):
@@ -193,27 +236,34 @@
         *values, self.near, self.far = hold(*values, self.near, self.far)
         return values
 
-    def parcels(self):
+    def across_chips(self):
+        if paired():
+            self.got = [
+                swap(jnp.concatenate([self.near[q : q + 1], self.far[q : q + 1]], axis=0), 2 * q)
+                for q in (1, 2, 3)
+            ]
+
+    def moving(self):
+        return self.got if paired() else []
+
+    def waiting(self):
+        return [self.near, self.far] if paired() else []
+
+    def resume(self, held):
         if not paired():
-            return []
-        return [
-            jnp.concatenate([self.near[q : q + 1], self.far[q : q + 1]], axis=0) for q in (1, 2, 3)
-        ]
-
-    def got_parcels(self):
-        return self.got if paired() else []
-
-    def across_chips(self, parcels=None):
-        if paired():
-            parcels = parcels or self.parcels()
-            self.got = [swap(p, 2 * q) for q, p in zip((1, 2, 3), parcels)]
-
-    def arrived(self, *values):
+            return held
+        if hasattr(self, "got"):
+            self.got, held = list(held[:3]), held[3:]
+        else:
+            (self.near, self.far), held = held[:2], held[2:]
+        return held
+
+    def arrived(self, *values, count=3):
         if not paired():
             return values
-        *values, g1, g2, g3 = hold(*values, *self.got)
-        self.got = [g1, g2, g3]
-        return values
+        held = hold(*values, *self.got[:count])
+        self.got[:count] = held[len(values) :]
+        return held[: len(values)]
 
     def results(self):
         if not paired():
@@ -252,31 +302,57 @@
     return lax.all_gather(v, "rep", axis=0, tiled=True)
 
 
-def share_kernel(shares, *refs):
+def share_kernel(blocks, shares, rows_at_end, *refs):
     *parts, out = refs
-    at = 0
-    for p in parts:
-        rows, w = p.shape[0] // shares, p.shape[1]
-        for i in range(shares):
-            out[i, 0, :, at : at + w] = p[i * rows : (i + 1) * rows, :]
-        at += w
-
-
-def rep_scatter_cols(parts):
+    rows = out.shape[2]
+
+    def put(some):
+        at = 0
+        for p in some:
+            w = p.shape[1]
+            for i in range(shares):
+                out[i, 0, :, at : at + w] = p[i * rows : (i + 1) * rows, :]
+            at += w
+
+    if not rows_at_end:
+        put(parts)
+        return
+
+    @pl.when(pl.program_id(0) < blocks)
+    def _():
+        put(parts[:-1])
+
+    @pl.when(pl.program_id(0) >= blocks)
+    def _():
+        put(parts[-1:])
+
+
+def rep_scatter_cols(parts, last=None):
     n, z = lax.axis_size("fsdp"), lax.axis_size("rep")
-    rows = parts[0].shape[0]
-    c = sum(p.shape[1] for p in parts)
+    rows, c = parts[0].shape[0], sum(p.shape[1] for p in parts)
+    share = rows // (n * z)
+    extra = 0 if last is None else last.shape[1] // c
+    specs = [
+        pl.BlockSpec((rows // n, p.shape[1]), lambda i: (jnp.minimum(i, n - 1), 0)) for p in parts
+    ]
+    if extra:
+        specs.append(pl.BlockSpec((rows // n, c), lambda i: (0, jnp.maximum(i - n, 0))))
+        parts = [*parts, last]
     v = pl.pallas_call(
-        functools.partial(share_kernel, z),
-        grid=(n,),
-        in_specs=[pl.BlockSpec((rows // n, p.shape[1]), lambda i: (i, 0)) for p in parts],
-        out_specs=pl.BlockSpec((z, 1, rows // (n * z), c), lambda i: (0, i, 0, 0)),
-        out_shape=jax.ShapeDtypeStruct((z, n, rows // (n * z), c), parts[0].dtype),
+        functools.partial(share_kernel, n, z, extra > 0),
+        grid=(n + extra,),
+        in_specs=specs,
+        out_specs=pl.BlockSpec((z, 1, share, c), lambda i: (0, i, 0, 0)),
+        out_shape=jax.ShapeDtypeStruct((z, n + extra, share, c), parts[0].dtype),
         compiler_params=pltpu.CompilerParams(vmem_limit_bytes=32 * MIB),
         cost_estimate=SHORT,
         name="shares",
     )(*parts)
-    return rep_scatter(v.reshape(rows, c))
+    v = rep_scatter(v.reshape(z * (n + extra) * share, c))
+    if last is None:
+        return v
+    tail = v[n * share :].reshape(extra, share, c).transpose(1, 0, 2).reshape(share, extra * c)
+    return v[: n * share], tail
 
 
 def widen_kernel(*refs):
@@ -361,7 +437,7 @@
 
 
 def front_kernel(
-    ranks, tok, gain, shift, lerp, narrow, widen, fnarrow, xk, xv, xr, xg, hid, low, nh, nl, wb, fh, fl
+    ranks, order, tok, gain, shift, lerp, narrow, widen, fnarrow, xk, xv, xr, xg, hid, low, nh, nl, wb, fh, fl
 ):
     @pl.when(pl.program_id(0) == 0)
     def _():
@@ -385,37 +461,46 @@
             low[...] = jnp.tanh(mm(dh, fh[...]) + mm(dh, fl[...]) + mm(dl, fh[...]))
 
 
+def ordered_rows(seq_len, d, seqs):
+    return pl.BlockSpec((seq_len, d), lambda s, o: (o[s // seqs] * seqs + lax.rem(s, seqs), 0))
+
+
 def front(seq_len, tokens, gain, shift, lerp, narrow, widen, fnarrow):
     g, d = tokens.shape
     ranks = widen.shape[0] // 5
     fd = fnarrow.shape[0]
-    per_seq = lambda w: pl.BlockSpec((seq_len, w), lambda s: (s, 0))
+    order = orders()
+    per_seq = lambda w: pl.BlockSpec((seq_len, w), lambda s, o: (s, 0))
     return pl.pallas_call(
         functools.partial(front_kernel, ranks),
-        grid=(g // seq_len,),
-        in_specs=[per_seq(d)]
-        + [whole_block(a) for a in (gain, shift, lerp, narrow, widen, fnarrow)],
-        out_specs=[per_seq(d)] * 4 + [per_seq(5 * ranks), per_seq(fd)],
+        grid_spec=pltpu.PrefetchScalarGridSpec(
+            num_scalar_prefetch=1,
+            grid=(g // seq_len,),
+            in_specs=[ordered_rows(seq_len, d, g // seq_len // order.shape[0])]
+            + [whole_block(a) for a in (gain, shift, lerp, narrow, widen, fnarrow)],
+            out_specs=[per_seq(d)] * 4 + [per_seq(5 * ranks), per_seq(fd)],
+            scratch_shapes=[
+                pltpu.VMEM((d, 5 * ranks), BF),
+                pltpu.VMEM((d, 5 * ranks), BF),
+                pltpu.VMEM((5 * ranks, d), BF),
+                pltpu.VMEM((d, fd), BF),
+                pltpu.VMEM((d, fd), BF),
+            ],
+        ),
         out_shape=[jax.ShapeDtypeStruct((g, d), BF)] * 4
         + [
             jax.ShapeDtypeStruct((g, 5 * ranks), F32),
             jax.ShapeDtypeStruct((g, fd), F32),
         ],
-        scratch_shapes=[
-            pltpu.VMEM((d, 5 * ranks), BF),
-            pltpu.VMEM((d, 5 * ranks), BF),
-            pltpu.VMEM((5 * ranks, d), BF),
-            pltpu.VMEM((d, fd), BF),
-            pltpu.VMEM((d, fd), BF),
-        ],
         compiler_params=pltpu.CompilerParams(vmem_limit_bytes=48 * MIB),
-        cost_estimate=lasts(22),
+        cost_estimate=SHORT,
         name="token_shift",
-    )(tokens, gain, shift, lerp, narrow, widen, fnarrow)
+    )(order, tokens, gain, shift, lerp, narrow, widen, fnarrow)
 
 
 def back_kernel(
     ranks,
+    order,
     tok,
     hid,
     low,
@@ -506,16 +591,30 @@
     gain, shift, lerp, narrow, widen, fnarrow, fwiden = params
     ranks = widen.shape[0] // 5
     fd = low.shape[1]
-    per_seq = lambda w: pl.BlockSpec((seq_len, w), lambda s: (s, 0))
-    kept = lambda r: pl.BlockSpec((r, d), lambda s: (0, 0))
+    order = orders()
+    per_seq = lambda w: pl.BlockSpec((seq_len, w), lambda s, o: (s, 0))
+    kept = lambda r: pl.BlockSpec((r, d), lambda s, o: (0, 0))
     return pl.pallas_call(
         functools.partial(back_kernel, ranks),
-        grid=(g // seq_len,),
-        in_specs=[per_seq(d), per_seq(5 * ranks), per_seq(fd)]
-        + [per_seq(c)] * 5
-        + [whole_block(a) for a in params]
-        + [whole_block(a) for a in weights],
-        out_specs=[per_seq(d), kept(8), kept(5 * ranks), kept(5 * ranks), kept(fd)],
+        grid_spec=pltpu.PrefetchScalarGridSpec(
+            num_scalar_prefetch=1,
+            grid=(g // seq_len,),
+            in_specs=[
+                ordered_rows(seq_len, d, g // seq_len // order.shape[0]),
+                per_seq(5 * ranks),
+                per_seq(fd),
+            ]
+            + [per_seq(c)] * 5
+            + [whole_block(a) for a in params]
+            + [whole_block(a) for a in weights],
+            out_specs=[per_seq(d), kept(8), kept(5 * ranks), kept(5 * ranks), kept(fd)],
+            scratch_shapes=[
+                pltpu.VMEM((5 * ranks, d), BF),
+                pltpu.VMEM((5 * ranks, d), BF),
+                pltpu.VMEM((fd, d), BF),
+                pltpu.VMEM((fd, c), BF),
+            ],
+        ),
         out_shape=[
             jax.ShapeDtypeStruct((g, d), BF),
             jax.ShapeDtypeStruct((8, d), F32),
@@ -523,16 +622,10 @@
             jax.ShapeDtypeStruct((5 * ranks, d), F32),
             jax.ShapeDtypeStruct((fd, d), F32),
         ],
-        scratch_shapes=[
-            pltpu.VMEM((5 * ranks, d), BF),
-            pltpu.VMEM((5 * ranks, d), BF),
-            pltpu.VMEM((fd, d), BF),
-            pltpu.VMEM((fd, c), BF),
-        ],
         compiler_params=pltpu.CompilerParams(vmem_limit_bytes=56 * MIB),
         cost_estimate=SHORT,
         name="token_shift_back",
-    )(tokens, hid, low, *grads, draw, *params, *weights)
+    )(order, tokens, hid, low, *grads, draw, *params, *weights)
 
 
 def level_tables(length):
@@ -601,12 +694,75 @@
     return lanes, level2, parts, scores, bonus, vb, center * rstd, rstd
 
 
-def wkv_kernel(levels, count, width, r, k, v, g, w, u, gain, bias, spans, level, out):
-    unit = mix_forward(
-        levels, count, width, r[...], k[...], v[...], w[...], u[...], spans[...], level[...]
-    )[6]
-    gate = g[...]
-    out[...] = ((unit * gain[...] + bias[...]) * (gate * jax.nn.sigmoid(gate))).astype(BF)
+def mix_kernel(levels, count, width, *refs):
+    xk, xv, xr, xg, low, wk, wv, wr, wg, we, base, fwiden, u, gain, bias, spans, level = refs[:17]
+    k_out, v_out, r_out, g_out, w_out, mixed_out, near_out, far_out = refs[17:]
+    for x, weights, out in ((xk, wk, k_out), (xv, wv, v_out), (xr, wr, r_out), (xg, wg, g_out)):
+        out[...] = mm(x[...], weights[...])
+    lh, ll = halves(low[...])
+    fh, fl = halves(fwiden[...])
+    w_out[...] = -jnp.exp(base[...] + (mm(lh, fh) + mm(lh, fl) + mm(ll, fh)))
+    lanes = count * width
+    for p in range(u.shape[1] // lanes):
+        at = slice(p * lanes, (p + 1) * lanes)
+        unit = mix_forward(
+            levels,
+            count,
+            width,
+            r_out[:, at],
+            k_out[:, at],
+            v_out[:, at],
+            w_out[:, at],
+            u[:, at],
+            spans[...],
+            level[...],
+        )[6]
+        gate = g_out[:, at]
+        mixed_out[:, at] = (
+            (unit * gain[:, at] + bias[:, at]) * (gate * jax.nn.sigmoid(gate))
+        ).astype(BF)
+    product = mm(mixed_out[...], we[...]).astype(BF)
+    step, steps = pl.program_id(0), pl.num_programs(0)
+
+    @pl.when(step < steps // 2)
+    def _():
+        near_out[...] = product
+
+    @pl.when(step >= steps // 2)
+    def _():
+        far_out[...] = product
+
+
+def mix(seq_len, xs, low, weights, we, vectors, fwiden):
+    rows, d = xs[0].shape
+    c = we.shape[0]
+    half = rows // 2
+    heads_here = c * HEADS // d
+    width = c // heads_here
+    count = 2 if heads_here % 2 == 0 else 1
+    levels, spans, level = level_tables(seq_len)
+    spans_a, level_a = jnp.asarray(spans, BF), jnp.asarray(level)
+    steps = half // seq_len
+    block = lambda w: pl.BlockSpec((seq_len, w), lambda s: (s, 0))
+    base, u, gain, bias = vectors
+    kept = (*weights, we, base, fwiden, u, gain, bias, spans_a, level_a)
+    shape = lambda w, t: jax.ShapeDtypeStruct((rows, w), t)
+    return pl.pallas_call(
+        functools.partial(mix_kernel, levels, count, width),
+        grid=(2 * steps,),
+        in_specs=[block(d)] * 4 + [block(low.shape[1])] + [whole_block(t) for t in kept],
+        out_specs=[block(c)] * 6
+        + [
+            pl.BlockSpec((seq_len, d), lambda s: (jnp.minimum(s, steps - 1), 0)),
+            pl.BlockSpec((seq_len, d), lambda s: (jnp.maximum(s - steps, 0), 0)),
+        ],
+        out_shape=[shape(c, F32)] * 5
+        + [shape(c, BF)]
+        + [jax.ShapeDtypeStruct((half, d), BF)] * 2,
+        compiler_params=pltpu.CompilerParams(vmem_limit_bytes=48 * MIB),
+        cost_estimate=lasts(20),
+        name="decay_mix",
+    )(*xs, low, *kept)
 
 
 def wkv_back_kernel(
@@ -699,9 +855,9 @@
     vec_out[3:4, :] += colsum(draw)
 
 
-def wkv(seq_len, r, k, v, g, w, u, gain, bias, dmixed=None):
+def mix_back(seq_len, r, k, v, g, w, u, gain, bias, dmixed):
     rows, c = r.shape
-    heads_here = c * HEADS // D_OF(u, c)
+    heads_here = HEADS // lax.axis_size("fsdp")
     width = c // heads_here
     count = 2 if heads_here % 2 == 0 else 1
     lanes = count * width
@@ -711,19 +867,7 @@
     cols = pl.BlockSpec((seq_len, lanes), lambda p, s: (s, p))
     vec = pl.BlockSpec((1, lanes), lambda p, s: (0, p))
     grid = (c // lanes, rows // seq_len)
-    flops = rows * c * seq_len * 2 * 16
     params = pltpu.CompilerParams(vmem_limit_bytes=40 * MIB)
-    if dmixed is None:
-        return pl.pallas_call(
-            functools.partial(wkv_kernel, levels, count, width),
-            grid=grid,
-            in_specs=[cols] * 5 + [vec] * 3 + [whole_block(spans_a), whole_block(level_a)],
-            out_specs=cols,
-            out_shape=jax.ShapeDtypeStruct((rows, c), BF),
-            compiler_params=params,
-            cost_estimate=SHORT,
-            name="decay_mix",
-        )(r, k, v, g, w, u, gain, bias, spans_a, level_a)
     spans_t = jnp.asarray(
         np.concatenate([s.T for s in spans.reshape(levels - 1, seq_len, seq_len)], 1), BF
     )
@@ -742,10 +886,6 @@
     )(r, k, v, g, w, dmixed, u, gain, bias, spans_a, spans_t, level_a)
 
 
-def D_OF(u, c):
-    return c * lax.axis_size("fsdp")
-
-
 def step_shift(length, v, back=False):
     rows = v.shape[0]
     at = lax.rem(lax.broadcasted_iota(jnp.int32, v.shape, 0), length)
@@ -753,70 +893,145 @@
     return jnp.where(edge, 0.0, pltpu.roll(v, rows - 1 if back else 1, 0))
 
 
-def feed_kernel(length, n2, lerp, wla, wc, *refs):
-    kc_out, sq_out, fac_out, va_out = refs[-4:]
+def feed_kernel(length, own_order, order, n2, lerp, wl, wc, *refs):
+    kc_out, sq_out, fac_out, near_out, far_out = refs[-5:]
     n = n2[...].astype(F32)
     delta = step_shift(length, n) - n
     kc = (n + delta * lerp[0:1, :]).astype(BF)
     kc_out[...] = kc
-    act = mm(kc, wla[:, : wc.shape[0]])
+    act = mm(kc, wl[...])
     soft = jnp.maximum(act, 0.0) + jnp.log1p(jnp.exp(-jnp.abs(act)))
     fac_out[...] = 2.0 * soft * jax.nn.sigmoid(act)
     sq = (soft * soft).astype(BF)
     sq_out[...] = sq
-    va_out[...] = mm(sq, wc[...]).astype(BF)
-
-
-def feed(length, n2, lerp, wla, wc, part, earlier=()):
+    some, _, c = near_out.shape
+    for i in range(2 * some):
+        at = pl.ds(pl.multiple_of(order[i] * c, c), c) if own_order else slice(i * c, (i + 1) * c)
+        out = near_out if i < some else far_out
+        out[i % some] = mm(sq, wc[:, at]).astype(BF)
+
+
+def feed(length, n2, lerp, wl, wc, part, earlier=()):
     g, d = n2.shape
     f = wc.shape[0]
+    n = lax.axis_size("fsdp")
     half = g // 2
     rows = 2 * length if half % (2 * length) == 0 else length
-    if half % rows:
-        rows = half
     first = part * (half // rows)
-    block = lambda w: pl.BlockSpec((rows, w), lambda s: (first + s, 0))
+    block = lambda w: pl.BlockSpec((rows, w), lambda s, o: (first + s, 0))
     shape = lambda w, t: jax.ShapeDtypeStruct((g, w), t)
     return pl.pallas_call(
-        functools.partial(feed_kernel, length),
-        grid=(half // rows,),
-        in_specs=[block(d)]
-        + [whole_block(a) for a in (lerp, wla, wc)]
-        + [pl.BlockSpec(memory_space=pl.ANY)] * len(earlier),
-        out_specs=[block(d), block(f), block(f), block(d)],
-        out_shape=[shape(d, BF), shape(f, BF), shape(f, F32), shape(d, BF)],
-        input_output_aliases={4 + i: i for i in range(len(earlier))},
+        functools.partial(feed_kernel, length, paired()),
+        grid_spec=pltpu.PrefetchScalarGridSpec(
+            num_scalar_prefetch=1,
+            grid=(half // rows,),
+            in_specs=[block(d)]
+            + [whole_block(a) for a in (lerp, wl, wc)]
+            + [pl.BlockSpec(memory_space=pl.ANY)] * len(earlier),
+            out_specs=[block(d), block(f), block(f)]
+            + [pl.BlockSpec((n // 2, rows, d // n), lambda s, o: (0, s, 0))] * 2,
+        ),
+        out_shape=[shape(d, BF), shape(f, BF), shape(f, F32)]
+        + [jax.ShapeDtypeStruct((n // 2, half, d // n), BF)] * 2,
+        input_output_aliases={5 + i: i for i in range(len(earlier))},
         compiler_params=pltpu.CompilerParams(vmem_limit_bytes=52 * MIB),
         cost_estimate=lasts(8),
         name="feed",
-    )(n2, lerp, wla, wc, *earlier)
-
-
-def gate_kernel(length, n2, lerp, wla, rc_out, gate_out):
+    )(orders(), n2, lerp, wl, wc, *earlier)
+
+
+def pair_kernel(near0, near1, got0, got1, *outs):
+    half = near0.shape[1]
+    for q, out in enumerate(outs):
+
+        @pl.when(pl.program_id(0) == q)
+        def _():
+            out[:half, :] = (near0[0].astype(F32) + got1[0].astype(F32)).astype(BF)
+            out[half:, :] = (near1[0].astype(F32) + got0[0].astype(F32)).astype(BF)
+
+
+def gated_kernel(paired_order, adj, gate, *refs):
+    *parts, gated_out, dgate_out = refs
+    rows = adj.shape[0] // (8 if paired_order else 1)
+    for i, own in enumerate(ORDER if paired_order else (0,)):
+        at = slice(i * rows, (i + 1) * rows)
+        value = parts[0][at, :].astype(F32)
+        for q, part in enumerate(parts[1:]):
+            p = ORDER.index((2 * q + 2) ^ own)
+            value = value + part[p * rows : (p + 1) * rows, :].astype(F32)
+        g = gate[at, :].astype(F32)
+        gated = g * value
+        gated_out[at, :] = gated.astype(BF)
+        dgate_out[at, :] = (adj[at, :].astype(F32) * gated * (1.0 - g)).astype(BF)
+
+
+def gated_value(adj, gate, halves_of_value):
+    (near0, far0), (near1, far1) = halves_of_value
+    g, c = gate.shape
+    if paired():
+        got0, got1 = swap(far0, 1), swap(far1, 1)
+        block = pl.BlockSpec((1, g // 2, c), lambda q: (q, 0, 0))
+        parts = pl.pallas_call(
+            pair_kernel,
+            grid=(4,),
+            in_specs=[block] * 4,
+            out_specs=[pl.BlockSpec((g, c), lambda q: (0, 0))] * 4,
+            out_shape=[jax.ShapeDtypeStruct((g, c), BF)] * 4,
+            compiler_params=pltpu.CompilerParams(vmem_limit_bytes=32 * MIB),
+            cost_estimate=SHORT,
+            name="pairs",
+        )(near0, near1, got0, got1)
+        parts = [parts[0]] + [swap(parts[q], 2 * q) for q in (1, 2, 3)]
+        rows = g
+    else:
+        sums = [
+            lax.psum_scatter(
+                jnp.concatenate(t, axis=0), "fsdp", scatter_dimension=0, tiled=True
+            )[0]
+            for t in halves_of_value
+        ]
+        parts = [jnp.concatenate(sums, axis=0)]
+        rows = g // lax.axis_size("fsdp")
+    block = pl.BlockSpec((rows, c), lambda s: (s, 0))
+    return pl.pallas_call(
+        functools.partial(gated_kernel, paired()),
+        grid=(g // rows,),
+        in_specs=[block] * (2 + len(parts)),
+        out_specs=[block] * 2,
+        out_shape=[jax.ShapeDtypeStruct((g, c), BF)] * 2,
+        compiler_params=pltpu.CompilerParams(vmem_limit_bytes=32 * MIB),
+        cost_estimate=SHORT,
+        name="gated_value",
+    )(adj, gate, *parts)
+
+
+def gate_kernel(length, n2, adj, lerp, wa, rc_out, gate_out, dv_out):
     n = n2[...].astype(F32)
     rc = (n + (step_shift(length, n) - n) * lerp[1:2, :]).astype(BF)
     rc_out[...] = rc
-    gate_out[...] = jax.nn.sigmoid(mm(rc, wla[:, wla.shape[1] - gate_out.shape[1] :])).astype(BF)
-
-
-def feed_gate(length, n2, lerp, wla):
+    gate = jax.nn.sigmoid(mm(rc, wa[...]))
+    gate_out[...] = gate.astype(BF)
+    dv_out[...] = (adj[...].astype(F32) * gate).astype(BF)
+
+
+def feed_gate(length, n2, adj, lerp, wa):
     g, d = n2.shape
-    c = d // lax.axis_size("fsdp")
+    c = wa.shape[1]
     rows = 2 * length if g % (2 * length) == 0 else length
     block = lambda w: pl.BlockSpec((rows, w), lambda s: (s, 0))
     return pl.pallas_call(
         functools.partial(gate_kernel, length),
         grid=(g // rows,),
-        in_specs=[block(d), whole_block(lerp), whole_block(wla)],
-        out_specs=[block(d), block(c)],
-        out_shape=[jax.ShapeDtypeStruct((g, d), BF), jax.ShapeDtypeStruct((g, c), BF)],
+        in_specs=[block(d), block(c), whole_block(lerp), whole_block(wa)],
+        out_specs=[block(d), block(c), block(c)],
+        out_shape=[jax.ShapeDtypeStruct((g, w), BF) for w in (d, c, c)],
         compiler_params=pltpu.CompilerParams(vmem_limit_bytes=32 * MIB),
         cost_estimate=SHORT,
         name="feed_gate",
-    )(n2, lerp, wla)
-
-
-def feed_back_kernel(length, dv, n2, fac, dgate, lerp, wla, wc, dkey_out, dn_out, vec_out):
+    )(n2, adj, lerp, wa)
+
+
+def feed_back_kernel(length, dv, n2, fac, dgate, lerp, wl, wa, wc, dkey_out, dn_out, vec_out):
     @pl.when(pl.program_id(0) == 0)
     def _():
         vec_out[...] = jnp.zeros_like(vec_out)
@@ -825,16 +1040,15 @@
     dkey_out[...] = dkey
     n = n2[...].astype(F32)
     delta = step_shift(length, n) - n
-    f = wc.shape[0]
-    dk = mm_nt(dkey, wla[:, :f])
-    dr = mm_nt(dgate[...], wla[:, f:])
+    dk = mm_nt(dkey, wl[...])
+    dr = mm_nt(dgate[...], wa[...])
     vec_out[0:1, :] += jnp.sum(dk * delta, axis=0, keepdims=True)
     vec_out[1:2, :] += jnp.sum(dr * delta, axis=0, keepdims=True)
     moved = dk * lerp[0:1, :] + dr * lerp[1:2, :]
     dn_out[...] = (dk + dr - moved + step_shift(length, moved, True)).astype(BF)
 
 
-def feed_back(length, dv, n2, fac, dgate, lerp, wla, wc):
+def feed_back(length, dv, n2, fac, dgate, lerp, wl, wa, wc):
     g, d = n2.shape
     f, c = wc.shape[0], dgate.shape[1]
     rows = 2 * length if g % (2 * length) == 0 else length
@@ -843,7 +1057,7 @@
         functools.partial(feed_back_kernel, length),
         grid=(g // rows,),
         in_specs=[block(d), block(d), block(f), block(c)]
-        + [whole_block(a) for a in (lerp, wla, wc)],
+        + [whole_block(a) for a in (lerp, wl, wa, wc)],
         out_specs=[block(f), block(d), pl.BlockSpec((2, d), lambda s: (0, 0))],
         out_shape=[
             jax.ShapeDtypeStruct((g, f), BF),
@@ -853,7 +1067,7 @@
         compiler_params=pltpu.CompilerParams(vmem_limit_bytes=52 * MIB),
         cost_estimate=SHORT,
         name="feed_back",
-    )(dv, n2, fac, dgate, lerp, wla, wc)
+    )(dv, n2, fac, dgate, lerp, wl, wa, wc)
 
 
 def body(
@@ -895,81 +1109,99 @@
     tok_home = incoming_symbols.reshape(home, d)
     z = lax.axis_index("rep")
     share = c // lax.axis_size("rep")
-    feed_weights = Exchange(
-        [
-            lax.dynamic_slice_in_dim(t, z * share, share, 0)
-            for t in (feed_lookup_weights, feed_acceptor_weights)
-        ],
+    lookup_quarter = Exchange(
+        [lax.dynamic_slice_in_dim(feed_lookup_weights, z * share, share, 0)], 1
+    )
+    lookup_quarter.across_cores()
+    lookup_quarter.across_chips()
+    tokens = lax.all_gather(tok_home, "fsdp", axis=0, tiled=True)
+    mix_weights = Exchange(
+        (
+            lookup_weights,
+            content_weights,
+            acceptor_weights,
+            valve_weights,
+            feed_acceptor_weights,
+        ),
         1,
     )
-    feed_weights.across_cores()
-    feed_weights.across_chips()
-    mix_weights = Exchange(
-        (lookup_weights, content_weights, acceptor_weights, valve_weights), 1
-    )
     mix_weights.across_cores()
-    parcels = mix_weights.parcels()
-    tokens, *held = gather_tokens(tok_home, *parcels, *feed_weights.got_parcels())
-    mix_weights.across_chips(held[: len(parcels)])
-    feed_weights.got = held[len(parcels) :]
+    mix_weights.across_chips()
     positions = lax.broadcasted_iota(jnp.int32, (seqs, length), 1)
     mask = (positions < string_extents[:, None]).astype(F32).reshape(home, 1)
-    d_out = adjoint_signal.reshape(home, d).astype(F32) * mask
+    adjoint = adjoint_signal.reshape(home, d) * mask.astype(BF)
+    d_out = adjoint.astype(F32)
 
     row = lambda v: v.reshape(1, -1)
     mine = lambda v: lax.dynamic_slice_in_dim(v, me * c, c, v.ndim - 1)
     gain1, shift1 = row(first_scaling_factor), row(first_scaling_shift)
     narrow, fnarrow = lerp_narrow_weights.T, fading_narrow_weights.T
     widen = lerp_widen_weights.reshape(5 * ranks, d)
-    feed_shares = jnp.concatenate(feed_weights.results(), axis=1).reshape(n, share, -1)
-    tokens, feed_shares = hold(tokens, feed_shares)
-    feed_full = lax.all_gather(feed_shares, "rep", axis=1, tiled=True).reshape(d, -1)
+    (tokens,) = mix_weights.arrived(tokens, count=2)
     xk, xv, xr, xg, hidden, low = front(
         length, tokens, gain1, shift1, lerp_factors, narrow, widen, fnarrow
     )
-    (low,) = mix_weights.arrived(low)
-    wk, wv, wr, wg = mix_weights.results()
+    (low,) = mix_weights.arrived(*lookup_quarter.arrived(low))
+    (lookup_share,) = lookup_quarter.results()
+    low, lookup_share = hold(low, lookup_share)
+    wl = lax.all_gather(lookup_share.reshape(n, share, -1), "rep", axis=1, tiled=True)
+    wl = wl.reshape(d, -1)
+    wk, wv, wr, wg, wa = mix_weights.results()
     fwiden_mine = mine(fading_widen_weights)
-    w = -jnp.exp(
-        mine(row(fading_baseline))
-        + jnp.dot(low, fwiden_mine, precision=lax.Precision.HIGHEST)
-    )
-    k, v, r, g = mm(xk, wk), mm(xv, wv), mm(xr, wr), mm(xg, wg)
-    u, gn_gain, gn_bias = (
-        mine(row(t)) for t in (present_reward, cluster_scaling_factor, cluster_scaling_shift)
-    )
-    mixed = wkv(length, r, k, v, g, w, u, gn_gain, gn_bias)
-    mixed, feed_full = hold(mixed, feed_full)
-    branch = scatter_tokens(mm(mixed, emission_weights).astype(BF))
+    base, u, gn_gain, gn_bias = (
+        mine(row(t))
+        for t in (
+            fading_baseline,
+            present_reward,
+            cluster_scaling_factor,
+            cluster_scaling_shift,
+        )
+    )
+    k, v, r, g, w, mixed, near, far = mix(
+        length,
+        (xk, xv, xr, xg),
+        low,
+        (wk, wv, wr, wg),
+        emission_weights,
+        (base, u, gn_gain, gn_bias),
+        fwiden_mine,
+    )
+    branch = scatter_tokens(near, far)
+    branch, wl, wa = hold(branch, wl, wa)
+    branch, adjoint = hold(branch, adjoint)
+    adjoint_cols = spread_features(adjoint)
     residual = tok_home.astype(F32) + branch
 
     center = residual - jnp.mean(residual, axis=-1, keepdims=True)
     rstd2 = lax.rsqrt(jnp.mean(center * center, axis=-1, keepdims=True) + norm_eps)
     unit2 = center * rstd2
-    (normed2,) = gather_tokens((unit2 * second_scaling_factor + second_scaling_shift_vec).astype(BF))
+    normed2, _ = gather_tokens(
+        (unit2 * second_scaling_factor + second_scaling_shift_vec).astype(BF)
+    )
     fc = feed_content_weights.shape[0]
-    recept_chan, gate = feed_gate(length, normed2, feed_lerp_factors, feed_full)
-    feed_part = lambda *t: feed(length, normed2, feed_lerp_factors, feed_full, feed_content_weights, *t)
-    gate, earlier = home_features(gate, lambda: feed_part(0))
-    gate = gate.astype(F32)
-    (d_value,) = gather_tokens((d_out * gate).astype(BF))
-    key_chan, squared, factor, value_part = feed_part(1, earlier)
+    recept_chan, gate, d_value_mine = feed_gate(
+        length, normed2, adjoint_cols, feed_lerp_factors, wa
+    )
+    feed_part = lambda *t: feed(length, normed2, feed_lerp_factors, wl, feed_content_weights, *t)
+
+    def second_part(*done):
+        return (*feed_part(1, done[:3]), *done[3:])
+
+    d_value, held = gather_features_of_tokens(d_value_mine, (lambda: feed_part(0), second_part))
+    key_chan, squared, factor, *values = held
     d_content = mm_tn(squared, d_value).astype(BF)
-    d_value, d_content, value_part = hold(d_value, d_content, value_part)
+    d_value, d_content, *values = hold(d_value, d_content, *values)
     content_share = lax.psum_scatter(d_content, "rep", scatter_dimension=0, tiled=True)
-    value_act = scatter_tokens(value_part)
-    gated = gate * value_act
-    layer_output = (residual + gated) * mask
-    d_gate = spread_features((d_out * gated * (1.0 - gate)).astype(BF))
+    gated, d_gate = gated_value(adjoint_cols, gate, (values[2:], values[:2]))
 
     d_key, d_normed2, feed_lerp_part = feed_back(
-        length, d_value, normed2, factor, d_gate, feed_lerp_factors, feed_full, feed_content_weights
+        length, d_value, normed2, factor, d_gate, feed_lerp_factors, wl, wa, feed_content_weights
     )
     d_normed2, content_share = hold(d_normed2, content_share)
     feed_share = rep_scatter_cols(
         (mm_tn(key_chan, d_key).astype(BF), mm_tn(recept_chan, d_gate).astype(BF))
     )
-    d_normed2 = scatter_tokens(d_normed2)
+    d_normed2 = scatter_tokens(d_normed2[: plane // 2], d_normed2[plane // 2 :])
     content_sum = rep_gather(content_share)
 
     def norm_back(unit, rstd, e):
@@ -979,18 +1211,20 @@
             - unit * jnp.mean(e * unit, axis=-1, keepdims=True)
         )
 
+    layer_output = (residual + home_features(gated).astype(F32)) * mask
     d_residual = d_out + norm_back(unit2, rstd2, d_normed2 * second_scaling_factor)
     norm2_part = jnp.stack([jnp.sum(d_normed2 * unit2, axis=0), jnp.sum(d_normed2, axis=0)])
 
-    (d_branch,) = gather_tokens(d_residual.astype(BF))
+    d_branch, _ = gather_tokens(d_residual.astype(BF))
     d_mixed = mm_nt(d_branch, emission_weights)
-    emission_share = rep_scatter(mm_tn(mixed, d_branch).astype(BF))
-    d_r, d_k, d_v, d_g, d_raw, mix_vec = wkv(
+    d_emission = mm_tn(mixed, d_branch).astype(BF)
+    d_r, d_k, d_v, d_g, d_raw, mix_vec = mix_back(
         length, r, k, v, g, w, u, gn_gain, gn_bias, d_mixed
     )
     d_r, d_k, d_v, d_g, feed_share = hold(d_r, d_k, d_v, d_g, feed_share)
-    time_share = rep_scatter_cols(
-        [mm_tn(x, t).astype(BF) for x, t in ((xk, d_k), (xv, d_v), (xr, d_r), (xg, d_g))]
+    time_share, emission_share = rep_scatter_cols(
+        [mm_tn(x, t).astype(BF) for x, t in ((xk, d_k), (xv, d_v), (xr, d_r), (xg, d_g))],
+        d_emission,
     )
     feed_sums = Exchange([feed_share[:, :fc], feed_share[:, fc:]], 0)
     feed_sums.across_cores()
@@ -1005,11 +1239,9 @@
         (gain1, shift1, lerp_factors, narrow, widen, fnarrow, fwiden_mine),
         (wk, wv, wr, wg),
     )
-    d_normed, content_sum, emission_share = feed_sums.arrived(
-        *hold(d_normed, content_sum, emission_share)
-    )
+    d_normed, content_sum = feed_sums.arrived(*hold(d_normed, content_sum))
     feed_sum = rep_gather(jnp.concatenate(feed_sums.results(), axis=1))
-    d_normed = scatter_tokens(d_normed)
+    d_normed = scatter_tokens(d_normed[: plane // 2], d_normed[plane // 2 :])
     small = scatter_features(
         jnp.concatenate(
             [vec_part, widen_part, narrow_part, fnarrow_part, norm2_part, feed_lerp_part], axis=0

time: 853 us -> 821 us (0.962)
  waiting for transfers between devices: 409 us -> 387 us
  local copies, waits for them, and re-layouts: 89.6 us -> 72.7 us
  Pallas kernels: 198 us -> 214 us
  matrix products: 35.6 us -> 24.6 us
    pallas_call x8 -> x11, Pallas kernels: 144 us -> 158 us  [the longest x1 49.7 us: back(): pl.pallas_call(functools.partial(back_kernel, ranks), grid_spec=pltpu.Pre...]
    ppermute x68 -> x64, waiting for transfers between devices: 242 us -> 229 us  [swap(): return lax.ppermute(v, 'fsdp', [(i, i ^ m) for i in range(8)])]
    unnamed x224 -> x223, local copies, waits for them, and re-layouts: 54.4 us -> 46.2 us
    ppermute x68 -> x64, starting transfers between devices: 64.8 us -> 63.6 us  [swap(): return lax.ppermute(v, 'fsdp', [(i, i ^ m) for i in range(8)])]
  transfers between devices with their start and end apart: 79 -> 75, of which waited for: 51 -> 50; matrix products, arithmetic and copies ran while one was open for 11% -> 9% of each run, Pallas kernels for 22% -> 25%
where the time goes in v3:
time: 821 us; the launch traced here: 815 us
  waiting for transfers between devices  387 us (47%)
  Pallas kernels  214 us (26%)
  local copies, waits for them, and re-layouts  72.7 us (9%)
  starting transfers between devices  70.8 us (9%)
  other arithmetic  29.9 us (4%)
  matrix products  24.6 us (3%)
  between operations  16.9 us (2%)
    ppermute x64, waiting for transfers between devices, swap(): return lax.ppermute(v, 'fsdp', [(i, i ^ m) for i in range(8)])  229 us
    all_gather x3, waiting for transfers between devices, rep_gather(): return lax.all_gather(v, 'rep', axis=0, tiled=True)  126 us
    ppermute x64, starting transfers between devices, swap(): return lax.ppermute(v, 'fsdp', [(i, i ^ m) for i in range(8)])  63.6 us
    pallas_call x1, Pallas kernels, back(): pl.pallas_call(functools.partial(back_kernel, ranks), grid_spec=pltpu.Pre...  49.7 us
    unnamed x223, local copies, waits for them, and re-layouts  46.2 us
    pallas_call x1, Pallas kernels, mix_back(): pl.pallas_call(functools.partial(wkv_back_kernel, levels, count, width),...  29.9 us
    pallas_call x1, Pallas kernels, front(): pl.pallas_call(functools.partial(front_kernel, ranks), grid_spec=pltpu.Pr...  26.8 us
    ppermute x3, waiting for transfers between devices, rep_sum(): lax.ppermute(v, 'rep', [(i, (i + s) % n) for i in range(n)]).astype(F32)  26 us
  transfers between devices with their start and end apart: 75, of which 50 were waited for; matrix products, arithmetic and copies ran while one was open for 9% of the time, Pallas kernels for 25%

profile of v3, /device:TPU:0, one launch (start us, length us, event | category | flops | bytes accessed | tf_op | source)
XLA Modules:
  0.0 815.2 jit_solution(15767496345100093327)
XLA Ops:
  18.6 4.7 collective-permute-done.refs_4_
  42.1 26.7 %collective-permute-done.2.refs_2_.refs_6_ = bf16[2,256,1280]{2,1,0:T(8,128)(2,1)S(1)} collective-permute-done((bf16[2,256,1280]{2,1,0:T(8,128)(2,1)S(1)}, bf16[2,256,1280]{2,1,0:T(8,128)(2,1)S(1)}, u32[]{:S(2)}, u32[]{:S(2)}) %collective-permute-start.2) | collective-permute-done | bytes 1310752 | tf_op jit(solution)/shard_map/ppermute | solution.py:50
  79.7 26.8 %token_shift.1 = (bf16[1024,2048]{1,0:T(8,128)(2,1)}, bf16[1024,2048]{1,0:T(8,128)(2,1)}, bf16[1024,2048]{1,0:T(8,128)(2,1)}, bf16[1024,2048]{1,0:T(8,128)(2,1)}...) custom-call(s32[8]{0:T(128)S(1)} %stack.26.order, bf16[1024,2048]{1,0:T(8,128)(2,1)} %bitcast.149, ...), custom_call_target="tpu_custom_call" | custom-call | flops 1 | bytes 1 | tf_op jit(solution)/shard_map/token_shift/pallas_call | solution.py:474
  121.8 24.2 %decay_mix.1 = (f32[1024,256]{1,0:T(8,128)S(1)}, f32[1024,256]{1,0:T(8,128)S(1)}, f32[1024,256]{1,0:T(8,128)S(1)}, f32[1024,256]{1,0:T(8,128)S(1)}, f32[1024,256...) custom-call(bf16[1024,2048]{1,0:T(8,128)(2,1)} %get-tuple-element.156.refs_0_, ...), custom_call_target="tpu_custom_call" | custom-call | flops 20000000000 | bytes 1 | tf_op jit(solution)/shard_map/decay_mix/pallas_call | solution.py:750
  158.7 21.0 %collective-permute-done.10 = bf16[128,2048]{1,0:T(8,128)(2,1)S(1)} collective-permute-done((bf16[128,2048]{1,0:T(8,128)(2,1)}, bf16[128,2048]{1,0:T(8,128)(2,1)S(1)}, u32[]{:S(2)}, u32[]{:S(2)}) %collective-permute-start.10) | collective-permute-done | bytes 524320 | tf_op jit(solution)/shard_map/ppermute | solution.py:50
  203.7 8.4 %collective-permute-done.18 = bf16[128,2048]{1,0:T(8,128)(2,1)S(1)} collective-permute-done((bf16[128,2048]{1,0:T(8,128)(2,1)S(1)}, bf16[128,2048]{1,0:T(8,128)(2,1)S(1)}, u32[]{:S(2)}, u32[]{:S(2)}) %collective-permute-start.18) | collective-permute-done | bytes 524320 | tf_op jit(solution)/shard_map/ppermute | solution.py:50
  227.5 11.1 %feed.2 = (bf16[1024,2048]{1,0:T(8,128)(2,1)}, bf16[1024,896]{1,0:T(8,128)(2,1)}, f32[1024,896]{1,0:T(8,128)}, bf16[4,512,256]{2,1,0:T(8,128)(2,1)S(1)}, bf16[4,512,256]{2,1,0:T(8,128)(2,1)}) custom-call(s32[8]{0:T(128)S(1)} %stack.26.order, bf16[1024,2048]{1,0:T(8,128)(2,1)} %copy-done.3, f32[2,2048]{1,0:T(2,128)S(1)} %copy-done.62, ...), custom_call_target="tpu_custom_call" | custom-call | flops 8000000000 | bytes 1 | tf_op jit(solution)/shard_map/feed/pallas_call | solution.py:923
  241.1 11.5 %feed.3 = (bf16[1024,2048]{1,0:T(8,128)(2,1)}, bf16[1024,896]{1,0:T(8,128)(2,1)}, f32[1024,896]{1,0:T(8,128)}, bf16[4,512,256]{2,1,0:T(8,128)(2,1)S(1)}, bf16[4,512,256]{2,1,0:T(8,128)(2,1)}) custom-call(s32[8]{0:T(128)S(1)} %stack.26.order, bf16[1024,2048]{1,0:T(8,128)(2,1)} %copy-done.3, ...), custom_call_target="tpu_custom_call", output_to_operand_aliasing={{0}: (5, {}), {1}: (6, {}), {2}: (7, {})} | custom-call | flops 8000000000 | bytes 1 | tf_op jit(solution)/shard_map/feed/pallas_call | solution.py:923
  261.1 5.5 convolution_convert_fusion.1
  277.9 11.3 %collective-permute-done.28.refs_1_ = bf16[1024,256]{1,0:T(8,128)(2,1)S(1)} collective-permute-done((bf16[1024,256]{1,0:T(8,128)(2,1)S(1)}, bf16[1024,256]{1,0:T(8,128)(2,1)S(1)}, u32[]{:S(2)}, u32[]{:S(2)}) %collective-permute-start.28) | collective-permute-done | bytes 524320 | tf_op jit(solution)/shard_map/ppermute | solution.py:50
  289.1 10.4 %collective-permute-done.29.refs_2_ = bf16[1024,256]{1,0:T(8,128)(2,1)S(1)} collective-permute-done((bf16[1024,256]{1,0:T(8,128)(2,1)S(1)}, bf16[1024,256]{1,0:T(8,128)(2,1)S(1)}, u32[]{:S(2)}, u32[]{:S(2)}) %collective-permute-start.29) | collective-permute-done | bytes 524320 | tf_op jit(solution)/shard_map/ppermute | solution.py:50
  302.2 18.9 %feed_back.1 = (bf16[1024,896]{1,0:T(8,128)(2,1)}, bf16[1024,2048]{1,0:T(8,128)(2,1)}, f32[2,2048]{1,0:T(2,128)S(1)}) custom-call(bf16[1024,2048]{1,0:T(8,128)(2,1)} %copy-done.5, bf16[1024,2048]{1,0:T(8,128)(2,1)} %copy-done.3, f32[1024,896]{1,0:T(8,128)} %get-tuple-element.223.fac, bf16[1024,256]{1,0:T(8,128)(2,1)S(1)} %get-tuple-element.224.dgate, ...), custom_call_target="tpu_custom_call" | custom-call | flops 1 | bytes 1 | tf_op jit(solution)/shard_map/feed_back/pallas_call | solution.py:1056
  321.1 6.5 convolution_convert_fusion.refs_0_
  351.1 21.7 %collective-permute-done.32 = bf16[128,512]{1,0:T(8,128)(2,1)S(1)} collective-permute-done((bf16[128,512]{1,0:T(8,128)(2,1)S(1)}, bf16[128,512]{1,0:T(8,128)(2,1)S(1)}, u32[]{:S(2)}, u32[]{:S(2)}) %collective-permute-start.32) | collective-permute-done | bytes 131104 | tf_op jit(solution)/shard_map/ppermute | solution.py:50
  393.3 9.4 %collective-permute-done.41 = bf16[128,2048]{1,0:T(8,128)(2,1)S(1)} collective-permute-done((bf16[128,2048]{1,0:T(8,128)(2,1)S(1)}, bf16[128,2048]{1,0:T(8,128)(2,1)S(1)}, u32[]{:S(2)}, u32[]{:S(2)}) %collective-permute-start.41) | collective-permute-done | bytes 524320 | tf_op jit(solution)/shard_map/ppermute | solution.py:50
  411.0 29.9 %decay_mix_back.1 = (bf16[1024,256]{1,0:T(8,128)(2,1)S(1)}, bf16[1024,256]{1,0:T(8,128)(2,1)S(1)}, bf16[1024,256]{1,0:T(8,128)(2,1)S(1)}, bf16[1024,256]{1,0:T(8...) custom-call(f32[1024,256]{1,0:T(8,128)S(1)} %copy-done.39, f32[1024,256]{1,0:T(8,128)S(1)} %get-tuple-element.230.k_ref, ...), custom_call_target="tpu_custom_call" | custom-call | flops 1 | bytes 1 | tf_op jit(solution)/shard_map/decay_mix_back/pallas_call | solution.py:874
  442.0 4.3 convolution_convert_fusion.3.refs_3_
  466.9 49.7 %token_shift_back.1 = (bf16[1024,2048]{1,0:T(8,128)(2,1)}, f32[8,2048]{1,0:T(8,128)}, f32[160,2048]{1,0:T(8,128)}, f32[160,2048]{1,0:T(8,128)}, f32[64,2048]{1,0:T(8,128)}) custom-call(s32[8]{0:T(128)} %copy-done.59, bf16[1024,2048]{1,0:T(8,128)(2,1)} %bitcast.150, f32[1024,160]{1,0:T(8,128)} %copy-done.26, f32[1024,64]{1,0:T(8,128)} %copy-done.19, ...), custom_call_target="tpu_custom_call" | custom-call | flops 1 | bytes 1 | tf_op jit(solution)/shard_map/token_shift_back/pallas_call | solution.py:597
  535.8 4.2 collective-permute-done.53
  540.0 4.7 collective-permute-done.54
  551.1 9.5 %collective-permute-done.56 = bf16[464,256]{1,0:T(8,128)(2,1)S(1)} collective-permute-done((bf16[464,256]{1,0:T(8,128)(2,1)S(1)}, bf16[464,256]{1,0:T(8,128)(2,1)S(1)}, u32[]{:S(2)}, u32[]{:S(2)}) %collective-permute-start.56) | collective-permute-done | bytes 237600 | tf_op jit(solution)/shard_map/ppermute | solution.py:386
  560.6 16.5 %collective-permute-done.57 = bf16[464,256]{1,0:T(8,128)(2,1)S(1)} collective-permute-done((bf16[464,256]{1,0:T(8,128)(2,1)S(1)}, bf16[464,256]{1,0:T(8,128)(2,1)S(1)}, u32[]{:S(2)}, u32[]{:S(2)}) %collective-permute-start.57) | collective-permute-done | bytes 237600 | tf_op jit(solution)/shard_map/ppermute | solution.py:386
  582.8 10.2 %collective-permute-done.60 = bf16[464,512]{1,0:T(8,128)(2,1)S(1)} collective-permute-done((bf16[464,512]{1,0:T(8,128)(2,1)S(1)}, bf16[464,512]{1,0:T(8,128)(2,1)S(1)}, u32[]{:S(2)}, u32[]{:S(2)}) %collective-permute-start.60) | collective-permute-done | bytes 475168 | tf_op jit(solution)/shard_map/ppermute | solution.py:50
  593.0 9.9 %collective-permute-done.61 = bf16[464,512]{1,0:T(8,128)(2,1)S(1)} collective-permute-done((bf16[464,512]{1,0:T(8,128)(2,1)S(1)}, bf16[464,512]{1,0:T(8,128)(2,1)S(1)}, u32[]{:S(2)}, u32[]{:S(2)}) %collective-permute-start.61) | collective-permute-done | bytes 475168 | tf_op jit(solution)/shard_map/ppermute | solution.py:50
  614.7 6.1 collective-permute-done.66.refs_3_.refs_7_
  620.8 4.8 collective-permute-done.65.refs_2_.refs_6_
  638.6 10.2 %widened.5 = f32[896,2048]{1,0:T(8,128)} custom-call(bf16[896,2048]{1,0:T(8,128)(2,1)S(1)} %copy-done.17), custom_call_target="tpu_custom_call" | custom-call | flops 1 | bytes 1 | tf_op jit(solution)/shard_map/widened/pallas_call | solution.py:370
  649.8 11.6 %collective-permute-done.50 = bf16[128,2048]{1,0:T(8,128)(2,1)S(1)} collective-permute-done((bf16[128,2048]{1,0:T(8,128)(2,1)S(1)}, bf16[128,2048]{1,0:T(8,128)(2,1)S(1)}, u32[]{:S(2)}, u32[]{:S(2)}) %collective-permute-start.50) | collective-permute-done | bytes 524320 | tf_op jit(solution)/shard_map/ppermute | solution.py:50
  663.5 38.6 %all-gather.13.cloned.1.call-done.refs_0_ = bf16[256,9216]{1,0:T(8,128)(2,1)} async-done(((bf16[64,9216]{1,0:T(8,128)(2,1)}), bf16[256,9216]{1,0:T(8,128)(2,1)}) %all-gather.13.cloned.1.call-update) | async-done | bytes 4718608 | tf_op jit(solution)/shard_map/all_gather | solution.py:302
  704.5 4.6 widened.4
  713.9 86.9 %all-gather.11.cloned.1.call-done.refs_0_ = bf16[256,10240]{1,0:T(8,128)(2,1)} async-done(((bf16[64,10240]{1,0:T(8,128)(2,1)}), bf16[256,10240]{1,0:T(8,128)(2,1)}) %all-gather.11.cloned.1.call-update) | async-done | bytes 5242896 | tf_op jit(solution)/shard_map/all_gather | solution.py:302
  803.3 4.8 widened.3
  (502 shorter events, 273.8 us)
Async XLA Ops:
  7.2 68.8 %all-gather.15.cloned.1.call-start = ((), (), s32[]{:S(2)}) async-start(), calls=%async_computation.10 | async-start | bytes 4718592 | tf_op jit(solution)/shard_map/all_gather | solution.py:1117
  7.9 177.9 %all-gather.7.cloned.1.call-start = ((), (), s32[]{:S(2)}) async-start(), calls=%async_computation.3 | async-start | bytes 4587520 | tf_op jit(solution)/shard_map/all_gather | solution.py:1147
  25.1 43.7 %collective-permute-start.2 = (bf16[2,256,1280]{2,1,0:T(8,128)(2,1)S(1)}, bf16[2,256,1280]{2,1,0:T(8,128)(2,1)S(1)}, u32[]{:S(2)}, u32[]{:S(2)}) collective-permute-start(bf16[2,256,1280]{2,1,0:T(8,128)(2,1)S(1)} %pad_maximum_fusion.1), channel_id=1, source_target_pairs={{0,16},{4,20},{8,24},{12,28},{16,0},{20,4},{24,8},{28,12},{1,17},{... | collective-permute-start | bytes 3932168 | tf_op jit(solution)/shard_map/ppermute | solution.py:50
  29.2 46.7 %collective-permute-start.1 = (bf16[2,256,1280]{2,1,0:T(8,128)(2,1)}, bf16[2,256,1280]{2,1,0:T(8,128)(2,1)}, u32[]{:S(2)}, u32[]{:S(2)}) collective-permute-start(bf16[2,256,1280]{2,1,0:T(8,128)(2,1)} %pad_maximum_fusion), channel_id=1, source_target_pairs={{0,8},{4,12},{8,0},{12,4},{16,24},{20,28},{24,16},{28,20},{1,9},{5... | collective-permute-start | bytes 3932168 | tf_op jit(solution)/shard_map/ppermute | solution.py:50
  31.9 77.1 %collective-permute-start.7 = (bf16[2,256,1280]{2,1,0:T(8,128)(2,1)}, bf16[2,256,1280]{2,1,0:T(8,128)(2,1)}, u32[]{:S(2)}, u32[]{:S(2)}) collective-permute-start(bf16[2,256,1280]{2,1,0:T(8,128)(2,1)} %pad_maximum_fusion.2), channel_id=1, source_target_pairs={{0,24},{4,28},{8,16},{12,20},{16,8},{20,12},{24,0},{28,4},{1,25},{... | collective-permute-start | bytes 3932168 | tf_op jit(solution)/shard_map/ppermute | solution.py:50
  37.5 69.0 %collective-permute-start.4 = (bf16[2,64,896]{2,1,0:T(8,128)(2,1)}, bf16[2,64,896]{2,1,0:T(8,128)(2,1)S(1)}, u32[]{:S(2)}, u32[]{:S(2)}) collective-permute-start(bf16[2,64,896]{2,1,0:T(8,128)(2,1)} %pad_maximum_fusion.19), channel_id=1, source_target_pairs={{0,8},{4,12},{8,0},{12,4},{16,24},{20,28},{24,16},{28,20},{1,9},{5... | collective-permute-start | bytes 688136 | tf_op jit(solution)/shard_map/ppermute | solution.py:50
  39.9 66.6 %collective-permute-start.5 = (bf16[2,64,896]{2,1,0:T(8,128)(2,1)}, bf16[2,64,896]{2,1,0:T(8,128)(2,1)}, u32[]{:S(2)}, u32[]{:S(2)}) collective-permute-start(bf16[2,64,896]{2,1,0:T(8,128)(2,1)} %pad_maximum_fusion.20), channel_id=1, source_target_pairs={{0,16},{4,20},{8,24},{12,28},{16,0},{20,4},{24,8},{28,12},{1,17},{... | collective-permute-start | bytes 688136 | tf_op jit(solution)/shard_map/ppermute | solution.py:50
  69.9 39.1 %collective-permute-start.6 = (bf16[2,64,896]{2,1,0:T(8,128)(2,1)}, bf16[2,64,896]{2,1,0:T(8,128)(2,1)}, u32[]{:S(2)}, u32[]{:S(2)}) collective-permute-start(bf16[2,64,896]{2,1,0:T(8,128)(2,1)} %pad_maximum_fusion.21), channel_id=1, source_target_pairs={{0,24},{4,28},{8,16},{12,20},{16,8},{20,12},{24,0},{28,4},{1,25},{... | collective-permute-start | bytes 688136 | tf_op jit(solution)/shard_map/ppermute | solution.py:50
  112.1 221.4 %reduce-scatter.4.cloned.1.call-start = ((), (), s32[]{:S(2)}) async-start(), calls=%async_computation.4 | async-start | bytes 4587520 | tf_op jit(solution)/shard_map/reduce_scatter | solution.py:1194
  154.3 25.5 %collective-permute-start.10 = (bf16[128,2048]{1,0:T(8,128)(2,1)}, bf16[128,2048]{1,0:T(8,128)(2,1)S(1)}, u32[]{:S(2)}, u32[]{:S(2)}) collective-permute-start(bf16[128,2048]{1,0:T(8,128)(2,1)} %get-tuple-element.307), channel_id=1, source_target_pairs={{0,16},{4,20},{8,24},{12,28},{16,0},{20,4},{24,8},{28,12},{1,17},{... | collective-permute-start | bytes 1572872 | tf_op jit(solution)/shard_map/ppermute | solution.py:50
  156.1 23.7 %collective-permute-start.11 = (bf16[128,2048]{1,0:T(8,128)(2,1)}, bf16[128,2048]{1,0:T(8,128)(2,1)}, u32[]{:S(2)}, u32[]{:S(2)}) collective-permute-start(bf16[128,2048]{1,0:T(8,128)(2,1)} %get-tuple-element.306), channel_id=1, source_target_pairs={{0,24},{4,28},{8,16},{12,20},{16,8},{20,12},{24,0},{28,4},{1,25},{... | collective-permute-start | bytes 1572872 | tf_op jit(solution)/shard_map/ppermute | solution.py:50
  157.5 23.6 %collective-permute-start.9 = (bf16[128,2048]{1,0:T(8,128)(2,1)S(1)}, bf16[128,2048]{1,0:T(8,128)(2,1)}, u32[]{:S(2)}, u32[]{:S(2)}) collective-permute-start(bf16[128,2048]{1,0:T(8,128)(2,1)S(1)} %get-tuple-element.305), channel_id=1, source_target_pairs={{0,8},{4,12},{8,0},{12,4},{16,24},{20,28},{24,16},{28,20},{1,9},{5... | collective-permute-start | bytes 1572872 | tf_op jit(solution)/shard_map/ppermute | solution.py:50
  266.6 175.3 %reduce-scatter.6.cloned.1.call-start = ((), (), s32[]{:S(2)}) async-start(), calls=%async_computation.5 | async-start | bytes 5898240 | tf_op jit(solution)/shard_map/reduce_scatter | solution.py:298
  275.6 23.9 %collective-permute-start.29 = (bf16[1024,256]{1,0:T(8,128)(2,1)S(1)}, bf16[1024,256]{1,0:T(8,128)(2,1)S(1)}, u32[]{:S(2)}, u32[]{:S(2)}) collective-permute-start(bf16[1024,256]{1,0:T(8,128)(2,1)S(1)} %get-tuple-element.219), channel_id=1, source_target_pairs={{0,16},{4,20},{8,24},{12,28},{16,0},{20,4},{24,8},{28,12},{1,17},{... | collective-permute-start | bytes 1572872 | tf_op jit(solution)/shard_map/ppermute | solution.py:50
  277.1 23.5 %collective-permute-start.30 = (bf16[1024,256]{1,0:T(8,128)(2,1)S(1)}, bf16[1024,256]{1,0:T(8,128)(2,1)S(1)}, u32[]{:S(2)}, u32[]{:S(2)}) collective-permute-start(bf16[1024,256]{1,0:T(8,128)(2,1)S(1)} %get-tuple-element.220), channel_id=1, source_target_pairs={{0,24},{4,28},{8,16},{12,20},{16,8},{20,12},{24,0},{28,4},{1,25},{... | collective-permute-start | bytes 1572872 | tf_op jit(solution)/shard_map/ppermute | solution.py:50
  332.0 184.6 %all-gather.9.cloned.1.call-start = ((), (), s32[]{:S(2)}) async-start(), calls=%async_computation.6 | async-start | bytes 4587520 | tf_op jit(solution)/shard_map/all_gather | solution.py:302
  344.8 33.9 %collective-permute-start.36 = (bf16[128,2048]{1,0:T(8,128)(2,1)S(1)}, bf16[128,2048]{1,0:T(8,128)(2,1)S(1)}, u32[]{:S(2)}, u32[]{:S(2)}) collective-permute-start(bf16[128,2048]{1,0:T(8,128)(2,1)S(1)} %get-tuple-element.302), channel_id=1, source_target_pairs={{0,8},{4,12},{8,0},{12,4},{16,24},{20,28},{24,16},{28,20},{1,9},{5... | collective-permute-start | bytes 1572872 | tf_op jit(solution)/shard_map/ppermute | solution.py:50
  346.0 32.7 %collective-permute-start.37 = (bf16[128,2048]{1,0:T(8,128)(2,1)S(1)}, bf16[128,2048]{1,0:T(8,128)(2,1)S(1)}, u32[]{:S(2)}, u32[]{:S(2)}) collective-permute-start(bf16[128,2048]{1,0:T(8,128)(2,1)S(1)} %get-tuple-element.304), channel_id=1, source_target_pairs={{0,16},{4,20},{8,24},{12,28},{16,0},{20,4},{24,8},{28,12},{1,17},{... | collective-permute-start | bytes 1572872 | tf_op jit(solution)/shard_map/ppermute | solution.py:50
  347.5 31.2 %collective-permute-start.38 = (bf16[128,2048]{1,0:T(8,128)(2,1)S(1)}, bf16[128,2048]{1,0:T(8,128)(2,1)S(1)}, u32[]{:S(2)}, u32[]{:S(2)}) collective-permute-start(bf16[128,2048]{1,0:T(8,128)(2,1)S(1)} %get-tuple-element.303), channel_id=1, source_target_pairs={{0,24},{4,28},{8,16},{12,20},{16,8},{20,12},{24,0},{28,4},{1,25},{... | collective-permute-start | bytes 1572872 | tf_op jit(solution)/shard_map/ppermute | solution.py:50
  348.4 24.4 %collective-permute-start.32 = (bf16[128,512]{1,0:T(8,128)(2,1)S(1)}, bf16[128,512]{1,0:T(8,128)(2,1)S(1)}, u32[]{:S(2)}, u32[]{:S(2)}) collective-permute-start(bf16[128,512]{1,0:T(8,128)(2,1)S(1)} %get-tuple-element.355), channel_id=1, source_target_pairs={{0,8},{4,12},{8,0},{12,4},{16,24},{20,28},{24,16},{28,20},{1,9},{5... | collective-permute-start | bytes 393224 | tf_op jit(solution)/shard_map/ppermute | solution.py:50
  349.6 25.3 %collective-permute-start.33 = (bf16[128,512]{1,0:T(8,128)(2,1)S(1)}, bf16[128,512]{1,0:T(8,128)(2,1)S(1)}, u32[]{:S(2)}, u32[]{:S(2)}) collective-permute-start(bf16[128,512]{1,0:T(8,128)(2,1)S(1)} %get-tuple-element.354), channel_id=1, source_target_pairs={{0,16},{4,20},{8,24},{12,28},{16,0},{20,4},{24,8},{28,12},{1,17},{... | collective-permute-start | bytes 393224 | tf_op jit(solution)/shard_map/ppermute | solution.py:50
  384.8 221.6 %reduce-scatter.8.cloned.1.call-start = ((), (), s32[]{:S(2)}) async-start(), calls=%async_computation.7 | async-start | bytes 6553600 | tf_op jit(solution)/shard_map/reduce_scatter | solution.py:298
  458.1 244.1 %all-gather.13.cloned.1.call-start = ((), (), s32[]{:S(2)}) async-start(), calls=%async_computation.9 | async-start | bytes 5898240 | tf_op jit(solution)/shard_map/all_gather | solution.py:302
  462.5 54.1 %collective-permute-start.47 = (bf16[2,64,1152]{2,1,0:T(8,128)(2,1)S(1)}, bf16[2,64,1152]{2,1,0:T(8,128)(2,1)S(1)}, u32[]{:S(2)}, u32[]{:S(2)}) collective-permute-start(bf16[2,64,1152]{2,1,0:T(8,128)(2,1)S(1)} %pad_maximum_fusion.14), channel_id=1, source_target_pairs={{0,24},{4,28},{8,16},{12,20},{16,8},{20,12},{24,0},{28,4},{1,25},{... | collective-permute-start | bytes 884744 | tf_op jit(solution)/shard_map/ppermute | solution.py:50
  464.0 52.6 %collective-permute-start.46 = (bf16[2,64,1152]{2,1,0:T(8,128)(2,1)S(1)}, bf16[2,64,1152]{2,1,0:T(8,128)(2,1)S(1)}, u32[]{:S(2)}, u32[]{:S(2)}) collective-permute-start(bf16[2,64,1152]{2,1,0:T(8,128)(2,1)S(1)} %pad_maximum_fusion.13), channel_id=1, source_target_pairs={{0,16},{4,20},{8,24},{12,28},{16,0},{20,4},{24,8},{28,12},{1,17},{... | collective-permute-start | bytes 884744 | tf_op jit(solution)/shard_map/ppermute | solution.py:50
  466.3 50.3 %collective-permute-start.45 = (bf16[2,64,1152]{2,1,0:T(8,128)(2,1)}, bf16[2,64,1152]{2,1,0:T(8,128)(2,1)S(1)}, u32[]{:S(2)}, u32[]{:S(2)}) collective-permute-start(bf16[2,64,1152]{2,1,0:T(8,128)(2,1)} %pad_maximum_fusion.12), channel_id=1, source_target_pairs={{0,8},{4,12},{8,0},{12,4},{16,24},{20,28},{24,16},{28,20},{1,9},{5... | collective-permute-start | bytes 884744 | tf_op jit(solution)/shard_map/ppermute | solution.py:50
  519.0 281.9 %all-gather.11.cloned.1.call-start = ((), (), s32[]{:S(2)}) async-start(), calls=%async_computation.8 | async-start | bytes 6553600 | tf_op jit(solution)/shard_map/all_gather | solution.py:302
  546.0 31.1 %collective-permute-start.57 = (bf16[464,256]{1,0:T(8,128)(2,1)S(1)}, bf16[464,256]{1,0:T(8,128)(2,1)S(1)}, u32[]{:S(2)}, u32[]{:S(2)}) collective-permute-start(bf16[464,256]{1,0:T(8,128)(2,1)S(1)} %pad_maximum_fusion.18), channel_id=1, source_target_pairs={{0,2},{1,3},{2,0},{3,1},{4,6},{5,7},{6,4},{7,5},{8,10},{9,11},{10,... | collective-permute-start | bytes 712712 | tf_op jit(solution)/shard_map/ppermute | solution.py:386
  548.0 29.1 %collective-permute-start.58 = (bf16[464,256]{1,0:T(8,128)(2,1)S(1)}, bf16[464,256]{1,0:T(8,128)(2,1)S(1)}, u32[]{:S(2)}, u32[]{:S(2)}) collective-permute-start(bf16[464,256]{1,0:T(8,128)(2,1)S(1)} %pad_maximum_fusion.18), channel_id=1, source_target_pairs={{0,3},{1,0},{2,1},{3,2},{4,7},{5,4},{6,5},{7,6},{8,11},{9,8},{10,9... | collective-permute-start | bytes 712712 | tf_op jit(solution)/shard_map/ppermute | solution.py:386
  580.1 22.8 %collective-permute-start.61 = (bf16[464,512]{1,0:T(8,128)(2,1)S(1)}, bf16[464,512]{1,0:T(8,128)(2,1)S(1)}, u32[]{:S(2)}, u32[]{:S(2)}) collective-permute-start(bf16[464,512]{1,0:T(8,128)(2,1)S(1)} %get-tuple-element.289), channel_id=1, source_target_pairs={{0,16},{4,20},{8,24},{12,28},{16,0},{20,4},{24,8},{28,12},{1,17},{... | collective-permute-start | bytes 1425416 | tf_op jit(solution)/shard_map/ppermute | solution.py:50
  636.5 24.9 %collective-permute-start.50 = (bf16[128,2048]{1,0:T(8,128)(2,1)S(1)}, bf16[128,2048]{1,0:T(8,128)(2,1)S(1)}, u32[]{:S(2)}, u32[]{:S(2)}) collective-permute-start(bf16[128,2048]{1,0:T(8,128)(2,1)S(1)} %get-tuple-element.301), channel_id=1, source_target_pairs={{0,16},{4,20},{8,24},{12,28},{16,0},{20,4},{24,8},{28,12},{1,17},{... | collective-permute-start | bytes 1572872 | tf_op jit(solution)/shard_map/ppermute | solution.py:50
  637.4 24.1 %collective-permute-start.51 = (bf16[128,2048]{1,0:T(8,128)(2,1)S(1)}, bf16[128,2048]{1,0:T(8,128)(2,1)S(1)}, u32[]{:S(2)}, u32[]{:S(2)}) collective-permute-start(bf16[128,2048]{1,0:T(8,128)(2,1)S(1)} %get-tuple-element.300), channel_id=1, source_target_pairs={{0,24},{4,28},{8,16},{12,20},{16,8},{20,12},{24,0},{28,4},{1,25},{... | collective-permute-start | bytes 1572872 | tf_op jit(solution)/shard_map/ppermute | solution.py:50
  (141 other events, 1748.2 us)
Sparse Core Ops, SparseCore 0:
  9.9 50.7 all-gather.14
  112.2 73.5 all-gather.6
  266.8 66.7 reduce-scatter.3
  336.2 85.5 reduce-scatter.5
  423.3 72.6 all-gather.8
  498.7 107.6 reduce-scatter.7
  608.5 93.5 all-gather.12
  704.3 96.5 all-gather.10

commit v4 on v3

--- a/solution.py
+++ b/solution.py
@@ -381,9 +381,12 @@
 
 def rep_sum(v):
     n = lax.axis_size("rep")
-    total = v.astype(F32)
-    for s in range(1, n):
-        total = total + lax.ppermute(v, "rep", [(i, (i + s) % n) for i in range(n)]).astype(F32)
+    if n & (n - 1):
+        return lax.psum(v, "rep").astype(F32)
+    total, step = v.astype(F32), 1
+    while step < n:
+        got = lax.ppermute(total.astype(v.dtype), "rep", [(i, i ^ step) for i in range(n)])
+        total, step = total + got.astype(F32), step * 2
     return total
 
 
@@ -436,19 +439,21 @@
     return center * lax.rsqrt(spread + norm_eps)
 
 
-def front_kernel(
-    ranks, order, tok, gain, shift, lerp, narrow, widen, fnarrow, xk, xv, xr, xg, hid, low, nh, nl, wb, fh, fl
-):
+def front_kernel(ranks, length, count, order, *refs):
+    tokens, (gain, shift, lerp, narrow, widen, fnarrow) = refs[:count], refs[count : count + 6]
+    xk, xv, xr, xg, hid, low, nw, wb, fw = refs[count + 6 :]
+    fd = low.shape[1]
+
     @pl.when(pl.program_id(0) == 0)
     def _():
-        nh[...], nl[...] = halves(jnp.transpose(narrow[...]))
-        fh[...], fl[...] = halves(jnp.transpose(fnarrow[...]))
+        nw[...] = jnp.transpose(narrow[...]).astype(BF)
         wb[...] = widen[...].astype(BF)
-
-    normed = normal_rows(tok[...].astype(F32)) * gain[...] + shift[...]
-    delta = shifted(normed) - normed
-    bh, bl = halves(normed + delta * lerp[0:1, :])
-    hidden = jnp.tanh(mm(bh, nh[...]) + mm(bh, nl[...]) + mm(bl, nh[...]))
+        fw[:, :fd], fw[:, fd:] = halves(jnp.transpose(fnarrow[...]))
+
+    tok = jnp.concatenate([t[...].astype(F32) for t in tokens], axis=0)
+    normed = normal_rows(tok) * gain[...] + shift[...]
+    delta = step_shift(length, normed) - normed
+    hidden = jnp.tanh(mm((normed + delta * lerp[0:1, :]).astype(BF), nw[...]))
     hid[...] = hidden
     hb = hidden.astype(BF)
     for f, out in ((1, xk), (2, xv), (3, xr), (4, xg), (0, None)):
@@ -458,7 +463,8 @@
             out[...] = x.astype(BF)
         else:
             dh, dl = halves(x)
-            low[...] = jnp.tanh(mm(dh, fh[...]) + mm(dh, fl[...]) + mm(dl, fh[...]))
+            pre = mm(dh, fw[...])
+            low[...] = jnp.tanh(pre[:, :fd] + pre[:, fd:] + mm(dl, fw[:, :fd]))
 
 
 def ordered_rows(seq_len, d, seqs):
@@ -470,21 +476,30 @@
     ranks = widen.shape[0] // 5
     fd = fnarrow.shape[0]
     order = orders()
-    per_seq = lambda w: pl.BlockSpec((seq_len, w), lambda s, o: (s, 0))
+    seqs = g // seq_len // order.shape[0]
+    count = 2 if g % (2 * seq_len) == 0 else 1
+    rows = count * seq_len
+    block = lambda w: pl.BlockSpec((rows, w), lambda s, o: (s, 0))
+
+    def sequence(i):
+        def at(s, o):
+            q = s * count + i
+            return (o[q // seqs] * seqs + lax.rem(q, seqs), 0)
+
+        return pl.BlockSpec((seq_len, d), at)
+
     return pl.pallas_call(
-        functools.partial(front_kernel, ranks),
+        functools.partial(front_kernel, ranks, seq_len, count),
         grid_spec=pltpu.PrefetchScalarGridSpec(
             num_scalar_prefetch=1,
-            grid=(g // seq_len,),
-            in_specs=[ordered_rows(seq_len, d, g // seq_len // order.shape[0])]
+            grid=(g // rows,),
+            in_specs=[sequence(i) for i in range(count)]
             + [whole_block(a) for a in (gain, shift, lerp, narrow, widen, fnarrow)],
-            out_specs=[per_seq(d)] * 4 + [per_seq(5 * ranks), per_seq(fd)],
+            out_specs=[block(d)] * 4 + [block(5 * ranks), block(fd)],
             scratch_shapes=[
                 pltpu.VMEM((d, 5 * ranks), BF),
-                pltpu.VMEM((d, 5 * ranks), BF),
                 pltpu.VMEM((5 * ranks, d), BF),
-                pltpu.VMEM((d, fd), BF),
-                pltpu.VMEM((d, fd), BF),
+                pltpu.VMEM((d, 2 * fd), BF),
             ],
         ),
         out_shape=[jax.ShapeDtypeStruct((g, d), BF)] * 4
@@ -495,7 +510,7 @@
         compiler_params=pltpu.CompilerParams(vmem_limit_bytes=48 * MIB),
         cost_estimate=SHORT,
         name="token_shift",
-    )(order, tokens, gain, shift, lerp, narrow, widen, fnarrow)
+    )(order, *[tokens] * count, gain, shift, lerp, narrow, widen, fnarrow)
 
 
 def back_kernel(
@@ -666,8 +681,7 @@
 def mix_forward(levels, count, width, r, k, v, w, u, spans, level):
     length, lanes_n = r.shape
     lanes = lax.broadcasted_iota(jnp.int32, (length, lanes_n), 1) // width
-    wh, wl = halves(w)
-    gaps = mm(spans, wh) + mm(spans, wl)
+    gaps = mm(spans, jnp.concatenate(halves(w), axis=0))
     factors = [None] + [
         jnp.exp(gaps[l * length : (l + 1) * length]) for l in range(levels - 1)
     ]
@@ -741,7 +755,8 @@
     width = c // heads_here
     count = 2 if heads_here % 2 == 0 else 1
     levels, spans, level = level_tables(seq_len)
-    spans_a, level_a = jnp.asarray(spans, BF), jnp.asarray(level)
+    spans_a = jnp.asarray(np.concatenate([spans, spans], axis=1), BF)
+    level_a = jnp.asarray(level)
     steps = half // seq_len
     block = lambda w: pl.BlockSpec((seq_len, w), lambda s: (s, 0))
     base, u, gain, bias = vectors
@@ -759,7 +774,7 @@
         out_shape=[shape(c, F32)] * 5
         + [shape(c, BF)]
         + [jax.ShapeDtypeStruct((half, d), BF)] * 2,
-        compiler_params=pltpu.CompilerParams(vmem_limit_bytes=48 * MIB),
+        compiler_params=pltpu.CompilerParams(vmem_limit_bytes=28 * MIB),
         cost_estimate=lasts(20),
         name="decay_mix",
     )(*xs, low, *kept)
@@ -862,7 +877,7 @@
     count = 2 if heads_here % 2 == 0 else 1
     lanes = count * width
     levels, spans, level = level_tables(seq_len)
-    spans_a = jnp.asarray(spans, BF)
+    spans_a = jnp.asarray(np.concatenate([spans, spans], axis=1), BF)
     level_a = jnp.asarray(level)
     cols = pl.BlockSpec((seq_len, lanes), lambda p, s: (s, p))
     vec = pl.BlockSpec((1, lanes), lambda p, s: (0, p))
@@ -893,8 +908,8 @@
     return jnp.where(edge, 0.0, pltpu.roll(v, rows - 1 if back else 1, 0))
 
 
-def feed_kernel(length, own_order, order, n2, lerp, wl, wc, *refs):
-    kc_out, sq_out, fac_out, near_out, far_out = refs[-5:]
+def feed_kernel(length, n2, lerp, wl, *refs):
+    kc_out, sq_out, fac_out = refs[-3:]
     n = n2[...].astype(F32)
     delta = step_shift(length, n) - n
     kc = (n + delta * lerp[0:1, :]).astype(BF)
@@ -902,42 +917,59 @@
     act = mm(kc, wl[...])
     soft = jnp.maximum(act, 0.0) + jnp.log1p(jnp.exp(-jnp.abs(act)))
     fac_out[...] = 2.0 * soft * jax.nn.sigmoid(act)
-    sq = (soft * soft).astype(BF)
-    sq_out[...] = sq
+    sq_out[...] = (soft * soft).astype(BF)
+
+
+def feed(length, n2, lerp, wl, part, earlier=()):
+    g, d = n2.shape
+    f = wl.shape[1]
+    half = g // 2
+    rows = 2 * length if half % (2 * length) == 0 else length
+    first = part * (half // rows)
+    block = lambda w: pl.BlockSpec((rows, w), lambda s: (first + s, 0))
+    shape = lambda w, t: jax.ShapeDtypeStruct((g, w), t)
+    return pl.pallas_call(
+        functools.partial(feed_kernel, length),
+        grid=(half // rows,),
+        in_specs=[block(d), whole_block(lerp), whole_block(wl)]
+        + [pl.BlockSpec(memory_space=pl.ANY)] * len(earlier),
+        out_specs=[block(d), block(f), block(f)],
+        out_shape=[shape(d, BF), shape(f, BF), shape(f, F32)],
+        input_output_aliases={3 + i: i for i in range(len(earlier))},
+        compiler_params=pltpu.CompilerParams(vmem_limit_bytes=52 * MIB),
+        cost_estimate=lasts(6),
+        name="feed",
+    )(n2, lerp, wl, *earlier)
+
+
+def value_kernel(own_order, order, sq, wc, near_out, far_out):
     some, _, c = near_out.shape
     for i in range(2 * some):
         at = pl.ds(pl.multiple_of(order[i] * c, c), c) if own_order else slice(i * c, (i + 1) * c)
         out = near_out if i < some else far_out
-        out[i % some] = mm(sq, wc[:, at]).astype(BF)
-
-
-def feed(length, n2, lerp, wl, wc, part, earlier=()):
-    g, d = n2.shape
-    f = wc.shape[0]
+        out[i % some] = mm(sq[...], wc[:, at]).astype(BF)
+
+
+def value_product(length, sq, wc, part):
+    g, f = sq.shape
+    d = wc.shape[1]
     n = lax.axis_size("fsdp")
     half = g // 2
     rows = 2 * length if half % (2 * length) == 0 else length
     first = part * (half // rows)
-    block = lambda w: pl.BlockSpec((rows, w), lambda s, o: (first + s, 0))
-    shape = lambda w, t: jax.ShapeDtypeStruct((g, w), t)
     return pl.pallas_call(
-        functools.partial(feed_kernel, length, paired()),
+        functools.partial(value_kernel, paired()),
         grid_spec=pltpu.PrefetchScalarGridSpec(
             num_scalar_prefetch=1,
             grid=(half // rows,),
-            in_specs=[block(d)]
-            + [whole_block(a) for a in (lerp, wl, wc)]
-            + [pl.BlockSpec(memory_space=pl.ANY)] * len(earlier),
-            out_specs=[block(d), block(f), block(f)]
-            + [pl.BlockSpec((n // 2, rows, d // n), lambda s, o: (0, s, 0))] * 2,
+            in_specs=[pl.BlockSpec((rows, f), lambda s, o: (first + s, 0)), whole_block(wc)],
+            out_specs=[pl.BlockSpec((n // 2, rows, d // n), lambda s, o: (0, s, 0))] * 2,
         ),
-        out_shape=[shape(d, BF), shape(f, BF), shape(f, F32)]
-        + [jax.ShapeDtypeStruct((n // 2, half, d // n), BF)] * 2,
-        input_output_aliases={5 + i: i for i in range(len(earlier))},
-        compiler_params=pltpu.CompilerParams(vmem_limit_bytes=52 * MIB),
-        cost_estimate=lasts(8),
-        name="feed",
-    )(orders(), n2, lerp, wl, wc, *earlier)
+        out_shape=[jax.ShapeDtypeStruct((n // 2, half, d // n), BF)] * 2,
+        compiler_params=pltpu.CompilerParams(vmem_limit_bytes=40 * MIB),
+        cost_estimate=lasts(4),
+        name="value_product",
+    )(orders(), sq, wc)
 
 
 def pair_kernel(near0, near1, got0, got1, *outs):
@@ -1107,13 +1139,6 @@
     fd = fading_narrow_weights.shape[1]
 
     tok_home = incoming_symbols.reshape(home, d)
-    z = lax.axis_index("rep")
-    share = c // lax.axis_size("rep")
-    lookup_quarter = Exchange(
-        [lax.dynamic_slice_in_dim(feed_lookup_weights, z * share, share, 0)], 1
-    )
-    lookup_quarter.across_cores()
-    lookup_quarter.across_chips()
     tokens = lax.all_gather(tok_home, "fsdp", axis=0, tiled=True)
     mix_weights = Exchange(
         (
@@ -1121,7 +1146,6 @@
             content_weights,
             acceptor_weights,
             valve_weights,
-            feed_acceptor_weights,
         ),
         1,
     )
@@ -1137,16 +1161,15 @@
     gain1, shift1 = row(first_scaling_factor), row(first_scaling_shift)
     narrow, fnarrow = lerp_narrow_weights.T, fading_narrow_weights.T
     widen = lerp_widen_weights.reshape(5 * ranks, d)
-    (tokens,) = mix_weights.arrived(tokens, count=2)
+    feed_weights = Exchange([feed_lookup_weights, feed_acceptor_weights], 1)
+    feed_weights.across_cores()
+    (tokens,) = feed_weights.after(*mix_weights.arrived(tokens, count=2))
     xk, xv, xr, xg, hidden, low = front(
         length, tokens, gain1, shift1, lerp_factors, narrow, widen, fnarrow
     )
-    (low,) = mix_weights.arrived(*lookup_quarter.arrived(low))
-    (lookup_share,) = lookup_quarter.results()
-    low, lookup_share = hold(low, lookup_share)
-    wl = lax.all_gather(lookup_share.reshape(n, share, -1), "rep", axis=1, tiled=True)
-    wl = wl.reshape(d, -1)
-    wk, wv, wr, wg, wa = mix_weights.results()
+    (low,) = feed_weights.after(*mix_weights.arrived(low))
+    feed_weights.across_chips()
+    wk, wv, wr, wg = mix_weights.results()
     fwiden_mine = mine(fading_widen_weights)
     base, u, gn_gain, gn_bias = (
         mine(row(t))
@@ -1166,7 +1189,9 @@
         (base, u, gn_gain, gn_bias),
         fwiden_mine,
     )
+    near, far = feed_weights.arrived(near, far)
     branch = scatter_tokens(near, far)
+    wl, wa = feed_weights.results()
     branch, wl, wa = hold(branch, wl, wa)
     branch, adjoint = hold(branch, adjoint)
     adjoint_cols = spread_features(adjoint)
@@ -1182,27 +1207,25 @@
     recept_chan, gate, d_value_mine = feed_gate(
         length, normed2, adjoint_cols, feed_lerp_factors, wa
     )
-    feed_part = lambda *t: feed(length, normed2, feed_lerp_factors, wl, feed_content_weights, *t)
-
-    def second_part(*done):
-        return (*feed_part(1, done[:3]), *done[3:])
-
-    d_value, held = gather_features_of_tokens(d_value_mine, (lambda: feed_part(0), second_part))
-    key_chan, squared, factor, *values = held
+    feed_part = lambda *t: feed(length, normed2, feed_lerp_factors, wl, *t)
+    d_value, (key_chan, squared, factor) = gather_features_of_tokens(
+        d_value_mine, (lambda: feed_part(0), lambda *done: feed_part(1, done))
+    )
     d_content = mm_tn(squared, d_value).astype(BF)
-    d_value, d_content, *values = hold(d_value, d_content, *values)
-    content_share = lax.psum_scatter(d_content, "rep", scatter_dimension=0, tiled=True)
-    gated, d_gate = gated_value(adjoint_cols, gate, (values[2:], values[:2]))
+    d_value, d_content, squared = hold(d_value, d_content, squared)
+    content_share = rep_scatter(d_content)
+    value_part = lambda part: value_product(length, squared, feed_content_weights, part)
+    gated, d_gate = gated_value(adjoint_cols, gate, (value_part(0), value_part(1)))
 
     d_key, d_normed2, feed_lerp_part = feed_back(
         length, d_value, normed2, factor, d_gate, feed_lerp_factors, wl, wa, feed_content_weights
     )
     d_normed2, content_share = hold(d_normed2, content_share)
+    content_sum = rep_gather(content_share)
     feed_share = rep_scatter_cols(
         (mm_tn(key_chan, d_key).astype(BF), mm_tn(recept_chan, d_gate).astype(BF))
     )
     d_normed2 = scatter_tokens(d_normed2[: plane // 2], d_normed2[plane // 2 :])
-    content_sum = rep_gather(content_share)
 
     def norm_back(unit, rstd, e):
         return rstd * (

time: 821 us -> 800 us (0.974)
  Pallas kernels: 214 us -> 199 us
    all_gather x3, waiting for transfers between devices: 126 us -> 107 us  [rep_gather(): return lax.all_gather(v, 'rep', axis=0, tiled=True)]
    ppermute x3 -> x2, waiting for transfers between devices: 26 us -> 41.9 us  [rep_sum(): lax.ppermute(total.astype(v.dtype), 'rep', [(i, i ^ step) for i in range(...]
    ppermute x64, waiting for transfers between devices: 229 us -> 240 us  [swap(): return lax.ppermute(v, 'fsdp', [(i, i ^ m) for i in range(8)])]
    pallas_call x3 -> x5, Pallas kernels: 49.4 us -> 38.4 us  [the longest x1 18.2 us: front(): pl.pallas_call(functools.partial(front_kernel, ranks, seq_len, count), gr...]
    unnamed x223 -> x231, local copies, waits for them, and re-layouts: 46.2 us -> 46.9 us
  transfers between devices with their start and end apart: 75 -> 73, of which waited for: 50 -> 47; matrix products, arithmetic and copies ran while one was open for 9% -> 8% of each run, Pallas kernels for 25% -> 24%
where the time goes in v4:
time: 800 us; the launch traced here: 791 us
  waiting for transfers between devices  390 us (49%)
  Pallas kernels  199 us (25%)
  local copies, waits for them, and re-layouts  69 us (9%)
  starting transfers between devices  64.1 us (8%)
  other arithmetic  25.8 us (3%)
  matrix products  25.6 us (3%)
  between operations  17.2 us (2%)
    ppermute x64, waiting for transfers between devices, swap(): return lax.ppermute(v, 'fsdp', [(i, i ^ m) for i in range(8)])  240 us
    all_gather x3, waiting for transfers between devices, rep_gather(): return lax.all_gather(v, 'rep', axis=0, tiled=True)  107 us
    ppermute x64, starting transfers between devices, swap(): return lax.ppermute(v, 'fsdp', [(i, i ^ m) for i in range(8)])  60.3 us
    pallas_call x1, Pallas kernels, back(): pl.pallas_call(functools.partial(back_kernel, ranks), grid_spec=pltpu.Pre...  49.6 us
    unnamed x231, local copies, waits for them, and re-layouts  46.9 us
    ppermute x2, waiting for transfers between devices, rep_sum(): lax.ppermute(total.astype(v.dtype), 'rep', [(i, i ^ step) for i in range(...  41.9 us
    pallas_call x1, Pallas kernels, mix_back(): pl.pallas_call(functools.partial(wkv_back_kernel, levels, count, width),...  29.2 us
    dot_general x9, matrix products, mm_tn(): lax.dot_general(a, b, (((0,), (0,)), ((), ())), preferred_element_type=F32)  24.3 us
  transfers between devices with their start and end apart: 73, of which 47 were waited for; matrix products, arithmetic and copies ran while one was open for 8% of the time, Pallas kernels for 24%

profile of v4, /device:TPU:0, one launch (start us, length us, event | category | flops | bytes accessed | tf_op | source)
XLA Modules:
  0.0 790.7 jit_solution(15117372650921694852)
XLA Ops:
  32.5 30.1 %collective-permute-done.2.refs_2_.refs_6_ = bf16[2,256,1024]{2,1,0:T(8,128)(2,1)} collective-permute-done((bf16[2,256,1024]{2,1,0:T(8,128)(2,1)}, bf16[2,256,1024]{2,1,0:T(8,128)(2,1)}, u32[]{:S(2)}, u32[]{:S(2)}) %collective-permute-start.2) | collective-permute-done | bytes 1048608 | tf_op jit(solution)/shard_map/ppermute | solution.py:50
  66.4 18.2 %token_shift.1 = (bf16[1024,2048]{1,0:T(8,128)(2,1)}, bf16[1024,2048]{1,0:T(8,128)(2,1)}, bf16[1024,2048]{1,0:T(8,128)(2,1)}, bf16[1024,2048]{1,0:T(8,128)(2,1)}...) custom-call(s32[8]{0:T(128)S(1)} %stack.26.order, bf16[1024,2048]{1,0:T(8,128)(2,1)} %bitcast.146, ...), custom_call_target="tpu_custom_call" | custom-call | flops 1 | bytes 1 | tf_op jit(solution)/shard_map/token_shift/pallas_call | solution.py:491
  99.1 20.0 %decay_mix.1 = (f32[1024,256]{1,0:T(8,128)S(1)}, f32[1024,256]{1,0:T(8,128)S(1)}, f32[1024,256]{1,0:T(8,128)S(1)}, f32[1024,256]{1,0:T(8,128)S(1)}, f32[1024,256...) custom-call(bf16[1024,2048]{1,0:T(8,128)(2,1)S(1)} %copy-done.68, ...), custom_call_target="tpu_custom_call" | custom-call | flops 20000000000 | bytes 1 | tf_op jit(solution)/shard_map/decay_mix/pallas_call | solution.py:765
  123.1 18.5 %collective-permute-done.6.refs_2_.refs_6_ = bf16[2,256,1152]{2,1,0:T(8,128)(2,1)S(1)} collective-permute-done((bf16[2,256,1152]{2,1,0:T(8,128)(2,1)S(1)}, bf16[2,256,1152]{2,1,0:T(8,128)(2,1)S(1)}, u32[]{:S(2)}, u32[]{:S(2)}) %collective-permute-start.6) | collective-permute-done | bytes 1179680 | tf_op jit(solution)/shard_map/ppermute | solution.py:50
  157.9 15.4 %collective-permute-done.10 = bf16[128,2048]{1,0:T(8,128)(2,1)} collective-permute-done((bf16[128,2048]{1,0:T(8,128)(2,1)}, bf16[128,2048]{1,0:T(8,128)(2,1)}, u32[]{:S(2)}, u32[]{:S(2)}) %collective-permute-start.10) | collective-permute-done | bytes 524320 | tf_op jit(solution)/shard_map/ppermute | solution.py:50
  194.5 7.6 collective-permute-done.18
  213.9 6.8 feed.2
  223.4 6.8 feed.3
  243.5 5.5 convolution_convert_fusion.1
  266.3 11.3 %collective-permute-done.28.refs_1_ = bf16[1024,256]{1,0:T(8,128)(2,1)S(1)} collective-permute-done((bf16[1024,256]{1,0:T(8,128)(2,1)S(1)}, bf16[1024,256]{1,0:T(8,128)(2,1)S(1)}, u32[]{:S(2)}, u32[]{:S(2)}) %collective-permute-start.28) | collective-permute-done | bytes 524320 | tf_op jit(solution)/shard_map/ppermute | solution.py:50
  277.6 11.1 %collective-permute-done.29.refs_2_ = bf16[1024,256]{1,0:T(8,128)(2,1)S(1)} collective-permute-done((bf16[1024,256]{1,0:T(8,128)(2,1)S(1)}, bf16[1024,256]{1,0:T(8,128)(2,1)S(1)}, u32[]{:S(2)}, u32[]{:S(2)}) %collective-permute-start.29) | collective-permute-done | bytes 524320 | tf_op jit(solution)/shard_map/ppermute | solution.py:50
  289.2 19.0 %feed_back.1 = (bf16[1024,896]{1,0:T(8,128)(2,1)}, bf16[1024,2048]{1,0:T(8,128)(2,1)}, f32[2,2048]{1,0:T(2,128)S(1)}) custom-call(bf16[1024,2048]{1,0:T(8,128)(2,1)} %copy-done.5, bf16[1024,2048]{1,0:T(8,128)(2,1)} %copy-done.3, f32[1024,896]{1,0:T(8,128)} %get-tuple-element.217.fac, bf16[1024,256]{1,0:T(8,128)(2,1)S(1)} %get-tuple-element.218.dgate, ...), custom_call_target="tpu_custom_call" | custom-call | flops 1 | bytes 1 | tf_op jit(solution)/shard_map/feed_back/pallas_call | solution.py:1088
  308.2 7.5 convolution_convert_fusion.refs_0_
  336.7 22.1 %collective-permute-done.32 = bf16[128,512]{1,0:T(8,128)(2,1)S(1)} collective-permute-done((bf16[128,512]{1,0:T(8,128)(2,1)S(1)}, bf16[128,512]{1,0:T(8,128)(2,1)S(1)}, u32[]{:S(2)}, u32[]{:S(2)}) %collective-permute-start.32) | collective-permute-done | bytes 131104 | tf_op jit(solution)/shard_map/ppermute | solution.py:50
  372.0 4.4 collective-permute-done.40
  378.7 10.3 %collective-permute-done.41 = bf16[128,2048]{1,0:T(8,128)(2,1)S(1)} collective-permute-done((bf16[128,2048]{1,0:T(8,128)(2,1)S(1)}, bf16[128,2048]{1,0:T(8,128)(2,1)S(1)}, u32[]{:S(2)}, u32[]{:S(2)}) %collective-permute-start.41) | collective-permute-done | bytes 524320 | tf_op jit(solution)/shard_map/ppermute | solution.py:50
  397.9 29.2 %decay_mix_back.1 = (bf16[1024,256]{1,0:T(8,128)(2,1)S(1)}, bf16[1024,256]{1,0:T(8,128)(2,1)S(1)}, bf16[1024,256]{1,0:T(8,128)(2,1)S(1)}, bf16[1024,256]{1,0:T(8...) custom-call(f32[1024,256]{1,0:T(8,128)S(1)} %copy-done.47, f32[1024,256]{1,0:T(8,128)S(1)} %copy-done.43, ...), custom_call_target="tpu_custom_call" | custom-call | flops 1 | bytes 1 | tf_op jit(solution)/shard_map/decay_mix_back/pallas_call | solution.py:889
  428.1 4.3 convolution_convert_fusion.3.refs_3_
  452.6 49.6 %token_shift_back.1 = (bf16[1024,2048]{1,0:T(8,128)(2,1)}, f32[8,2048]{1,0:T(8,128)}, f32[160,2048]{1,0:T(8,128)}, f32[160,2048]{1,0:T(8,128)}, f32[64,2048]{1,0:T(8,128)}) custom-call(s32[8]{0:T(128)} %copy-done.62, bf16[1024,2048]{1,0:T(8,128)(2,1)} %bitcast.148, f32[1024,160]{1,0:T(8,128)} %copy-done.37, f32[1024,64]{1,0:T(8,128)} %copy-done.29, ...), custom_call_target="tpu_custom_call" | custom-call | flops 1 | bytes 1 | tf_op jit(solution)/shard_map/token_shift_back/pallas_call | solution.py:612
  518.2 4.2 collective-permute-done.53
  527.8 16.4 %collective-permute-done.56 = bf16[464,256]{1,0:T(8,128)(2,1)S(1)} collective-permute-done((bf16[464,256]{1,0:T(8,128)(2,1)S(1)}, bf16[464,256]{1,0:T(8,128)(2,1)S(1)}, u32[]{:S(2)}, u32[]{:S(2)}) %collective-permute-start.56) | collective-permute-done | bytes 237600 | tf_op jit(solution)/shard_map/ppermute | solution.py:388
  546.6 25.4 %collective-permute-done.57 = bf16[464,256]{1,0:T(8,128)(2,1)S(1)} collective-permute-done((bf16[464,256]{1,0:T(8,128)(2,1)S(1)}, bf16[464,256]{1,0:T(8,128)(2,1)S(1)}, u32[]{:S(2)}, u32[]{:S(2)}) %collective-permute-start.57) | collective-permute-done | bytes 237600 | tf_op jit(solution)/shard_map/ppermute | solution.py:388
  577.6 10.2 %collective-permute-done.59 = bf16[464,512]{1,0:T(8,128)(2,1)S(1)} collective-permute-done((bf16[464,512]{1,0:T(8,128)(2,1)S(1)}, bf16[464,512]{1,0:T(8,128)(2,1)S(1)}, u32[]{:S(2)}, u32[]{:S(2)}) %collective-permute-start.59) | collective-permute-done | bytes 475168 | tf_op jit(solution)/shard_map/ppermute | solution.py:50
  587.9 10.5 %collective-permute-done.60 = bf16[464,512]{1,0:T(8,128)(2,1)S(1)} collective-permute-done((bf16[464,512]{1,0:T(8,128)(2,1)S(1)}, bf16[464,512]{1,0:T(8,128)(2,1)S(1)}, u32[]{:S(2)}, u32[]{:S(2)}) %collective-permute-start.60) | collective-permute-done | bytes 475168 | tf_op jit(solution)/shard_map/ppermute | solution.py:50
  609.2 6.1 collective-permute-done.65.refs_3_.refs_7_
  615.2 4.8 collective-permute-done.64.refs_2_.refs_6_
  633.0 10.2 %widened.5 = f32[896,2048]{1,0:T(8,128)} custom-call(bf16[896,2048]{1,0:T(8,128)(2,1)S(1)} %copy-done.26), custom_call_target="tpu_custom_call" | custom-call | flops 1 | bytes 1 | tf_op jit(solution)/shard_map/widened/pallas_call | solution.py:370
  645.0 10.6 %collective-permute-done.51 = bf16[128,2048]{1,0:T(8,128)(2,1)S(1)} collective-permute-done((bf16[128,2048]{1,0:T(8,128)(2,1)S(1)}, bf16[128,2048]{1,0:T(8,128)(2,1)S(1)}, u32[]{:S(2)}, u32[]{:S(2)}) %collective-permute-start.51) | collective-permute-done | bytes 524320 | tf_op jit(solution)/shard_map/ppermute | solution.py:50
  657.6 19.8 %all-gather.10.cloned.1.call-done.refs_0_ = bf16[256,9216]{1,0:T(8,128)(2,1)} async-done(((bf16[64,9216]{1,0:T(8,128)(2,1)}), bf16[256,9216]{1,0:T(8,128)(2,1)}) %all-gather.10.cloned.1.call-update) | async-done | bytes 4718608 | tf_op jit(solution)/shard_map/all_gather | solution.py:302
  679.7 4.6 widened.4
  689.1 86.9 %all-gather.8.cloned.1.call-done.refs_0_ = bf16[256,10240]{1,0:T(8,128)(2,1)} async-done(((bf16[64,10240]{1,0:T(8,128)(2,1)}), bf16[256,10240]{1,0:T(8,128)(2,1)}) %all-gather.8.cloned.1.call-update) | async-done | bytes 5242896 | tf_op jit(solution)/shard_map/all_gather | solution.py:302
  778.6 4.8 widened.3
  (507 shorter events, 261.3 us)
Async XLA Ops:
  7.2 56.6 %all-gather.12.cloned.1.call-start = ((), (), s32[]{:S(2)}) async-start(), calls=%async_computation.9 | async-start | bytes 4718592 | tf_op jit(solution)/shard_map/all_gather | solution.py:1142
  7.9 312.3 %reduce-scatter.4.cloned.1.call-start = ((), (), s32[]{:S(2)}) async-start(), calls=%async_computation.3 | async-start | bytes 4587520 | tf_op jit(solution)/shard_map/reduce_scatter | solution.py:298
  20.3 43.4 %collective-permute-start.3 = (bf16[4,256,1152]{2,1,0:T(8,128)(2,1)}, bf16[4,256,1152]{2,1,0:T(8,128)(2,1)}, u32[]{:S(2)}, u32[]{:S(2)}) collective-permute-start(bf16[4,256,1152]{2,1,0:T(8,128)(2,1)} %get-tuple-element.154), channel_id=1, source_target_pairs={{0,4},{4,0},{8,12},{12,8},{16,20},{20,16},{24,28},{28,24},{1,5},{5... | collective-permute-start | bytes 7077896 | tf_op jit(solution)/shard_map/ppermute | solution.py:50
  22.6 40.0 %collective-permute-start.2 = (bf16[2,256,1024]{2,1,0:T(8,128)(2,1)}, bf16[2,256,1024]{2,1,0:T(8,128)(2,1)}, u32[]{:S(2)}, u32[]{:S(2)}) collective-permute-start(bf16[2,256,1024]{2,1,0:T(8,128)(2,1)} %pad_maximum_fusion.5), channel_id=1, source_target_pairs={{0,16},{4,20},{8,24},{12,28},{16,0},{20,4},{24,8},{28,12},{1,17},{... | collective-permute-start | bytes 3145736 | tf_op jit(solution)/shard_map/ppermute | solution.py:50
  26.2 37.5 %collective-permute-start.1 = (bf16[2,256,1024]{2,1,0:T(8,128)(2,1)}, bf16[2,256,1024]{2,1,0:T(8,128)(2,1)}, u32[]{:S(2)}, u32[]{:S(2)}) collective-permute-start(bf16[2,256,1024]{2,1,0:T(8,128)(2,1)} %pad_maximum_fusion.4), channel_id=1, source_target_pairs={{0,8},{4,12},{8,0},{12,4},{16,24},{20,28},{24,16},{28,20},{1,9},{5... | collective-permute-start | bytes 3145736 | tf_op jit(solution)/shard_map/ppermute | solution.py:50
  28.8 56.9 %collective-permute-start.4 = (bf16[2,256,1024]{2,1,0:T(8,128)(2,1)}, bf16[2,256,1024]{2,1,0:T(8,128)(2,1)}, u32[]{:S(2)}, u32[]{:S(2)}) collective-permute-start(bf16[2,256,1024]{2,1,0:T(8,128)(2,1)} %pad_maximum_fusion.6), channel_id=1, source_target_pairs={{0,24},{4,28},{8,16},{12,20},{16,8},{20,12},{24,0},{28,4},{1,25},{... | collective-permute-start | bytes 3145736 | tf_op jit(solution)/shard_map/ppermute | solution.py:50
  87.5 35.6 %collective-permute-start.7 = (bf16[2,256,1152]{2,1,0:T(8,128)(2,1)S(1)}, bf16[2,256,1152]{2,1,0:T(8,128)(2,1)S(1)}, u32[]{:S(2)}, u32[]{:S(2)}) collective-permute-start(bf16[2,256,1152]{2,1,0:T(8,128)(2,1)S(1)} %pad_maximum_fusion.2), channel_id=1, source_target_pairs={{0,24},{4,28},{8,16},{12,20},{16,8},{20,12},{24,0},{28,4},{1,25},{... | collective-permute-start | bytes 3538952 | tf_op jit(solution)/shard_map/ppermute | solution.py:50
  90.0 51.6 %collective-permute-start.6 = (bf16[2,256,1152]{2,1,0:T(8,128)(2,1)S(1)}, bf16[2,256,1152]{2,1,0:T(8,128)(2,1)S(1)}, u32[]{:S(2)}, u32[]{:S(2)}) collective-permute-start(bf16[2,256,1152]{2,1,0:T(8,128)(2,1)S(1)} %pad_maximum_fusion.1), channel_id=1, source_target_pairs={{0,16},{4,20},{8,24},{12,28},{16,0},{20,4},{24,8},{28,12},{1,17},{... | collective-permute-start | bytes 3538952 | tf_op jit(solution)/shard_map/ppermute | solution.py:50
  90.7 50.8 %collective-permute-start.5 = (bf16[2,256,1152]{2,1,0:T(8,128)(2,1)S(1)}, bf16[2,256,1152]{2,1,0:T(8,128)(2,1)S(1)}, u32[]{:S(2)}, u32[]{:S(2)}) collective-permute-start(bf16[2,256,1152]{2,1,0:T(8,128)(2,1)S(1)} %pad_maximum_fusion), channel_id=1, source_target_pairs={{0,8},{4,12},{8,0},{12,4},{16,24},{20,28},{24,16},{28,20},{1,9},{5... | collective-permute-start | bytes 3538952 | tf_op jit(solution)/shard_map/ppermute | solution.py:50
  147.7 25.6 %collective-permute-start.10 = (bf16[128,2048]{1,0:T(8,128)(2,1)}, bf16[128,2048]{1,0:T(8,128)(2,1)}, u32[]{:S(2)}, u32[]{:S(2)}) collective-permute-start(bf16[128,2048]{1,0:T(8,128)(2,1)} %get-tuple-element.301), channel_id=1, source_target_pairs={{0,16},{4,20},{8,24},{12,28},{16,0},{20,4},{24,8},{28,12},{1,17},{... | collective-permute-start | bytes 1572872 | tf_op jit(solution)/shard_map/ppermute | solution.py:50
  148.5 24.7 %collective-permute-start.11 = (bf16[128,2048]{1,0:T(8,128)(2,1)}, bf16[128,2048]{1,0:T(8,128)(2,1)}, u32[]{:S(2)}, u32[]{:S(2)}) collective-permute-start(bf16[128,2048]{1,0:T(8,128)(2,1)} %get-tuple-element.300), channel_id=1, source_target_pairs={{0,24},{4,28},{8,16},{12,20},{16,8},{20,12},{24,0},{28,4},{1,25},{... | collective-permute-start | bytes 1572872 | tf_op jit(solution)/shard_map/ppermute | solution.py:50
  150.0 24.5 %collective-permute-start.9 = (bf16[128,2048]{1,0:T(8,128)(2,1)}, bf16[128,2048]{1,0:T(8,128)(2,1)}, u32[]{:S(2)}, u32[]{:S(2)}) collective-permute-start(bf16[128,2048]{1,0:T(8,128)(2,1)} %get-tuple-element.299), channel_id=1, source_target_pairs={{0,8},{4,12},{8,0},{12,4},{16,24},{20,28},{24,16},{28,20},{1,9},{5... | collective-permute-start | bytes 1572872 | tf_op jit(solution)/shard_map/ppermute | solution.py:50
  249.0 179.1 %reduce-scatter.6.cloned.1.call-start = ((), (), s32[]{:S(2)}) async-start(), calls=%async_computation.4 | async-start | bytes 5898240 | tf_op jit(solution)/shard_map/reduce_scatter | solution.py:298
  263.6 25.1 %collective-permute-start.29 = (bf16[1024,256]{1,0:T(8,128)(2,1)S(1)}, bf16[1024,256]{1,0:T(8,128)(2,1)S(1)}, u32[]{:S(2)}, u32[]{:S(2)}) collective-permute-start(bf16[1024,256]{1,0:T(8,128)(2,1)S(1)} %get-tuple-element.213), channel_id=1, source_target_pairs={{0,16},{4,20},{8,24},{12,28},{16,0},{20,4},{24,8},{28,12},{1,17},{... | collective-permute-start | bytes 1572872 | tf_op jit(solution)/shard_map/ppermute | solution.py:50
  265.0 23.7 %collective-permute-start.30 = (bf16[1024,256]{1,0:T(8,128)(2,1)S(1)}, bf16[1024,256]{1,0:T(8,128)(2,1)S(1)}, u32[]{:S(2)}, u32[]{:S(2)}) collective-permute-start(bf16[1024,256]{1,0:T(8,128)(2,1)S(1)} %get-tuple-element.214), channel_id=1, source_target_pairs={{0,24},{4,28},{8,16},{12,20},{16,8},{20,12},{24,0},{28,4},{1,25},{... | collective-permute-start | bytes 1572872 | tf_op jit(solution)/shard_map/ppermute | solution.py:50
  320.2 182.1 %all-gather.6.cloned.1.call-start = ((), (), s32[]{:S(2)}) async-start(), calls=%async_computation.5 | async-start | bytes 4587520 | tf_op jit(solution)/shard_map/all_gather | solution.py:302
  330.7 34.0 %collective-permute-start.36 = (bf16[128,2048]{1,0:T(8,128)(2,1)S(1)}, bf16[128,2048]{1,0:T(8,128)(2,1)S(1)}, u32[]{:S(2)}, u32[]{:S(2)}) collective-permute-start(bf16[128,2048]{1,0:T(8,128)(2,1)S(1)} %get-tuple-element.296), channel_id=1, source_target_pairs={{0,8},{4,12},{8,0},{12,4},{16,24},{20,28},{24,16},{28,20},{1,9},{5... | collective-permute-start | bytes 1572872 | tf_op jit(solution)/shard_map/ppermute | solution.py:50
  332.0 32.6 %collective-permute-start.37 = (bf16[128,2048]{1,0:T(8,128)(2,1)S(1)}, bf16[128,2048]{1,0:T(8,128)(2,1)S(1)}, u32[]{:S(2)}, u32[]{:S(2)}) collective-permute-start(bf16[128,2048]{1,0:T(8,128)(2,1)S(1)} %get-tuple-element.298), channel_id=1, source_target_pairs={{0,16},{4,20},{8,24},{12,28},{16,0},{20,4},{24,8},{28,12},{1,17},{... | collective-permute-start | bytes 1572872 | tf_op jit(solution)/shard_map/ppermute | solution.py:50
  333.0 31.7 %collective-permute-start.38 = (bf16[128,2048]{1,0:T(8,128)(2,1)S(1)}, bf16[128,2048]{1,0:T(8,128)(2,1)S(1)}, u32[]{:S(2)}, u32[]{:S(2)}) collective-permute-start(bf16[128,2048]{1,0:T(8,128)(2,1)S(1)} %get-tuple-element.297), channel_id=1, source_target_pairs={{0,24},{4,28},{8,16},{12,20},{16,8},{20,12},{24,0},{28,4},{1,25},{... | collective-permute-start | bytes 1572872 | tf_op jit(solution)/shard_map/ppermute | solution.py:50
  334.3 24.5 %collective-permute-start.32 = (bf16[128,512]{1,0:T(8,128)(2,1)S(1)}, bf16[128,512]{1,0:T(8,128)(2,1)S(1)}, u32[]{:S(2)}, u32[]{:S(2)}) collective-permute-start(bf16[128,512]{1,0:T(8,128)(2,1)S(1)} %get-tuple-element.355), channel_id=1, source_target_pairs={{0,8},{4,12},{8,0},{12,4},{16,24},{20,28},{24,16},{28,20},{1,9},{5... | collective-permute-start | bytes 393224 | tf_op jit(solution)/shard_map/ppermute | solution.py:50
  335.7 24.9 %collective-permute-start.33 = (bf16[128,512]{1,0:T(8,128)(2,1)S(1)}, bf16[128,512]{1,0:T(8,128)(2,1)S(1)}, u32[]{:S(2)}, u32[]{:S(2)}) collective-permute-start(bf16[128,512]{1,0:T(8,128)(2,1)S(1)} %get-tuple-element.354), channel_id=1, source_target_pairs={{0,16},{4,20},{8,24},{12,28},{16,0},{20,4},{24,8},{28,12},{1,17},{... | collective-permute-start | bytes 393224 | tf_op jit(solution)/shard_map/ppermute | solution.py:50
  371.0 229.9 %reduce-scatter.8.cloned.1.call-start = ((), (), s32[]{:S(2)}) async-start(), calls=%async_computation.6 | async-start | bytes 6553600 | tf_op jit(solution)/shard_map/reduce_scatter | solution.py:298
  444.2 233.2 %all-gather.10.cloned.1.call-start = ((), (), s32[]{:S(2)}) async-start(), calls=%async_computation.8 | async-start | bytes 5898240 | tf_op jit(solution)/shard_map/all_gather | solution.py:302
  448.8 53.4 %collective-permute-start.47 = (bf16[2,64,1152]{2,1,0:T(8,128)(2,1)S(1)}, bf16[2,64,1152]{2,1,0:T(8,128)(2,1)S(1)}, u32[]{:S(2)}, u32[]{:S(2)}) collective-permute-start(bf16[2,64,1152]{2,1,0:T(8,128)(2,1)S(1)} %pad_maximum_fusion.17), channel_id=1, source_target_pairs={{0,24},{4,28},{8,16},{12,20},{16,8},{20,12},{24,0},{28,4},{1,25},{... | collective-permute-start | bytes 884744 | tf_op jit(solution)/shard_map/ppermute | solution.py:50
  450.5 51.7 %collective-permute-start.46 = (bf16[2,64,1152]{2,1,0:T(8,128)(2,1)S(1)}, bf16[2,64,1152]{2,1,0:T(8,128)(2,1)S(1)}, u32[]{:S(2)}, u32[]{:S(2)}) collective-permute-start(bf16[2,64,1152]{2,1,0:T(8,128)(2,1)S(1)} %pad_maximum_fusion.16), channel_id=1, source_target_pairs={{0,16},{4,20},{8,24},{12,28},{16,0},{20,4},{24,8},{28,12},{1,17},{... | collective-permute-start | bytes 884744 | tf_op jit(solution)/shard_map/ppermute | solution.py:50
  451.2 51.1 %collective-permute-start.45 = (bf16[2,64,1152]{2,1,0:T(8,128)(2,1)S(1)}, bf16[2,64,1152]{2,1,0:T(8,128)(2,1)S(1)}, u32[]{:S(2)}, u32[]{:S(2)}) collective-permute-start(bf16[2,64,1152]{2,1,0:T(8,128)(2,1)S(1)} %pad_maximum_fusion.15), channel_id=1, source_target_pairs={{0,8},{4,12},{8,0},{12,4},{16,24},{20,28},{24,16},{28,20},{1,9},{5... | collective-permute-start | bytes 884744 | tf_op jit(solution)/shard_map/ppermute | solution.py:50
  504.7 271.4 %all-gather.8.cloned.1.call-start = ((), (), s32[]{:S(2)}) async-start(), calls=%async_computation.7 | async-start | bytes 6553600 | tf_op jit(solution)/shard_map/all_gather | solution.py:302
  526.5 17.7 %collective-permute-start.56 = (bf16[464,256]{1,0:T(8,128)(2,1)S(1)}, bf16[464,256]{1,0:T(8,128)(2,1)S(1)}, u32[]{:S(2)}, u32[]{:S(2)}) collective-permute-start(bf16[464,256]{1,0:T(8,128)(2,1)S(1)} %pad_maximum_fusion.21), channel_id=1, source_target_pairs={{0,1},{1,0},{2,3},{3,2},{4,5},{5,4},{6,7},{7,6},{8,9},{9,8},{10,11... | collective-permute-start | bytes 712712 | tf_op jit(solution)/shard_map/ppermute | solution.py:388
  544.3 27.7 %collective-permute-start.57 = (bf16[464,256]{1,0:T(8,128)(2,1)S(1)}, bf16[464,256]{1,0:T(8,128)(2,1)S(1)}, u32[]{:S(2)}, u32[]{:S(2)}) collective-permute-start(bf16[464,256]{1,0:T(8,128)(2,1)S(1)} %fusion.14), channel_id=1, source_target_pairs={{0,2},{1,3},{2,0},{3,1},{4,6},{5,7},{6,4},{7,5},{8,10},{9,11},{10,... | collective-permute-start | bytes 712712 | tf_op jit(solution)/shard_map/ppermute | solution.py:388
  575.6 22.8 %collective-permute-start.60 = (bf16[464,512]{1,0:T(8,128)(2,1)S(1)}, bf16[464,512]{1,0:T(8,128)(2,1)S(1)}, u32[]{:S(2)}, u32[]{:S(2)}) collective-permute-start(bf16[464,512]{1,0:T(8,128)(2,1)S(1)} %get-tuple-element.283), channel_id=1, source_target_pairs={{0,16},{4,20},{8,24},{12,28},{16,0},{20,4},{24,8},{28,12},{1,17},{... | collective-permute-start | bytes 1425416 | tf_op jit(solution)/shard_map/ppermute | solution.py:50
  577.1 21.4 %collective-permute-start.61 = (bf16[464,512]{1,0:T(8,128)(2,1)S(1)}, bf16[464,512]{1,0:T(8,128)(2,1)S(1)}, u32[]{:S(2)}, u32[]{:S(2)}) collective-permute-start(bf16[464,512]{1,0:T(8,128)(2,1)S(1)} %get-tuple-element.283), channel_id=1, source_target_pairs={{0,24},{4,28},{8,16},{12,20},{16,8},{20,12},{24,0},{28,4},{1,25},{... | collective-permute-start | bytes 1425416 | tf_op jit(solution)/shard_map/ppermute | solution.py:50
  631.5 24.1 %collective-permute-start.51 = (bf16[128,2048]{1,0:T(8,128)(2,1)S(1)}, bf16[128,2048]{1,0:T(8,128)(2,1)S(1)}, u32[]{:S(2)}, u32[]{:S(2)}) collective-permute-start(bf16[128,2048]{1,0:T(8,128)(2,1)S(1)} %get-tuple-element.294), channel_id=1, source_target_pairs={{0,24},{4,28},{8,16},{12,20},{16,8},{20,12},{24,0},{28,4},{1,25},{... | collective-permute-start | bytes 1572872 | tf_op jit(solution)/shard_map/ppermute | solution.py:50
  (143 other events, 1807.1 us)
Sparse Core Ops, SparseCore 0:
  9.9 52.3 all-gather.11
  249.2 68.3 reduce-scatter.3
  320.4 85.6 reduce-scatter.5
  407.5 72.6 all-gather.5
  482.9 102.5 reduce-scatter.7
  587.5 89.8 all-gather.9
  679.5 96.5 all-gather.7

commit v5 on v4

--- a/solution.py
+++ b/solution.py
@@ -1164,11 +1164,11 @@
     feed_weights = Exchange([feed_lookup_weights, feed_acceptor_weights], 1)
     feed_weights.across_cores()
     (tokens,) = feed_weights.after(*mix_weights.arrived(tokens, count=2))
+    feed_weights.across_chips()
     xk, xv, xr, xg, hidden, low = front(
         length, tokens, gain1, shift1, lerp_factors, narrow, widen, fnarrow
     )
-    (low,) = feed_weights.after(*mix_weights.arrived(low))
-    feed_weights.across_chips()
+    (low,) = mix_weights.arrived(low)
     wk, wv, wr, wg = mix_weights.results()
     fwiden_mine = mine(fading_widen_weights)
     base, u, gn_gain, gn_bias = (

time: 800 us -> 797 us (level)
  waiting for transfers between devices: 390 us -> 380 us
    unnamed x231 -> x243, local copies, waits for them, and re-layouts: 46.9 us -> 43.5 us
  transfers between devices with their start and end apart: 73 -> 73, of which waited for: 47 -> 47; matrix products, arithmetic and copies ran while one was open for 8% -> 9% of each run, Pallas kernels for 24% -> 24%
where the time goes in v5:
time: 797 us; the launch traced here: 787 us
  waiting for transfers between devices  380 us (48%)
  Pallas kernels  200 us (25%)
  local copies, waits for them, and re-layouts  70.7 us (9%)
  starting transfers between devices  63.6 us (8%)
  other arithmetic  30.6 us (4%)
  matrix products  24.6 us (3%)
  between operations  17.3 us (2%)
    ppermute x64, waiting for transfers between devices, swap(): return lax.ppermute(v, 'fsdp', [(i, i ^ m) for i in range(8)])  233 us
    all_gather x3, waiting for transfers between devices, rep_gather(): return lax.all_gather(v, 'rep', axis=0, tiled=True)  107 us
    ppermute x64, starting transfers between devices, swap(): return lax.ppermute(v, 'fsdp', [(i, i ^ m) for i in range(8)])  59.4 us
    pallas_call x1, Pallas kernels, back(): pl.pallas_call(functools.partial(back_kernel, ranks), grid_spec=pltpu.Pre...  49.7 us
    unnamed x243, local copies, waits for them, and re-layouts  43.5 us
    ppermute x2, waiting for transfers between devices, rep_sum(): lax.ppermute(total.astype(v.dtype), 'rep', [(i, i ^ step) for i in range(...  40 us
    pallas_call x1, Pallas kernels, mix_back(): pl.pallas_call(functools.partial(wkv_back_kernel, levels, count, width),...  28.9 us
    dot_general x9, matrix products, mm_tn(): lax.dot_general(a, b, (((0,), (0,)), ((), ())), preferred_element_type=F32)  23.4 us
  transfers between devices with their start and end apart: 73, of which 47 were waited for; matrix products, arithmetic and copies ran while one was open for 9% of the time, Pallas kernels for 24%

profile of v5, /device:TPU:0, one launch (start us, length us, event | category | flops | bytes accessed | tf_op | source)
XLA Modules:
  0.0 787.2 jit_solution(6920920445411097156)
XLA Ops:
  34.0 28.6 %collective-permute-done.2.refs_2_.refs_6_ = bf16[2,256,1024]{2,1,0:T(8,128)(2,1)} collective-permute-done((bf16[2,256,1024]{2,1,0:T(8,128)(2,1)}, bf16[2,256,1024]{2,1,0:T(8,128)(2,1)}, u32[]{:S(2)}, u32[]{:S(2)}) %collective-permute-start.2) | collective-permute-done | bytes 1048608 | tf_op jit(solution)/shard_map/ppermute | solution.py:50
  73.0 18.6 %token_shift.1 = (bf16[1024,2048]{1,0:T(8,128)(2,1)}, bf16[1024,2048]{1,0:T(8,128)(2,1)}, bf16[1024,2048]{1,0:T(8,128)(2,1)}, bf16[1024,2048]{1,0:T(8,128)(2,1)}...) custom-call(s32[8]{0:T(128)S(1)} %stack.26.order, bf16[1024,2048]{1,0:T(8,128)(2,1)} %bitcast.146, ...), custom_call_target="tpu_custom_call" | custom-call | flops 1 | bytes 1 | tf_op jit(solution)/shard_map/token_shift/pallas_call | solution.py:491
  99.4 20.3 %decay_mix.1 = (f32[1024,256]{1,0:T(8,128)S(1)}, f32[1024,256]{1,0:T(8,128)S(1)}, f32[1024,256]{1,0:T(8,128)S(1)}, f32[1024,256]{1,0:T(8,128)S(1)}, f32[1024,256...) custom-call(bf16[1024,2048]{1,0:T(8,128)(2,1)S(1)} %copy-done.68, ...), custom_call_target="tpu_custom_call" | custom-call | flops 20000000000 | bytes 1 | tf_op jit(solution)/shard_map/decay_mix/pallas_call | solution.py:765
  123.7 12.5 %collective-permute-done.6.refs_2_.refs_6_ = bf16[2,256,1152]{2,1,0:T(8,128)(2,1)S(1)} collective-permute-done((bf16[2,256,1152]{2,1,0:T(8,128)(2,1)}, bf16[2,256,1152]{2,1,0:T(8,128)(2,1)S(1)}, u32[]{:S(2)}, u32[]{:S(2)}) %collective-permute-start.6) | collective-permute-done | bytes 1179680 | tf_op jit(solution)/shard_map/ppermute | solution.py:50
  153.7 14.5 %collective-permute-done.10 = bf16[128,2048]{1,0:T(8,128)(2,1)} collective-permute-done((bf16[128,2048]{1,0:T(8,128)(2,1)}, bf16[128,2048]{1,0:T(8,128)(2,1)}, u32[]{:S(2)}, u32[]{:S(2)}) %collective-permute-start.10) | collective-permute-done | bytes 524320 | tf_op jit(solution)/shard_map/ppermute | solution.py:50
  189.9 7.6 collective-permute-done.18
  210.0 6.8 feed.2
  219.1 6.9 feed.3
  226.0 4.5 collective-permute-done.24
  239.7 5.5 convolution_convert_fusion.1
  262.9 11.3 %collective-permute-done.28.refs_1_ = bf16[1024,256]{1,0:T(8,128)(2,1)S(1)} collective-permute-done((bf16[1024,256]{1,0:T(8,128)(2,1)S(1)}, bf16[1024,256]{1,0:T(8,128)(2,1)S(1)}, u32[]{:S(2)}, u32[]{:S(2)}) %collective-permute-start.28) | collective-permute-done | bytes 524320 | tf_op jit(solution)/shard_map/ppermute | solution.py:50
  274.2 11.1 %collective-permute-done.29.refs_2_ = bf16[1024,256]{1,0:T(8,128)(2,1)S(1)} collective-permute-done((bf16[1024,256]{1,0:T(8,128)(2,1)S(1)}, bf16[1024,256]{1,0:T(8,128)(2,1)S(1)}, u32[]{:S(2)}, u32[]{:S(2)}) %collective-permute-start.29) | collective-permute-done | bytes 524320 | tf_op jit(solution)/shard_map/ppermute | solution.py:50
  285.8 19.0 %feed_back.1 = (bf16[1024,896]{1,0:T(8,128)(2,1)}, bf16[1024,2048]{1,0:T(8,128)(2,1)}, f32[2,2048]{1,0:T(2,128)S(1)}) custom-call(bf16[1024,2048]{1,0:T(8,128)(2,1)} %copy-done.5, bf16[1024,2048]{1,0:T(8,128)(2,1)} %copy-done.3, f32[1024,896]{1,0:T(8,128)} %get-tuple-element.211.fac, bf16[1024,256]{1,0:T(8,128)(2,1)S(1)} %get-tuple-element.212.dgate, ...), custom_call_target="tpu_custom_call" | custom-call | flops 1 | bytes 1 | tf_op jit(solution)/shard_map/feed_back/pallas_call | solution.py:1088
  304.7 6.5 convolution_convert_fusion.refs_0_
  332.7 21.8 %collective-permute-done.32 = bf16[128,512]{1,0:T(8,128)(2,1)S(1)} collective-permute-done((bf16[128,512]{1,0:T(8,128)(2,1)S(1)}, bf16[128,512]{1,0:T(8,128)(2,1)S(1)}, u32[]{:S(2)}, u32[]{:S(2)}) %collective-permute-start.32) | collective-permute-done | bytes 131104 | tf_op jit(solution)/shard_map/ppermute | solution.py:50
  375.2 9.7 %collective-permute-done.41 = bf16[128,2048]{1,0:T(8,128)(2,1)S(1)} collective-permute-done((bf16[128,2048]{1,0:T(8,128)(2,1)S(1)}, bf16[128,2048]{1,0:T(8,128)(2,1)S(1)}, u32[]{:S(2)}, u32[]{:S(2)}) %collective-permute-start.41) | collective-permute-done | bytes 524320 | tf_op jit(solution)/shard_map/ppermute | solution.py:50
  393.4 28.9 %decay_mix_back.1 = (bf16[1024,256]{1,0:T(8,128)(2,1)S(1)}, bf16[1024,256]{1,0:T(8,128)(2,1)S(1)}, bf16[1024,256]{1,0:T(8,128)(2,1)S(1)}, bf16[1024,256]{1,0:T(8...) custom-call(f32[1024,256]{1,0:T(8,128)S(1)} %copy-done.47, f32[1024,256]{1,0:T(8,128)S(1)} %copy-done.43, ...), custom_call_target="tpu_custom_call" | custom-call | flops 1 | bytes 1 | tf_op jit(solution)/shard_map/decay_mix_back/pallas_call | solution.py:889
  423.3 4.3 convolution_convert_fusion.3.refs_3_
  447.6 49.7 %token_shift_back.1 = (bf16[1024,2048]{1,0:T(8,128)(2,1)}, f32[8,2048]{1,0:T(8,128)}, f32[160,2048]{1,0:T(8,128)}, f32[160,2048]{1,0:T(8,128)}, f32[64,2048]{1,0:T(8,128)}) custom-call(s32[8]{0:T(128)} %copy-done.62, bf16[1024,2048]{1,0:T(8,128)(2,1)} %bitcast.148, f32[1024,160]{1,0:T(8,128)} %copy-done.37, f32[1024,64]{1,0:T(8,128)} %copy-done.29, ...), custom_call_target="tpu_custom_call" | custom-call | flops 1 | bytes 1 | tf_op jit(solution)/shard_map/token_shift_back/pallas_call | solution.py:612
  520.9 4.3 collective-permute-done.54
  526.9 15.3 %collective-permute-done.56 = bf16[464,256]{1,0:T(8,128)(2,1)S(1)} collective-permute-done((bf16[464,256]{1,0:T(8,128)(2,1)S(1)}, bf16[464,256]{1,0:T(8,128)(2,1)S(1)}, u32[]{:S(2)}, u32[]{:S(2)}) %collective-permute-start.56) | collective-permute-done | bytes 237600 | tf_op jit(solution)/shard_map/ppermute | solution.py:388
  543.9 24.8 %collective-permute-done.57 = bf16[464,256]{1,0:T(8,128)(2,1)S(1)} collective-permute-done((bf16[464,256]{1,0:T(8,128)(2,1)S(1)}, bf16[464,256]{1,0:T(8,128)(2,1)S(1)}, u32[]{:S(2)}, u32[]{:S(2)}) %collective-permute-start.57) | collective-permute-done | bytes 237600 | tf_op jit(solution)/shard_map/ppermute | solution.py:388
  574.3 10.2 %collective-permute-done.59 = bf16[464,512]{1,0:T(8,128)(2,1)S(1)} collective-permute-done((bf16[464,512]{1,0:T(8,128)(2,1)S(1)}, bf16[464,512]{1,0:T(8,128)(2,1)S(1)}, u32[]{:S(2)}, u32[]{:S(2)}) %collective-permute-start.59) | collective-permute-done | bytes 475168 | tf_op jit(solution)/shard_map/ppermute | solution.py:50
  584.6 10.4 %collective-permute-done.60 = bf16[464,512]{1,0:T(8,128)(2,1)S(1)} collective-permute-done((bf16[464,512]{1,0:T(8,128)(2,1)S(1)}, bf16[464,512]{1,0:T(8,128)(2,1)S(1)}, u32[]{:S(2)}, u32[]{:S(2)}) %collective-permute-start.60) | collective-permute-done | bytes 475168 | tf_op jit(solution)/shard_map/ppermute | solution.py:50
  605.8 6.1 collective-permute-done.65.refs_3_.refs_7_
  611.9 4.8 collective-permute-done.64.refs_2_.refs_6_
  629.6 10.2 %widened.5 = f32[896,2048]{1,0:T(8,128)} custom-call(bf16[896,2048]{1,0:T(8,128)(2,1)S(1)} %copy-done.26), custom_call_target="tpu_custom_call" | custom-call | flops 1 | bytes 1 | tf_op jit(solution)/shard_map/widened/pallas_call | solution.py:370
  641.6 10.6 %collective-permute-done.51 = bf16[128,2048]{1,0:T(8,128)(2,1)S(1)} collective-permute-done((bf16[128,2048]{1,0:T(8,128)(2,1)S(1)}, bf16[128,2048]{1,0:T(8,128)(2,1)S(1)}, u32[]{:S(2)}, u32[]{:S(2)}) %collective-permute-start.51) | collective-permute-done | bytes 524320 | tf_op jit(solution)/shard_map/ppermute | solution.py:50
  654.3 19.7 %all-gather.10.cloned.1.call-done.refs_0_ = bf16[256,9216]{1,0:T(8,128)(2,1)} async-done(((bf16[64,9216]{1,0:T(8,128)(2,1)}), bf16[256,9216]{1,0:T(8,128)(2,1)}) %all-gather.10.cloned.1.call-update) | async-done | bytes 4718608 | tf_op jit(solution)/shard_map/all_gather | solution.py:302
  676.3 4.6 widened.4
  685.8 86.9 %all-gather.8.cloned.1.call-done.refs_0_ = bf16[256,10240]{1,0:T(8,128)(2,1)} async-done(((bf16[64,10240]{1,0:T(8,128)(2,1)}), bf16[256,10240]{1,0:T(8,128)(2,1)}) %all-gather.8.cloned.1.call-update) | async-done | bytes 5242896 | tf_op jit(solution)/shard_map/all_gather | solution.py:302
  775.2 4.8 widened.3
  (519 shorter events, 269.5 us)
Async XLA Ops:
  7.2 57.1 %all-gather.12.cloned.1.call-start = ((), (), s32[]{:S(2)}) async-start(), calls=%async_computation.9 | async-start | bytes 4718592 | tf_op jit(solution)/shard_map/all_gather | solution.py:1142
  7.9 307.8 %reduce-scatter.4.cloned.1.call-start = ((), (), s32[]{:S(2)}) async-start(), calls=%async_computation.3 | async-start | bytes 4587520 | tf_op jit(solution)/shard_map/reduce_scatter | solution.py:298
  20.3 43.9 %collective-permute-start.3 = (bf16[4,256,1152]{2,1,0:T(8,128)(2,1)}, bf16[4,256,1152]{2,1,0:T(8,128)(2,1)}, u32[]{:S(2)}, u32[]{:S(2)}) collective-permute-start(bf16[4,256,1152]{2,1,0:T(8,128)(2,1)} %get-tuple-element.151), channel_id=1, source_target_pairs={{0,4},{4,0},{8,12},{12,8},{16,20},{20,16},{24,28},{28,24},{1,5},{5... | collective-permute-start | bytes 7077896 | tf_op jit(solution)/shard_map/ppermute | solution.py:50
  23.1 39.4 %collective-permute-start.2 = (bf16[2,256,1024]{2,1,0:T(8,128)(2,1)}, bf16[2,256,1024]{2,1,0:T(8,128)(2,1)}, u32[]{:S(2)}, u32[]{:S(2)}) collective-permute-start(bf16[2,256,1024]{2,1,0:T(8,128)(2,1)} %pad_maximum_fusion.5), channel_id=1, source_target_pairs={{0,16},{4,20},{8,24},{12,28},{16,0},{20,4},{24,8},{28,12},{1,17},{... | collective-permute-start | bytes 3145736 | tf_op jit(solution)/shard_map/ppermute | solution.py:50
  26.7 37.5 %collective-permute-start.1 = (bf16[2,256,1024]{2,1,0:T(8,128)(2,1)}, bf16[2,256,1024]{2,1,0:T(8,128)(2,1)}, u32[]{:S(2)}, u32[]{:S(2)}) collective-permute-start(bf16[2,256,1024]{2,1,0:T(8,128)(2,1)} %pad_maximum_fusion.4), channel_id=1, source_target_pairs={{0,8},{4,12},{8,0},{12,4},{16,24},{20,28},{24,16},{28,20},{1,9},{5... | collective-permute-start | bytes 3145736 | tf_op jit(solution)/shard_map/ppermute | solution.py:50
  34.0 57.5 %collective-permute-start.4 = (bf16[2,256,1024]{2,1,0:T(8,128)(2,1)}, bf16[2,256,1024]{2,1,0:T(8,128)(2,1)}, u32[]{:S(2)}, u32[]{:S(2)}) collective-permute-start(bf16[2,256,1024]{2,1,0:T(8,128)(2,1)} %pad_maximum_fusion.6), channel_id=1, source_target_pairs={{0,24},{4,28},{8,16},{12,20},{16,8},{20,12},{24,0},{28,4},{1,25},{... | collective-permute-start | bytes 3145736 | tf_op jit(solution)/shard_map/ppermute | solution.py:50
  67.1 56.6 %collective-permute-start.7 = (bf16[2,256,1152]{2,1,0:T(8,128)(2,1)}, bf16[2,256,1152]{2,1,0:T(8,128)(2,1)S(1)}, u32[]{:S(2)}, u32[]{:S(2)}) collective-permute-start(bf16[2,256,1152]{2,1,0:T(8,128)(2,1)} %pad_maximum_fusion.2), channel_id=1, source_target_pairs={{0,24},{4,28},{8,16},{12,20},{16,8},{20,12},{24,0},{28,4},{1,25},{... | collective-permute-start | bytes 3538952 | tf_op jit(solution)/shard_map/ppermute | solution.py:50
  69.7 66.5 %collective-permute-start.6 = (bf16[2,256,1152]{2,1,0:T(8,128)(2,1)}, bf16[2,256,1152]{2,1,0:T(8,128)(2,1)S(1)}, u32[]{:S(2)}, u32[]{:S(2)}) collective-permute-start(bf16[2,256,1152]{2,1,0:T(8,128)(2,1)} %pad_maximum_fusion.1), channel_id=1, source_target_pairs={{0,16},{4,20},{8,24},{12,28},{16,0},{20,4},{24,8},{28,12},{1,17},{... | collective-permute-start | bytes 3538952 | tf_op jit(solution)/shard_map/ppermute | solution.py:50
  72.4 64.2 %collective-permute-start.5 = (bf16[2,256,1152]{2,1,0:T(8,128)(2,1)}, bf16[2,256,1152]{2,1,0:T(8,128)(2,1)S(1)}, u32[]{:S(2)}, u32[]{:S(2)}) collective-permute-start(bf16[2,256,1152]{2,1,0:T(8,128)(2,1)} %pad_maximum_fusion), channel_id=1, source_target_pairs={{0,8},{4,12},{8,0},{12,4},{16,24},{20,28},{24,16},{28,20},{1,9},{5... | collective-permute-start | bytes 3538952 | tf_op jit(solution)/shard_map/ppermute | solution.py:50
  142.6 25.6 %collective-permute-start.10 = (bf16[128,2048]{1,0:T(8,128)(2,1)}, bf16[128,2048]{1,0:T(8,128)(2,1)}, u32[]{:S(2)}, u32[]{:S(2)}) collective-permute-start(bf16[128,2048]{1,0:T(8,128)(2,1)} %get-tuple-element.295), channel_id=1, source_target_pairs={{0,16},{4,20},{8,24},{12,28},{16,0},{20,4},{24,8},{28,12},{1,17},{... | collective-permute-start | bytes 1572872 | tf_op jit(solution)/shard_map/ppermute | solution.py:50
  144.1 24.0 %collective-permute-start.11 = (bf16[128,2048]{1,0:T(8,128)(2,1)}, bf16[128,2048]{1,0:T(8,128)(2,1)}, u32[]{:S(2)}, u32[]{:S(2)}) collective-permute-start(bf16[128,2048]{1,0:T(8,128)(2,1)} %get-tuple-element.294), channel_id=1, source_target_pairs={{0,24},{4,28},{8,16},{12,20},{16,8},{20,12},{24,0},{28,4},{1,25},{... | collective-permute-start | bytes 1572872 | tf_op jit(solution)/shard_map/ppermute | solution.py:50
  145.6 23.8 %collective-permute-start.9 = (bf16[128,2048]{1,0:T(8,128)(2,1)}, bf16[128,2048]{1,0:T(8,128)(2,1)}, u32[]{:S(2)}, u32[]{:S(2)}) collective-permute-start(bf16[128,2048]{1,0:T(8,128)(2,1)} %get-tuple-element.293), channel_id=1, source_target_pairs={{0,8},{4,12},{8,0},{12,4},{16,24},{20,28},{24,16},{28,20},{1,9},{5... | collective-permute-start | bytes 1572872 | tf_op jit(solution)/shard_map/ppermute | solution.py:50
  245.2 178.0 %reduce-scatter.6.cloned.1.call-start = ((), (), s32[]{:S(2)}) async-start(), calls=%async_computation.4 | async-start | bytes 5898240 | tf_op jit(solution)/shard_map/reduce_scatter | solution.py:298
  260.1 25.1 %collective-permute-start.29 = (bf16[1024,256]{1,0:T(8,128)(2,1)S(1)}, bf16[1024,256]{1,0:T(8,128)(2,1)S(1)}, u32[]{:S(2)}, u32[]{:S(2)}) collective-permute-start(bf16[1024,256]{1,0:T(8,128)(2,1)S(1)} %get-tuple-element.207), channel_id=1, source_target_pairs={{0,16},{4,20},{8,24},{12,28},{16,0},{20,4},{24,8},{28,12},{1,17},{... | collective-permute-start | bytes 1572872 | tf_op jit(solution)/shard_map/ppermute | solution.py:50
  261.5 23.7 %collective-permute-start.30 = (bf16[1024,256]{1,0:T(8,128)(2,1)S(1)}, bf16[1024,256]{1,0:T(8,128)(2,1)S(1)}, u32[]{:S(2)}, u32[]{:S(2)}) collective-permute-start(bf16[1024,256]{1,0:T(8,128)(2,1)S(1)} %get-tuple-element.208), channel_id=1, source_target_pairs={{0,24},{4,28},{8,16},{12,20},{16,8},{20,12},{24,0},{28,4},{1,25},{... | collective-permute-start | bytes 1572872 | tf_op jit(solution)/shard_map/ppermute | solution.py:50
  315.6 181.6 %all-gather.6.cloned.1.call-start = ((), (), s32[]{:S(2)}) async-start(), calls=%async_computation.5 | async-start | bytes 4587520 | tf_op jit(solution)/shard_map/all_gather | solution.py:302
  326.3 34.1 %collective-permute-start.36 = (bf16[128,2048]{1,0:T(8,128)(2,1)S(1)}, bf16[128,2048]{1,0:T(8,128)(2,1)S(1)}, u32[]{:S(2)}, u32[]{:S(2)}) collective-permute-start(bf16[128,2048]{1,0:T(8,128)(2,1)S(1)} %get-tuple-element.290), channel_id=1, source_target_pairs={{0,8},{4,12},{8,0},{12,4},{16,24},{20,28},{24,16},{28,20},{1,9},{5... | collective-permute-start | bytes 1572872 | tf_op jit(solution)/shard_map/ppermute | solution.py:50
  328.0 32.5 %collective-permute-start.37 = (bf16[128,2048]{1,0:T(8,128)(2,1)S(1)}, bf16[128,2048]{1,0:T(8,128)(2,1)S(1)}, u32[]{:S(2)}, u32[]{:S(2)}) collective-permute-start(bf16[128,2048]{1,0:T(8,128)(2,1)S(1)} %get-tuple-element.292), channel_id=1, source_target_pairs={{0,16},{4,20},{8,24},{12,28},{16,0},{20,4},{24,8},{28,12},{1,17},{... | collective-permute-start | bytes 1572872 | tf_op jit(solution)/shard_map/ppermute | solution.py:50
  329.1 31.4 %collective-permute-start.38 = (bf16[128,2048]{1,0:T(8,128)(2,1)S(1)}, bf16[128,2048]{1,0:T(8,128)(2,1)S(1)}, u32[]{:S(2)}, u32[]{:S(2)}) collective-permute-start(bf16[128,2048]{1,0:T(8,128)(2,1)S(1)} %get-tuple-element.291), channel_id=1, source_target_pairs={{0,24},{4,28},{8,16},{12,20},{16,8},{20,12},{24,0},{28,4},{1,25},{... | collective-permute-start | bytes 1572872 | tf_op jit(solution)/shard_map/ppermute | solution.py:50
  330.0 24.6 %collective-permute-start.32 = (bf16[128,512]{1,0:T(8,128)(2,1)S(1)}, bf16[128,512]{1,0:T(8,128)(2,1)S(1)}, u32[]{:S(2)}, u32[]{:S(2)}) collective-permute-start(bf16[128,512]{1,0:T(8,128)(2,1)S(1)} %get-tuple-element.349), channel_id=1, source_target_pairs={{0,8},{4,12},{8,0},{12,4},{16,24},{20,28},{24,16},{28,20},{1,9},{5... | collective-permute-start | bytes 393224 | tf_op jit(solution)/shard_map/ppermute | solution.py:50
  331.7 24.9 %collective-permute-start.33 = (bf16[128,512]{1,0:T(8,128)(2,1)S(1)}, bf16[128,512]{1,0:T(8,128)(2,1)S(1)}, u32[]{:S(2)}, u32[]{:S(2)}) collective-permute-start(bf16[128,512]{1,0:T(8,128)(2,1)S(1)} %get-tuple-element.348), channel_id=1, source_target_pairs={{0,16},{4,20},{8,24},{12,28},{16,0},{20,4},{24,8},{28,12},{1,17},{... | collective-permute-start | bytes 393224 | tf_op jit(solution)/shard_map/ppermute | solution.py:50
  366.9 230.6 %reduce-scatter.8.cloned.1.call-start = ((), (), s32[]{:S(2)}) async-start(), calls=%async_computation.6 | async-start | bytes 6553600 | tf_op jit(solution)/shard_map/reduce_scatter | solution.py:298
  439.4 234.6 %all-gather.10.cloned.1.call-start = ((), (), s32[]{:S(2)}) async-start(), calls=%async_computation.8 | async-start | bytes 5898240 | tf_op jit(solution)/shard_map/all_gather | solution.py:302
  443.8 53.5 %collective-permute-start.47 = (bf16[2,64,1152]{2,1,0:T(8,128)(2,1)S(1)}, bf16[2,64,1152]{2,1,0:T(8,128)(2,1)S(1)}, u32[]{:S(2)}, u32[]{:S(2)}) collective-permute-start(bf16[2,64,1152]{2,1,0:T(8,128)(2,1)S(1)} %pad_maximum_fusion.17), channel_id=1, source_target_pairs={{0,24},{4,28},{8,16},{12,20},{16,8},{20,12},{24,0},{28,4},{1,25},{... | collective-permute-start | bytes 884744 | tf_op jit(solution)/shard_map/ppermute | solution.py:50
  445.3 51.9 %collective-permute-start.46 = (bf16[2,64,1152]{2,1,0:T(8,128)(2,1)S(1)}, bf16[2,64,1152]{2,1,0:T(8,128)(2,1)S(1)}, u32[]{:S(2)}, u32[]{:S(2)}) collective-permute-start(bf16[2,64,1152]{2,1,0:T(8,128)(2,1)S(1)} %pad_maximum_fusion.16), channel_id=1, source_target_pairs={{0,16},{4,20},{8,24},{12,28},{16,0},{20,4},{24,8},{28,12},{1,17},{... | collective-permute-start | bytes 884744 | tf_op jit(solution)/shard_map/ppermute | solution.py:50
  446.5 50.8 %collective-permute-start.45 = (bf16[2,64,1152]{2,1,0:T(8,128)(2,1)S(1)}, bf16[2,64,1152]{2,1,0:T(8,128)(2,1)S(1)}, u32[]{:S(2)}, u32[]{:S(2)}) collective-permute-start(bf16[2,64,1152]{2,1,0:T(8,128)(2,1)S(1)} %pad_maximum_fusion.15), channel_id=1, source_target_pairs={{0,8},{4,12},{8,0},{12,4},{16,24},{20,28},{24,16},{28,20},{1,9},{5... | collective-permute-start | bytes 884744 | tf_op jit(solution)/shard_map/ppermute | solution.py:50
  499.6 273.0 %all-gather.8.cloned.1.call-start = ((), (), s32[]{:S(2)}) async-start(), calls=%async_computation.7 | async-start | bytes 6553600 | tf_op jit(solution)/shard_map/all_gather | solution.py:302
  525.3 16.9 %collective-permute-start.56 = (bf16[464,256]{1,0:T(8,128)(2,1)S(1)}, bf16[464,256]{1,0:T(8,128)(2,1)S(1)}, u32[]{:S(2)}, u32[]{:S(2)}) collective-permute-start(bf16[464,256]{1,0:T(8,128)(2,1)S(1)} %pad_maximum_fusion.21), channel_id=1, source_target_pairs={{0,1},{1,0},{2,3},{3,2},{4,5},{5,4},{6,7},{7,6},{8,9},{9,8},{10,11... | collective-permute-start | bytes 712712 | tf_op jit(solution)/shard_map/ppermute | solution.py:388
  542.2 26.4 %collective-permute-start.57 = (bf16[464,256]{1,0:T(8,128)(2,1)S(1)}, bf16[464,256]{1,0:T(8,128)(2,1)S(1)}, u32[]{:S(2)}, u32[]{:S(2)}) collective-permute-start(bf16[464,256]{1,0:T(8,128)(2,1)S(1)} %fusion.14), channel_id=1, source_target_pairs={{0,2},{1,3},{2,0},{3,1},{4,6},{5,7},{6,4},{7,5},{8,10},{9,11},{10,... | collective-permute-start | bytes 712712 | tf_op jit(solution)/shard_map/ppermute | solution.py:388
  572.2 22.8 %collective-permute-start.60 = (bf16[464,512]{1,0:T(8,128)(2,1)S(1)}, bf16[464,512]{1,0:T(8,128)(2,1)S(1)}, u32[]{:S(2)}, u32[]{:S(2)}) collective-permute-start(bf16[464,512]{1,0:T(8,128)(2,1)S(1)} %get-tuple-element.277), channel_id=1, source_target_pairs={{0,16},{4,20},{8,24},{12,28},{16,0},{20,4},{24,8},{28,12},{1,17},{... | collective-permute-start | bytes 1425416 | tf_op jit(solution)/shard_map/ppermute | solution.py:50
  573.7 21.4 %collective-permute-start.61 = (bf16[464,512]{1,0:T(8,128)(2,1)S(1)}, bf16[464,512]{1,0:T(8,128)(2,1)S(1)}, u32[]{:S(2)}, u32[]{:S(2)}) collective-permute-start(bf16[464,512]{1,0:T(8,128)(2,1)S(1)} %get-tuple-element.277), channel_id=1, source_target_pairs={{0,24},{4,28},{8,16},{12,20},{16,8},{20,12},{24,0},{28,4},{1,25},{... | collective-permute-start | bytes 1425416 | tf_op jit(solution)/shard_map/ppermute | solution.py:50
  628.1 24.0 %collective-permute-start.51 = (bf16[128,2048]{1,0:T(8,128)(2,1)S(1)}, bf16[128,2048]{1,0:T(8,128)(2,1)S(1)}, u32[]{:S(2)}, u32[]{:S(2)}) collective-permute-start(bf16[128,2048]{1,0:T(8,128)(2,1)S(1)} %get-tuple-element.288), channel_id=1, source_target_pairs={{0,24},{4,28},{8,16},{12,20},{16,8},{20,12},{24,0},{28,4},{1,25},{... | collective-permute-start | bytes 1572872 | tf_op jit(solution)/shard_map/ppermute | solution.py:50
  (149 other events, 1752.5 us)
Sparse Core Ops, SparseCore 0:
  9.9 51.8 all-gather.11
  245.4 68.7 reduce-scatter.3
  317.1 85.5 reduce-scatter.5
  404.1 72.6 all-gather.5
  479.5 102.5 reduce-scatter.7
  584.1 89.8 all-gather.9
  676.1 96.5 all-gather.7
